TPU v7x, 32 devices: a whole 2x2x4 slice. The times are simulated.
32 devices in a mesh: dp: 8 (over z, core), tensor: 4 (over y, x).
Axes of the slice: x: 2, y: 2, z: 4, core: 2. Of those that a mesh axis runs over, the one named last changes fastest.
Arguments:
- inputs: bfloat16 [8192, 2048], P(('dp', 'tensor')), may hold values from -6 to 6
- cotangent: bfloat16 [8192, 2048], P(('dp', 'tensor')), may hold values from -6 to 6
- lengths: int32 [8], P('dp'), may hold values from 256 to 1024, as said below
- norm_gain: float32 [2048], replicated, may hold values from 0.1 to 1.9
- w_query: float32 [2048, 2048], P('dp', 'tensor'), may hold values from -0.125 to 0.125
- w_key: float32 [2048, 2048], P('dp', 'tensor'), may hold values from -0.125 to 0.125
- w_value: float32 [2048, 2048], P('dp', 'tensor'), may hold values from -0.125 to 0.125
- w_gate_out: float32 [2048, 2048], P('dp', 'tensor'), may hold values from -0.125 to 0.125
- w_beta: float32 [2048, 16], P('dp', 'tensor'), may hold values from -0.125 to 0.125
- conv_weight: float32 [3, 4, 2048], P(None, None, 'tensor'), may hold values from -3 to 3
- out_norm_gain: float32 [128], replicated, may hold values from 0.1 to 1.9
- w_output: float32 [2048, 2048], P('tensor', 'dp'), may hold values from -0.125 to 0.125
- ffn_norm_gain: float32 [2048], replicated, may hold values from 0.1 to 1.9
- w_gate: float32 [2048, 5632], P('dp', 'tensor'), may hold values from -0.125 to 0.125
- w_up: float32 [2048, 5632], P('dp', 'tensor'), may hold values from -0.125 to 0.125
- w_down: float32 [5632, 2048], P('tensor', 'dp'), may hold values from -0.078125 to 0.078125
Outputs:
- output: bfloat16 [8192, 2048], P(('dp', 'tensor'))
- input_grad: float32 [8192, 2048], P(('dp', 'tensor'))
- norm_gain_grad: float32 [2048], replicated
- w_query_grad: float32 [2048, 2048], P('dp', 'tensor')
- w_key_grad: float32 [2048, 2048], P('dp', 'tensor')
- w_value_grad: float32 [2048, 2048], P('dp', 'tensor')
- w_gate_out_grad: float32 [2048, 2048], P('dp', 'tensor')
- w_beta_grad: float32 [2048, 16], P('dp', 'tensor')
- conv_weight_grad: float32 [3, 4, 2048], P(None, None, 'tensor')
- out_norm_gain_grad: float32 [128], replicated
- w_output_grad: float32 [2048, 2048], P('tensor', 'dp')
- ffn_norm_gain_grad: float32 [2048], replicated
- w_gate_grad: float32 [2048, 5632], P('dp', 'tensor')
- w_up_grad: float32 [2048, 5632], P('dp', 'tensor')
- w_down_grad: float32 [5632, 2048], P('tensor', 'dp')
Inputs may be any that keep to these rules, and one draw needn't show every extreme that they name: `lengths`: each entry is the number of valid tokens at the start of its sequence of 1024 slots; the rest is padding. In every draw some sequence is full.
All inputs are finite; a program needn't handle non-finite values.
Results may differ from a plain program's by a relative error of at most 0.02.
Values may be sent and summed in bfloat16 or wider, within the bound.
A program may use at most 320 MiB of HBM per device.

v0:
```python
import jax
import jax.numpy as jnp
from jax import lax
from jax.sharding import PartitionSpec as P

GROUP = 64


norm_epsilon = 1e-06
head_epsilon = 1e-05
highest_precision = lax.Precision.HIGHEST


def rms_norm(values, gain):
    return (
        values * lax.rsqrt(jnp.mean(values * values, axis=-1, keepdims=True) + norm_epsilon) * gain
    )


def short_conv(signal, taps):
    width = taps.shape[0]
    length = signal.shape[0]
    padded = jnp.pad(signal, ((width - 1, 0), (0, 0)))
    total = taps[0] * padded[0:length]
    for offset in range(1, width):
        total = total + taps[offset] * padded[offset : offset + length]
    return total


def unit_rows(values):
    return values * lax.rsqrt(jnp.sum(values * values, axis=-1, keepdims=True) + norm_epsilon)


def delta_rule(query, keys, values, beta):
    length, heads, head_size = query.shape
    blocks = length // GROUP

    def to_blocks(array):
        return array.reshape(blocks, GROUP, heads, array.shape[-1]).transpose(0, 2, 1, 3)

    query_blocks = to_blocks(query)
    key_blocks = to_blocks(keys)
    value_blocks = to_blocks(values)
    beta_blocks = beta.reshape(blocks, GROUP, heads).transpose(0, 2, 1)
    strict_lower = jnp.tril(jnp.ones((GROUP, GROUP), jnp.float32), -1)
    with_diagonal = jnp.tril(jnp.ones((GROUP, GROUP), jnp.float32))
    identity = jnp.eye(GROUP, dtype=jnp.float32)
    gram = jnp.einsum("nhcd,nhed->nhce", key_blocks, key_blocks, precision=highest_precision)
    system = identity + gram * beta_blocks[..., None] * strict_lower
    stacked = jnp.concatenate(
        [key_blocks * beta_blocks[..., None], value_blocks * beta_blocks[..., None]], axis=-1
    )
    solved = lax.linalg.triangular_solve(
        system, stacked, left_side=True, lower=True, unit_diagonal=True
    )
    weights_part = solved[..., :head_size]
    update_part = solved[..., head_size:]

    def state_step(state, block):
        weight_block, update_block, key_block = block
        fresh = update_block - jnp.einsum(
            "hcd,hde->hce", weight_block, state, precision=highest_precision
        )
        following = state + jnp.einsum(
            "hcd,hce->hde", key_block, fresh, precision=highest_precision
        )
        return (following, state)

    start_state = jnp.zeros((heads, head_size, head_size), jnp.float32)
    end_state, entering = lax.scan(state_step, start_state, (weights_part, update_part, key_blocks))
    fresh_all = update_part - jnp.einsum(
        "nhcd,nhde->nhce", weights_part, entering, precision=highest_precision
    )
    scores = (
        jnp.einsum("nhcd,nhed->nhce", query_blocks, key_blocks, precision=highest_precision)
        * with_diagonal
    )
    results = jnp.einsum("nhcd,nhde->nhce", query_blocks, entering, precision=highest_precision)
    results = results + jnp.einsum(
        "nhce,nhef->nhcf", scores, fresh_all, precision=highest_precision
    )
    return results.transpose(0, 2, 1, 3).reshape(length, heads, head_size)


def mix_sequence(q_pre, k_pre, v_pre, gate_pre, beta_pre, conv_taps, head_gain):
    length, width = q_pre.shape
    head_size = head_gain.shape[0]
    heads = width // head_size
    query = jax.nn.silu(short_conv(q_pre, conv_taps[0])).reshape(length, heads, head_size)
    keys = jax.nn.silu(short_conv(k_pre, conv_taps[1])).reshape(length, heads, head_size)
    values = jax.nn.silu(short_conv(v_pre, conv_taps[2])).reshape(length, heads, head_size)
    query = unit_rows(query) * head_size ** (-0.5)
    keys = unit_rows(keys)
    beta = jax.nn.sigmoid(beta_pre)
    mixed = delta_rule(query, keys, values, beta)
    normed = (
        mixed
        * lax.rsqrt(jnp.mean(mixed * mixed, axis=-1, keepdims=True) + head_epsilon)
        * head_gain
    )
    gated = normed * jax.nn.silu(gate_pre.reshape(length, heads, head_size))
    return gated.reshape(length, width)


def transposed_product(left, right):
    return lax.dot_general(
        left, right, (((0,), (0,)), ((), ())), preferred_element_type=jnp.float32
    )


def product_with_transpose(left, right):
    return lax.dot_general(
        left, right, (((1,), (1,)), ((), ())), preferred_element_type=jnp.float32
    )


def body(
    inputs,
    cotangent,
    lengths,
    norm_gain,
    w_query,
    w_key,
    w_value,
    w_gate_out,
    w_beta,
    conv_weight,
    out_norm_gain,
    w_output,
    ffn_norm_gain,
    w_gate,
    w_up,
    w_down,
):
    tensor_count = lax.axis_size("tensor")
    rows = inputs.shape[0]
    seq_count = lengths.shape[0]
    total_rows = rows * tensor_count
    seq_len = total_rows // seq_count
    (
        full_query,
        full_key,
        full_value,
        full_gate_out,
        full_beta,
        full_output,
        full_gate,
        full_up,
        full_down,
    ) = (
        lax.all_gather(w_query.astype(jnp.bfloat16), "dp", axis=0, tiled=True),
        lax.all_gather(w_key.astype(jnp.bfloat16), "dp", axis=0, tiled=True),
        lax.all_gather(w_value.astype(jnp.bfloat16), "dp", axis=0, tiled=True),
        lax.all_gather(w_gate_out.astype(jnp.bfloat16), "dp", axis=0, tiled=True),
        lax.all_gather(w_beta.astype(jnp.bfloat16), "dp", axis=0, tiled=True),
        lax.all_gather(w_output.astype(jnp.bfloat16), "dp", axis=1, tiled=True),
        lax.all_gather(w_gate.astype(jnp.bfloat16), "dp", axis=0, tiled=True),
        lax.all_gather(w_up.astype(jnp.bfloat16), "dp", axis=0, tiled=True),
        lax.all_gather(w_down.astype(jnp.bfloat16), "dp", axis=1, tiled=True),
    )
    local_width = full_query.shape[1]
    inner_weights = jnp.concatenate(
        [full_query, full_key, full_value, full_gate_out, full_beta], axis=1
    )
    positions = lax.axis_index("tensor") * rows + jnp.arange(rows, dtype=jnp.int32)
    seq_of_row = positions // seq_len
    within = positions % seq_len
    seq_ids = jnp.arange(seq_count, dtype=jnp.int32)
    row_length = jnp.sum(
        jnp.where(seq_of_row[:, None] == seq_ids[None, :], lengths[None, :], 0), axis=1
    )
    mask = (within < row_length).astype(jnp.float32)
    features = inputs.astype(jnp.float32)
    normed, first_pull = jax.vjp(rms_norm, features, norm_gain)
    normed_full = lax.all_gather(normed.astype(jnp.bfloat16), "tensor", axis=0, tiled=True)
    projected = jnp.dot(normed_full, inner_weights, preferred_element_type=jnp.float32)
    q_pre = projected[:, 0:local_width]
    k_pre = projected[:, local_width : 2 * local_width]
    v_pre = projected[:, 2 * local_width : 3 * local_width]
    gate_pre = projected[:, 3 * local_width : 4 * local_width]
    beta_pre = projected[:, 4 * local_width :]

    def mixer(q_part, k_part, v_part, gate_part, beta_part, conv_taps, head_gain):

        def per_seq(array):
            return array.reshape(seq_count, seq_len, array.shape[1])

        mapped = jax.vmap(mix_sequence, in_axes=(0, 0, 0, 0, 0, None, None))(
            per_seq(q_part),
            per_seq(k_part),
            per_seq(v_part),
            per_seq(gate_part),
            per_seq(beta_part),
            conv_taps,
            head_gain,
        )
        return mapped.reshape(total_rows, local_width)

    mixed, mixer_pull = jax.vjp(
        mixer, q_pre, k_pre, v_pre, gate_pre, beta_pre, conv_weight, out_norm_gain
    )
    mixed_low = mixed.astype(jnp.bfloat16)
    branch_rows = lax.psum_scatter(
        jnp.dot(mixed_low, full_output, preferred_element_type=jnp.float32).astype(jnp.bfloat16),
        "tensor",
        scatter_dimension=0,
        tiled=True,
    ).astype(jnp.float32)
    resid = features + branch_rows
    normed2, second_pull = jax.vjp(rms_norm, resid, ffn_norm_gain)
    normed2_full = lax.all_gather(normed2.astype(jnp.bfloat16), "tensor", axis=0, tiled=True)
    gate = jnp.dot(normed2_full, full_gate, preferred_element_type=jnp.float32)
    up_part = jnp.dot(normed2_full, full_up, preferred_element_type=jnp.float32)
    gate_sig = jax.nn.sigmoid(gate)
    gate_act = gate * gate_sig
    middle_low = (gate_act * up_part).astype(jnp.bfloat16)
    ffn_out = lax.psum_scatter(
        jnp.dot(middle_low, full_down, preferred_element_type=jnp.float32).astype(jnp.bfloat16),
        "tensor",
        scatter_dimension=0,
        tiled=True,
    ).astype(jnp.float32)
    output = ((resid + ffn_out) * mask[:, None]).astype(jnp.bfloat16)
    grad_out = cotangent.astype(jnp.float32) * mask[:, None]
    grad_out_full = lax.all_gather(grad_out.astype(jnp.bfloat16), "tensor", axis=0, tiled=True)
    grad_middle = product_with_transpose(grad_out_full, full_down)
    grad_gate_low = (grad_middle * up_part * gate_sig * (1.0 + gate * (1.0 - gate_sig))).astype(
        jnp.bfloat16
    )
    grad_up_low = (grad_middle * gate_act).astype(jnp.bfloat16)
    down_grad = transposed_product(middle_low, grad_out_full)
    gate_grad = transposed_product(normed2_full, grad_gate_low)
    up_grad = transposed_product(normed2_full, grad_up_low)
    grad_normed2 = lax.psum_scatter(
        (
            product_with_transpose(grad_gate_low, full_gate)
            + product_with_transpose(grad_up_low, full_up)
        ).astype(jnp.bfloat16),
        "tensor",
        scatter_dimension=0,
        tiled=True,
    ).astype(jnp.float32)
    resid_part, ffn_gain_grad = second_pull(grad_normed2)
    grad_resid = grad_out + resid_part
    grad_resid_full = lax.all_gather(grad_resid.astype(jnp.bfloat16), "tensor", axis=0, tiled=True)
    grad_mixed = product_with_transpose(grad_resid_full, full_output)
    output_grad = transposed_product(mixed_low, grad_resid_full)
    grad_q, grad_k, grad_v, grad_gate_pre, grad_beta, conv_grad, head_gain_grad = mixer_pull(
        grad_mixed
    )
    grad_pre_low = jnp.concatenate(
        [grad_q, grad_k, grad_v, grad_gate_pre, grad_beta], axis=1
    ).astype(jnp.bfloat16)
    inner_grad = transposed_product(normed_full, grad_pre_low)
    query_grad = inner_grad[:, 0:local_width]
    key_grad = inner_grad[:, local_width : 2 * local_width]
    value_grad = inner_grad[:, 2 * local_width : 3 * local_width]
    gate_out_grad = inner_grad[:, 3 * local_width : 4 * local_width]
    beta_grad = inner_grad[:, 4 * local_width :]
    grad_normed = lax.psum_scatter(
        product_with_transpose(grad_pre_low, inner_weights).astype(jnp.bfloat16),
        "tensor",
        scatter_dimension=0,
        tiled=True,
    ).astype(jnp.float32)
    feature_part, first_gain_grad = first_pull(grad_normed)
    input_grad = grad_resid + feature_part
    weight_totals = (
        lax.psum_scatter(
            query_grad.astype(jnp.bfloat16), "dp", scatter_dimension=0, tiled=True
        ).astype(jnp.float32),
        lax.psum_scatter(
            key_grad.astype(jnp.bfloat16), "dp", scatter_dimension=0, tiled=True
        ).astype(jnp.float32),
        lax.psum_scatter(
            value_grad.astype(jnp.bfloat16), "dp", scatter_dimension=0, tiled=True
        ).astype(jnp.float32),
        lax.psum_scatter(
            gate_out_grad.astype(jnp.bfloat16), "dp", scatter_dimension=0, tiled=True
        ).astype(jnp.float32),
        lax.psum_scatter(
            beta_grad.astype(jnp.bfloat16), "dp", scatter_dimension=0, tiled=True
        ).astype(jnp.float32),
        lax.psum_scatter(
            output_grad.astype(jnp.bfloat16), "dp", scatter_dimension=1, tiled=True
        ).astype(jnp.float32),
        lax.psum_scatter(
            gate_grad.astype(jnp.bfloat16), "dp", scatter_dimension=0, tiled=True
        ).astype(jnp.float32),
        lax.psum_scatter(
            up_grad.astype(jnp.bfloat16), "dp", scatter_dimension=0, tiled=True
        ).astype(jnp.float32),
        lax.psum_scatter(
            down_grad.astype(jnp.bfloat16), "dp", scatter_dimension=1, tiled=True
        ).astype(jnp.float32),
    )
    conv_total = lax.psum(conv_grad, "dp")
    first_total, ffn_total, head_total = lax.psum(
        (first_gain_grad, ffn_gain_grad, head_gain_grad), ("dp", "tensor")
    )
    return (
        output,
        input_grad,
        first_total,
        weight_totals[0],
        weight_totals[1],
        weight_totals[2],
        weight_totals[3],
        weight_totals[4],
        conv_total,
        head_total,
        weight_totals[5],
        ffn_total,
        weight_totals[6],
        weight_totals[7],
        weight_totals[8],
    )


def solution(mesh):
    placed = (
        P(("dp", "tensor"), None),
        P(("dp", "tensor"), None),
        P("dp"),
        P(),
        P("dp", "tensor"),
        P("dp", "tensor"),
        P("dp", "tensor"),
        P("dp", "tensor"),
        P("dp", "tensor"),
        P(None, None, "tensor"),
        P(),
        P("tensor", "dp"),
        P(),
        P("dp", "tensor"),
        P("dp", "tensor"),
        P("tensor", "dp"),
    )
    return jax.shard_map(
        body,
        mesh=mesh,
        in_specs=placed,
        out_specs=(
            P(("dp", "tensor"), None),
            P(("dp", "tensor"), None),
            P(),
            P("dp", "tensor"),
            P("dp", "tensor"),
            P("dp", "tensor"),
            P("dp", "tensor"),
            P("dp", "tensor"),
            P(None, None, "tensor"),
            P(),
            P("tensor", "dp"),
            P(),
            P("dp", "tensor"),
            P("dp", "tensor"),
            P("tensor", "dp"),
        ),
        check_vma=False,
    )
```

profile of v0, /device:TPU:0, one launch (start us, length us, event | category | flops | bytes accessed | tf_op | source)
XLA Modules:
  0.0 1838.5 jit_solution(18000258059856964436)
XLA Ops:
  16.7 14.6 all_gather.44
  31.8 10.4 all-gather.15.cloned.1.call-done
  45.3 27.6 %all-gather.17.cloned.1.call-done = bf16[2048,512]{1,0:T(8,128)(2,1)} async-done(((bf16[256,512]{1,0:T(8,128)(2,1)}), bf16[2048,512]{1,0:T(8,128)(2,1)}) %all-gather.17.cloned.1.call-update) | async-done | bytes 2097168 | tf_op jit(solution)/shard_map/all_gather | solution.py:152
  76.0 27.7 %all-gather.19.cloned.1.call-done = bf16[2048,512]{1,0:T(8,128)(2,1)} async-done(((bf16[256,512]{1,0:T(8,128)(2,1)}), bf16[2048,512]{1,0:T(8,128)(2,1)}) %all-gather.19.cloned.1.call-update) | async-done | bytes 2097168 | tf_op jit(solution)/shard_map/all_gather | solution.py:153
  107.0 27.4 %all-gather.21.cloned.1.call-done = bf16[2048,512]{1,0:T(8,128)(2,1)} async-done(((bf16[256,512]{1,0:T(8,128)(2,1)}), bf16[2048,512]{1,0:T(8,128)(2,1)}) %all-gather.21.cloned.1.call-update) | async-done | bytes 2097168 | tf_op jit(solution)/shard_map/all_gather | solution.py:154
  138.6 50.3 %all-gather.13.cloned.1.call-done = bf16[1024,2048]{1,0:T(8,128)(2,1)} async-done(((bf16[256,2048]{1,0:T(8,128)(2,1)}), bf16[1024,2048]{1,0:T(8,128)(2,1)}) %all-gather.13.cloned.1.call-update) | async-done | bytes 4194320 | tf_op jit(solution)/shard_map/all_gather | solution.py:175
  188.9 15.5 fusion.198
  209.5 14.5 fusion.123
  224.1 4.6 copy.118
  232.7 5.4 fusion.105
  244.3 316.0 %custom-call.7 = f32[1,16,4,1,64,64]{4,5,3,2,1,0:T(8,128)} custom-call(f32[1,16,4,1,64,64]{5,4,3,2,1,0:T(8,128)} %add_bitcast_fusion.3), custom_call_target="InvertDiagBlocksLowerTriangular" | custom-call | tf_op jit(solution)/shard_map/jvp(vmap())/triangular_solve | solution.py:53
  560.2 6.0 copy.123
  577.8 67.8 %while.36 = (s32[]{:T(128)}, f32[1,4,128,128]{3,2,1,0:T(8,128)S(1)}, f32[16,1,4,128,128]{4,3,2,1,0:T(8,128)}, f32[16,1,4,64,128]{4,3,2,1,0:T(8,128)}, f32[16,1,4...) while((s32[]{:T(128)}, ...), condition=%wide.region_4.5_spmd.clone, body=%wide.region_3.4_spmd.clone.sunk | while | flops 100958208 | bytes 2099305 | solution.py:70
  645.6 6.1 copy.115
  654.3 5.8 fusion.103
  660.1 6.5 bitcast_subtract_fusion
  678.5 4.8 reshape.1099
  687.2 6.3 convolution_convert_fusion.6
  696.0 50.4 %reduce-scatter.16.cloned.1.call-done = bf16[256,2048]{1,0:T(8,128)(2,1)} async-done(((bf16[1024,2048]{1,0:T(8,128)(2,1)}), bf16[256,2048]{1,0:T(8,128)(2,1)}) %reduce-scatter.16.cloned.1.call-update) | async-done | bytes 1048592 | tf_op jit(solution)/shard_map/reduce_scatter | solution.py:203
  758.2 50.9 %all-gather.27.cloned.1.call-done = bf16[2048,1408]{1,0:T(8,128)(2,1)} async-done(((bf16[256,1408]{1,0:T(8,128)(2,1)}), bf16[2048,1408]{1,0:T(8,128)(2,1)}) %all-gather.27.cloned.1.call-update) | async-done | bytes 5767184 | tf_op jit(solution)/shard_map/all_gather | solution.py:157
  809.2 54.0 %all-gather.25.cloned.1.call-done = bf16[1024,2048]{1,0:T(8,128)(2,1)} async-done(((bf16[256,2048]{1,0:T(8,128)(2,1)}), bf16[1024,2048]{1,0:T(8,128)(2,1)}) %all-gather.25.cloned.1.call-update) | async-done | bytes 4194320 | tf_op jit(solution)/shard_map/all_gather | solution.py:211
  863.2 11.7 fusion.199
  874.8 50.4 %all-gather.29.cloned.1.call-done = bf16[2048,1408]{1,0:T(8,128)(2,1)} async-done(((bf16[256,1408]{1,0:T(8,128)(2,1)}), bf16[2048,1408]{1,0:T(8,128)(2,1)}) %all-gather.29.cloned.1.call-update) | async-done | bytes 5767184 | tf_op jit(solution)/shard_map/all_gather | solution.py:158
  925.2 11.7 fusion.200
  936.9 42.3 %all-gather.33.cloned.1.call-done = bf16[1024,2048]{1,0:T(8,128)(2,1)} async-done(((bf16[256,2048]{1,0:T(8,128)(2,1)}), bf16[1024,2048]{1,0:T(8,128)(2,1)}) %all-gather.33.cloned.1.call-update) | async-done | bytes 4194320 | tf_op jit(solution)/shard_map/all_gather | solution.py:225
  979.2 62.4 %all-gather.31.cloned.1.call-done = bf16[1408,2048]{1,0:T(8,128)(2,1)} async-done(((bf16[1408,256]{1,0:T(8,128)(2,1)}), bf16[1408,2048]{1,0:T(8,128)(2,1)}) %all-gather.31.cloned.1.call-update) | async-done | bytes 5767184 | tf_op jit(solution)/shard_map/all_gather | solution.py:159
  1041.6 15.6 multiply_convert_fusion
  1057.2 10.9 fusion.201
  1068.1 8.3 add_convert_fusion
  1076.7 50.8 %reduce-scatter.20.cloned.1.call-done = bf16[256,2048]{1,0:T(8,128)(2,1)} async-done(((bf16[1024,2048]{1,0:T(8,128)(2,1)}), bf16[256,2048]{1,0:T(8,128)(2,1)}) %reduce-scatter.20.cloned.1.call-update) | async-done | bytes 1048592 | tf_op jit(solution)/shard_map/reduce_scatter | solution.py:234
  1132.8 11.0 convolution_convert_fusion.3
  1143.8 11.0 convolution_convert_fusion.2
  1160.7 10.9 convolution_convert_fusion.1
  1171.8 13.8 all-gather.35.cloned.1.call-done
  1185.6 5.4 fusion.202
  1192.4 4.5 fusion.78
  1196.9 4.5 reshape.1100
  1201.4 4.5 reshape.1103
  1223.9 7.3 fusion.107
  1231.2 9.4 add_bitcast_fusion
  1245.4 127.1 %while.37 = (s32[]{:T(128)}, f32[1,4,128,128]{2,3,1,0:T(8,128)S(1)}, f32[16,1,4,64,128]{4,3,2,1,0:T(8,128)}, f32[16,1,4,64,128]{4,3,2,1,0:T(8,128)}, f32[16,1,4,...) while((s32[]{:T(128)}, ...), condition=%wide.region_14.15_spmd.clone, body=%wide.region_13.14_spmd.clone.sunk | while | flops 201719808 | bytes 2758290 | solution.py:70
  1376.1 8.2 fusion.87
  1392.6 4.7 fusion.45
  1401.2 4.8 fusion.99
  1409.2 4.5 fusion.86
  1418.0 8.3 fusion.51
  1433.1 6.1 copy.138
  1442.3 6.1 copy.151
  1455.5 6.2 copy.155
  1468.5 10.1 multiply_reduce_fusion.12
  1486.7 9.7 convolution_convert_fusion
  1500.8 6.0 fusion.196
  1509.1 5.9 convolution_convert_fusion.7
  1515.1 15.2 convolution_convert_fusion.4
  1530.4 11.0 convolution_convert_fusion.5
  1548.5 29.4 %psum.29 = f32[3,4,512]{2,1,0:T(4,128)} all-reduce(f32[3,4,512]{2,1,0:T(4,128)S(1)} %pad_add_fusion.12), channel_id=1, replica_groups=mesh['dp'=8,'tensor'=4] {'dp'}, use_global_device_ids=true, to_apply=%region_40.41 | all-reduce | flops 6144 | bytes 49152 | tf_op jit(solution)/shard_map/psum | solution.py:297
  1581.3 23.7 %reduce-scatter.26.cloned.1.call-done = bf16[256,512]{0,1:T(8,128)(2,1)} async-done(((bf16[2048,512]{0,1:T(8,128)(2,1)}), bf16[256,512]{0,1:T(8,128)(2,1)}) %reduce-scatter.26.cloned.1.call-update) | async-done | bytes 262160 | tf_op jit(solution)/shard_map/reduce_scatter | solution.py:272
  1607.0 35.0 %reduce-scatter.28.cloned.1.call-done = bf16[256,512]{0,1:T(8,128)(2,1)} async-done(((bf16[2048,512]{0,1:T(8,128)(2,1)}), bf16[256,512]{0,1:T(8,128)(2,1)}) %reduce-scatter.28.cloned.1.call-update) | async-done | bytes 262160 | tf_op jit(solution)/shard_map/reduce_scatter | solution.py:275
  1643.8 35.4 %reduce-scatter.30.cloned.1.call-done = bf16[256,512]{0,1:T(8,128)(2,1)} async-done(((bf16[2048,512]{0,1:T(8,128)(2,1)}), bf16[256,512]{0,1:T(8,128)(2,1)}) %reduce-scatter.30.cloned.1.call-update) | async-done | bytes 262160 | tf_op jit(solution)/shard_map/reduce_scatter | solution.py:278
  1681.2 34.7 %reduce-scatter.32.cloned.1.call-done = bf16[512,256]{1,0:T(8,128)(2,1)} async-done(((bf16[512,2048]{1,0:T(8,128)(2,1)}), bf16[512,256]{1,0:T(8,128)(2,1)}) %reduce-scatter.32.cloned.1.call-update) | async-done | bytes 262160 | tf_op jit(solution)/shard_map/reduce_scatter | solution.py:284
  1717.6 52.7 %reduce-scatter.22.cloned.1.call-done = bf16[256,2048]{1,0:T(8,128)(2,1)} async-done(((bf16[1024,2048]{1,0:T(8,128)(2,1)}), bf16[256,2048]{1,0:T(8,128)(2,1)}) %reduce-scatter.22.cloned.1.call-update) | async-done | bytes 1048592 | tf_op jit(solution)/shard_map/reduce_scatter | solution.py:260
  1772.6 40.1 %all-reduce.32 = (f32[2048]{0:T(1024)}, f32[128]{0:T(128)}, f32[2048]{0:T(1024)}) all-reduce(f32[2048]{0:T(1024)S(1)} %get-tuple-element.438, f32[128]{0:T(128)S(1)} %get-tuple-element.414, f32[2048]{0:T(1024)S(1)} %copy-done.69), channel_id=1, replica_groups=mesh['dp'=8,'tensor'=4] {'dp','tensor'}, use_global_device_ids=true, to_apply=%region_22.23 | all-reduce | flops 4224 | bytes 33792 | tf_op jit(solution)/shard_map/psum | solution.py:298
  1812.8 13.6 reduce-scatter.18.cloned.1.call-done
  1826.4 5.3 fusion.79
  (509 shorter events, 393.1 us)
Async XLA Ops:
  7.2 35.0 %all-gather.15.cloned.1.call-start = ((), (), s32[]{:S(2)}) async-start(), calls=%async_computation.14 | async-start | bytes 2359296 | tf_op jit(solution)/shard_map/all_gather | solution.py:151
  9.2 63.7 %all-gather.17.cloned.1.call-start = ((), (), s32[]{:S(2)}) async-start(), calls=%async_computation.15 | async-start | bytes 2359296 | tf_op jit(solution)/shard_map/all_gather | solution.py:152
  11.1 92.7 %all-gather.19.cloned.1.call-start = ((), (), s32[]{:S(2)}) async-start(), calls=%async_computation.16 | async-start | bytes 2359296 | tf_op jit(solution)/shard_map/all_gather | solution.py:153
  11.9 122.5 %all-gather.21.cloned.1.call-start = ((), (), s32[]{:S(2)}) async-start(), calls=%async_computation.17 | async-start | bytes 2359296 | tf_op jit(solution)/shard_map/all_gather | solution.py:154
  12.7 176.2 %all-gather.13.cloned.1.call-start = ((), (), s32[]{:S(2)}) async-start(), calls=%async_computation.13 | async-start | bytes 5242880 | tf_op jit(solution)/shard_map/all_gather | solution.py:175
  13.1 18.5 %copy-start.72 = (f32[3,4,512]{2,1,0:T(4,128)S(1)}, f32[3,4,512]{2,1,0:T(4,128)}, u32[]{:S(2)}) copy-start(f32[3,4,512]{2,1,0:T(4,128)} %param.29) | copy-start | bytes 73732
  13.1 18.7 %copy-start.105 = (f32[128]{0:T(128)S(1)}, f32[128]{0:T(128)}, u32[]{:S(2)}) copy-start(f32[128]{0:T(128)} %param.30) | copy-start | bytes 1540
  14.4 672.8 %all-gather.23.cloned.1.call-start = ((), (), s32[]{:S(2)}) async-start(), calls=%async_computation.18 | async-start | bytes 2359296 | tf_op jit(solution)/shard_map/all_gather | solution.py:156
  15.3 731.1 %reduce-scatter.16.cloned.1.call-start = ((), (), s32[]{:S(2)}) async-start(), calls=%async_computation.19 | async-start | bytes 5242880 | tf_op jit(solution)/shard_map/reduce_scatter | solution.py:203
  16.0 225.3 %copy-start.66 = (pred[64,64]{1,0:T(8,128)(4,1)}, pred[64,64]{1,0:T(8,128)(4,1)S(1)}, u32[]{:S(2)}) copy-start(pred[64,64]{1,0:T(8,128)(4,1)S(1)} %get-tuple-element.545) | copy-start | bytes 12292
  16.0 225.3 %copy-start.53 = (f32[64,64]{1,0:T(8,128)}, f32[64,64]{1,0:T(8,128)S(1)}, u32[]{:S(2)}) copy-start(f32[64,64]{1,0:T(8,128)S(1)} %broadcast_select_fusion) | copy-start | bytes 49156
  31.7 177.2 %copy-start.73 = (f32[1,1,512]{2,1,0:T(1,128)}, f32[1,1,512]{2,1,0:T(1,128)S(1)}, u32[]{:S(2)}) copy-start(f32[1,1,512]{2,1,0:T(1,128)S(1)} %get-tuple-element.526) | copy-start | bytes 6148
  31.7 177.2 %copy-start.75 = (f32[1,1,512]{2,1,0:T(1,128)}, f32[1,1,512]{2,1,0:T(1,128)S(1)}, u32[]{:S(2)}) copy-start(f32[1,1,512]{2,1,0:T(1,128)S(1)} %get-tuple-element.527) | copy-start | bytes 6148
  31.7 177.2 %copy-start.77 = (f32[1,1,512]{2,1,0:T(1,128)}, f32[1,1,512]{2,1,0:T(1,128)S(1)}, u32[]{:S(2)}) copy-start(f32[1,1,512]{2,1,0:T(1,128)S(1)} %get-tuple-element.535) | copy-start | bytes 6148
  31.7 177.2 %copy-start.79 = (f32[1,1,512]{2,1,0:T(1,128)}, f32[1,1,512]{2,1,0:T(1,128)S(1)}, u32[]{:S(2)}) copy-start(f32[1,1,512]{2,1,0:T(1,128)S(1)} %get-tuple-element.536) | copy-start | bytes 6148
  31.7 177.2 %copy-start.81 = (f32[1,1,512]{2,1,0:T(1,128)}, f32[1,1,512]{2,1,0:T(1,128)S(1)}, u32[]{:S(2)}) copy-start(f32[1,1,512]{2,1,0:T(1,128)S(1)} %get-tuple-element.528) | copy-start | bytes 6148
  31.7 177.2 %copy-start.83 = (f32[1,1,512]{2,1,0:T(1,128)}, f32[1,1,512]{2,1,0:T(1,128)S(1)}, u32[]{:S(2)}) copy-start(f32[1,1,512]{2,1,0:T(1,128)S(1)} %get-tuple-element.529) | copy-start | bytes 6148
  31.7 177.2 %copy-start.85 = (f32[1,1,512]{2,1,0:T(1,128)}, f32[1,1,512]{2,1,0:T(1,128)S(1)}, u32[]{:S(2)}) copy-start(f32[1,1,512]{2,1,0:T(1,128)S(1)} %get-tuple-element.530) | copy-start | bytes 6148
  31.7 177.2 %copy-start.87 = (f32[1,1,512]{2,1,0:T(1,128)}, f32[1,1,512]{2,1,0:T(1,128)S(1)}, u32[]{:S(2)}) copy-start(f32[1,1,512]{2,1,0:T(1,128)S(1)} %get-tuple-element.531) | copy-start | bytes 6148
  31.7 177.2 %copy-start.89 = (f32[1,1,512]{2,1,0:T(1,128)}, f32[1,1,512]{2,1,0:T(1,128)S(1)}, u32[]{:S(2)}) copy-start(f32[1,1,512]{2,1,0:T(1,128)S(1)} %get-tuple-element.525) | copy-start | bytes 6148
  31.8 177.2 %copy-start.91 = (f32[1,1,512]{2,1,0:T(1,128)}, f32[1,1,512]{2,1,0:T(1,128)S(1)}, u32[]{:S(2)}) copy-start(f32[1,1,512]{2,1,0:T(1,128)S(1)} %get-tuple-element.532) | copy-start | bytes 6148
  31.8 177.2 %copy-start.93 = (f32[1,1,512]{2,1,0:T(1,128)}, f32[1,1,512]{2,1,0:T(1,128)S(1)}, u32[]{:S(2)}) copy-start(f32[1,1,512]{2,1,0:T(1,128)S(1)} %get-tuple-element.533) | copy-start | bytes 6148
  31.8 177.2 %copy-start.95 = (f32[1,1,512]{2,1,0:T(1,128)}, f32[1,1,512]{2,1,0:T(1,128)S(1)}, u32[]{:S(2)}) copy-start(f32[1,1,512]{2,1,0:T(1,128)S(1)} %get-tuple-element.534) | copy-start | bytes 6148
  207.7 16.3 copy-start.23
  228.7 425.5 %copy-start = (f32[1,1024,512]{2,0,1:T(1,128)}, f32[1,1024,512]{2,0,1:T(1,128)S(1)}, u32[]{:S(2)}) copy-start(f32[1,1024,512]{2,0,1:T(1,128)S(1)} %copy.118) | copy-start | bytes 6291460
  232.6 421.6 %copy-start.45 = (f32[16,64,4]{1,2,0:T(4,128)}, f32[16,64,4]{1,2,0:T(4,128)S(1)}, u32[]{:S(2)}) copy-start(f32[16,64,4]{1,2,0:T(4,128)S(1)} %copy.119) | copy-start | bytes 49156
  241.3 325.0 %copy-start.47 = (f32[1,16,64,4]{2,3,1,0:T(4,128)}, f32[1,16,64,4]{2,3,1,0:T(4,128)S(1)}, u32[]{:S(2)}) copy-start(f32[1,16,64,4]{2,3,1,0:T(4,128)S(1)} %copy.223) | copy-start | bytes 49156
  693.5 54.6 %copy-start.62 = (f32[2048]{0:T(1024)S(1)}, f32[2048]{0:T(1024)}, u32[]{:S(2)}) copy-start(f32[2048]{0:T(1024)} %param.32) | copy-start | bytes 24580
  693.5 115.6 %all-gather.27.cloned.1.call-start = ((), (), s32[]{:S(2)}) async-start(), calls=%async_computation.21 | async-start | bytes 6488064 | tf_op jit(solution)/shard_map/all_gather | solution.py:157
  695.9 167.2 %all-gather.25.cloned.1.call-start = ((), (), s32[]{:S(2)}) async-start(), calls=%async_computation.20 | async-start | bytes 5242880 | tf_op jit(solution)/shard_map/all_gather | solution.py:211
  748.2 382.6 %copy-start.70 = (f32[256]{0:T(256)}, f32[256]{0:T(256)S(1)}, u32[]{:S(2)}) copy-start(f32[256]{0:T(256)S(1)} %fusion.184) | copy-start | bytes 3076
  749.7 175.5 %all-gather.29.cloned.1.call-start = ((), (), s32[]{:S(2)}) async-start(), calls=%async_computation.22 | async-start | bytes 6488064 | tf_op jit(solution)/shard_map/all_gather | solution.py:158
  752.1 227.1 %all-gather.33.cloned.1.call-start = ((), (), s32[]{:S(2)}) async-start(), calls=%async_computation.25 | async-start | bytes 5242880 | tf_op jit(solution)/shard_map/all_gather | solution.py:225
  752.8 378.0 %copy-start.99 = (f32[256]{0:T(256)}, f32[256]{0:T(256)S(1)}, u32[]{:S(2)}) copy-start(f32[256]{0:T(256)S(1)} %compare_convert_fusion) | copy-start | bytes 3076
  755.2 286.4 %all-gather.31.cloned.1.call-start = ((), (), s32[]{:S(2)}) async-start(), calls=%async_computation.23 | async-start | bytes 6488064 | tf_op jit(solution)/shard_map/all_gather | solution.py:159
  757.7 369.8 %reduce-scatter.20.cloned.1.call-start = ((), (), s32[]{:S(2)}) async-start(), calls=%async_computation.26 | async-start | bytes 5242880 | tf_op jit(solution)/shard_map/reduce_scatter | solution.py:234
  1057.2 10.9 copy-start.108
  1076.5 109.2 %all-gather.35.cloned.1.call-start = ((), (), s32[]{:S(2)}) async-start(), calls=%async_computation.27 | async-start | bytes 5242880 | tf_op jit(solution)/shard_map/all_gather | solution.py:245
  1132.7 408.7 %reduce-scatter.34.cloned.1.call-start = ((), (), s32[]{:S(2)}) async-start(), calls=%async_computation.34 | async-start | bytes 6488064 | tf_op jit(solution)/shard_map/reduce_scatter | solution.py:287
  1143.8 400.0 %reduce-scatter.36.cloned.1.call-start = ((), (), s32[]{:S(2)}) async-start(), calls=%async_computation.35 | async-start | bytes 6488064 | tf_op jit(solution)/shard_map/reduce_scatter | solution.py:290
  1154.9 391.2 %reduce-scatter.38.cloned.1.call-start = ((), (), s32[]{:S(2)}) async-start(), calls=%async_computation.36 | async-start | bytes 6488064 | tf_op jit(solution)/shard_map/reduce_scatter | solution.py:293
  1171.6 406.3 %reduce-scatter.40.cloned.1.call-start = ((), (), s32[]{:S(2)}) async-start(), calls=%async_computation.37 | async-start | bytes 589824
  1245.4 127.1 %copy-start.15 = (f32[16,4,128,64]{2,3,1,0:T(8,128)S(1)}, f32[16,4,128,64]{2,3,1,0:T(8,128)}, u32[]{:S(2)}) copy-start(f32[16,4,128,64]{2,3,1,0:T(8,128)} %copy-done.14) | copy-start | bytes 6291460
  1388.7 20.4 %copy-start.17 = (f32[1,16,4,64,256]{4,3,2,1,0:T(8,128)}, f32[1,16,4,64,256]{4,3,2,1,0:T(8,128)S(1)}, u32[]{:S(2)}) copy-start(f32[1,16,4,64,256]{4,3,2,1,0:T(8,128)S(1)} %fusion.61) | copy-start | bytes 12582916
  1455.5 12.4 copy-start.61
  1455.5 12.5 copy-start.40
  1500.7 78.7 %reduce-scatter.24.cloned.1.call-start = ((), (), s32[]{:S(2)}) async-start(), calls=%async_computation.29 | async-start | bytes 2359296 | tf_op jit(solution)/shard_map/reduce_scatter | solution.py:269
  1506.8 98.2 %reduce-scatter.26.cloned.1.call-start = ((), (), s32[]{:S(2)}) async-start(), calls=%async_computation.30 | async-start | bytes 2359296 | tf_op jit(solution)/shard_map/reduce_scatter | solution.py:272
  1507.4 134.6 %reduce-scatter.28.cloned.1.call-start = ((), (), s32[]{:S(2)}) async-start(), calls=%async_computation.31 | async-start | bytes 2359296 | tf_op jit(solution)/shard_map/reduce_scatter | solution.py:275
  1508.1 171.1 %reduce-scatter.30.cloned.1.call-start = ((), (), s32[]{:S(2)}) async-start(), calls=%async_computation.32 | async-start | bytes 2359296 | tf_op jit(solution)/shard_map/reduce_scatter | solution.py:278
  1508.9 207.0 %reduce-scatter.32.cloned.1.call-start = ((), (), s32[]{:S(2)}) async-start(), calls=%async_computation.33 | async-start | bytes 2359296 | tf_op jit(solution)/shard_map/reduce_scatter | solution.py:284
  1515.0 255.3 %reduce-scatter.22.cloned.1.call-start = ((), (), s32[]{:S(2)}) async-start(), calls=%async_computation.28 | async-start | bytes 5242880 | tf_op jit(solution)/shard_map/reduce_scatter | solution.py:260
  1530.4 296.0 %reduce-scatter.18.cloned.1.call-start = ((), (), s32[]{:S(2)}) async-start(), calls=%async_computation.24 | async-start | bytes 5242880 | tf_op jit(solution)/shard_map/reduce_scatter | solution.py:217
  1548.4 222.0 %copy-start.8 = (bf16[256,2048]{1,0:T(8,128)(2,1)S(1)}, bf16[256,2048]{1,0:T(8,128)(2,1)}, u32[]{:S(2)}) copy-start(bf16[256,2048]{1,0:T(8,128)(2,1)} %param.20) | copy-start | bytes 3145732
  1548.4 222.0 %copy-start.65 = (f32[2048]{0:T(1024)S(1)}, f32[2048]{0:T(1024)}, u32[]{:S(2)}) copy-start(f32[2048]{0:T(1024)} %param.23) | copy-start | bytes 24580
  1548.4 222.0 %copy-start.98 = (f32[256]{0:T(256)S(1)}, f32[256]{0:T(256)}, u32[]{:S(2)}) copy-start(f32[256]{0:T(256)} %copy-done.97) | copy-start | bytes 3076
  1606.9 165.7 %copy-start.69 = (f32[2048]{0:T(1024)S(1)}, f32[2048]{0:T(1024)}, u32[]{:S(2)}) copy-start(f32[2048]{0:T(1024)} %get-tuple-element.427) | copy-start | bytes 24580
  1606.9 205.9 %copy-start.102 = (f32[256]{0:T(256)S(1)}, f32[256]{0:T(256)}, u32[]{:S(2)}) copy-start(f32[256]{0:T(256)} %copy-done.101) | copy-start | bytes 3076
  1606.9 219.5 %copy-start.20 = (bf16[256,2048]{1,0:T(8,128)(2,1)S(1)}, bf16[256,2048]{1,0:T(8,128)(2,1)}, u32[]{:S(2)}) copy-start(bf16[256,2048]{1,0:T(8,128)(2,1)} %reduce-scatter.16.cloned.1.call-done) | copy-start | bytes 3145732
  1606.9 219.5 %copy-start.36 = (bf16[256,2048]{1,0:T(8,128)(2,1)S(1)}, bf16[256,2048]{1,0:T(8,128)(2,1)}, u32[]{:S(2)}) copy-start(bf16[256,2048]{1,0:T(8,128)(2,1)} %param.21) | copy-start | bytes 3145732
  1606.9 219.5 %copy-start.63 = (f32[2048]{0:T(1024)S(1)}, f32[2048]{0:T(1024)}, u32[]{:S(2)}) copy-start(f32[2048]{0:T(1024)} %param.32) | copy-start | bytes 24580
  1606.9 219.4 %copy-start.71 = (f32[256]{0:T(256)S(1)}, f32[256]{0:T(256)}, u32[]{:S(2)}) copy-start(f32[256]{0:T(256)} %copy-done.70) | copy-start | bytes 3076
  1606.9 219.4 %copy-start.100 = (f32[256]{0:T(256)S(1)}, f32[256]{0:T(256)}, u32[]{:S(2)}) copy-start(f32[256]{0:T(256)} %copy-done.99) | copy-start | bytes 3076
  1606.9 219.4 %copy-start.104 = (f32[256]{0:T(256)S(1)}, f32[256]{0:T(256)}, u32[]{:S(2)}) copy-start(f32[256]{0:T(256)} %copy-done.103) | copy-start | bytes 3076
  (73 other events, 308.2 us)
Sparse Core Ops, SparseCore 0:
  10.2 31.9 all-gather.14
  44.4 28.5 all-gather.16
  75.1 28.5 all-gather.18
  105.8 28.5 all-gather.20
  136.7 52.1 all-gather.12
  190.9 30.8 all-gather.22
  693.6 52.6 reduce-scatter.15
  748.7 60.4 all-gather.26
  811.7 51.3 all-gather.24
  864.7 60.4 all-gather.28
  927.8 51.3 all-gather.32
  980.7 60.8 all-gather.30
  1076.6 50.8 reduce-scatter.19
  1132.9 52.7 all-gather.34
  1187.8 64.8 reduce-scatter.33
  1254.8 63.2 reduce-scatter.35
  1320.2 63.2 reduce-scatter.37
  1500.9 30.8 reduce-scatter.39
  1534.2 34.0 reduce-scatter.23
  1570.5 34.4 reduce-scatter.25
  1607.4 34.4 reduce-scatter.27
  1644.9 34.2 reduce-scatter.29
  1681.7 34.1 reduce-scatter.31
  1718.9 51.3 reduce-scatter.21
  1773.3 53.0 reduce-scatter.17
where the time goes:
time: 1850 us; the launch traced here: 1840 us
  waiting for transfers between devices  716 us (39%)
  other arithmetic  443 us (24%)
  matrix products  442 us (24%)
  local copies, waits for them, and re-layouts  134 us (7%)
  blocking collectives  84.2 us (5%)
    another operation x5, other arithmetic, delta_rule(): lax.linalg.triangular_solve(system, stacked, left_side=True, lower=True,...  320 us
    dot_general x48, matrix products, state_step(): jnp.einsum('hcd,hde->hce', weight_block, state, precision=highest_precision)  93.2 us
    dot_general x48, matrix products, state_step(): jnp.einsum('hcd,hce->hde', key_block, fresh, precision=highest_precision)  89.7 us
    all_gather x1, waiting for transfers between devices, body(): lax.all_gather(w_down.astype(jnp.bfloat16), 'dp', axis=1, tiled=True)  62.4 us
    dot_general x5, matrix products, product_with_transpose(): lax.dot_general(left, right, (((1,), (1,)), ((), ())), preferred_element_...  55.4 us
    all_gather x1, waiting for transfers between devices, body(): lax.all_gather(normed2.astype(jnp.bfloat16), 'tensor', axis=0, tiled=True)  54 us
    reduce_scatter x1, waiting for transfers between devices, body(): lax.psum_scatter(product_with_transpose(grad_pre_low, inner_weights).asty...  52.7 us
    all_gather x1, waiting for transfers between devices, body(): lax.all_gather(w_gate.astype(jnp.bfloat16), 'dp', axis=0, tiled=True)  50.9 us
  transfers between devices with their start and end apart: 25, of which 19 were waited for; matrix products, arithmetic and copies ran while one was open for 52% of the time, Pallas kernels for 0%

commit v1 on v0

v1 whole, which is shorter than its diff:
```python
import functools
import jax
import jax.numpy as jnp
from jax import lax
from jax.experimental import pallas as pl
from jax.experimental.pallas import tpu as pltpu
from jax.sharding import PartitionSpec as P

norm_epsilon = 1e-06
head_epsilon = 1e-05
HEAD = 128
CHUNK = 128
STEP = 256
TAPS = 4
BETA_PAD = 128
VMEM_LIMIT = 56 * 1024 * 1024
f32 = jnp.float32
bf16 = jnp.bfloat16


def mm(a, b):
    return lax.dot_general(a, b, (((1,), (0,)), ((), ())), preferred_element_type=f32)


def mm_nt(a, b):
    return lax.dot_general(a, b, (((1,), (1,)), ((), ())), preferred_element_type=f32)


def mm_tn(a, b):
    return lax.dot_general(a, b, (((0,), (0,)), ((), ())), preferred_element_type=f32)


def chunk_indices():
    row = lax.broadcasted_iota(jnp.int32, (CHUNK, CHUNK), 0)
    col = lax.broadcasted_iota(jnp.int32, (CHUNK, CHUNK), 1)
    return row, col


def unit_lower_inverses(stricts, row, col):
    apart = row ^ col
    inverses = [jnp.where(row == col, 1.0, jnp.where(apart == 1, -strict, 0.0)) for strict in stricts]
    span = 2
    while span < CHUNK:
        here = (apart >= span) & (apart < 2 * span)
        lows = [inverse.astype(bf16) for inverse in inverses]
        firsts = [mm(low, jnp.where(here, strict, 0.0).astype(bf16)).astype(bf16) for low, strict in zip(lows, stricts)]
        inverses = [inverse - mm(first, low) for inverse, first, low in zip(inverses, firsts, lows)]
        span *= 2
    return [inverse.astype(bf16) for inverse in inverses]


def silu_parts(conv):
    sig = jax.nn.sigmoid(conv)
    return conv * sig, sig


def forward_kernel(
    heads, pre_ref, taps_ref, gain_ref, z_ref, conv_ref, mixed_ref, inv_ref, state_ref, hist, state
):
    step = pl.program_id(0)
    width = heads * HEAD
    rows = pre_ref.shape[0]

    @pl.when(step == 0)
    def _():
        hist[0:8, :] = jnp.zeros((8, 3 * width), f32)
        state[...] = jnp.zeros_like(state)

    @pl.when(step > 0)
    def _():
        hist[0:8, :] = hist[rows : rows + 8, :]

    hist[8 : 8 + rows, :] = pre_ref[:, 0 : 3 * width].astype(f32)
    row, col = chunk_indices()
    beta_all = jax.nn.sigmoid(pre_ref[:, 4 * width : 4 * width + BETA_PAD].astype(f32))
    work = []
    for head in range(heads):
        parts = []
        for kind in range(3):
            lanes = slice(kind * width + head * HEAD, kind * width + (head + 1) * HEAD)
            total = taps_ref[kind * TAPS : kind * TAPS + 1, head * HEAD : (head + 1) * HEAD] * hist[5 : 5 + rows, lanes]
            for tap in range(1, TAPS):
                total = total + taps_ref[
                    kind * TAPS + tap : kind * TAPS + tap + 1, head * HEAD : (head + 1) * HEAD
                ] * hist[5 + tap : 5 + tap + rows, lanes]
            conv_ref[:, lanes] = total
            act, _ = silu_parts(total)
            if kind < 2:
                act = act * lax.rsqrt(jnp.sum(act * act, axis=-1, keepdims=True) + norm_epsilon)
            if kind == 0:
                act = act * HEAD ** (-0.5)
            parts.append(act)
        beta = beta_all[:, head : head + 1]
        for part in range(rows // CHUNK):
            here = slice(part * CHUNK, (part + 1) * CHUNK)
            query, key, value = (p[here] for p in parts)
            query_low, key_low = query.astype(bf16), key.astype(bf16)
            b = beta[here]
            stacked = jnp.concatenate([(b * key).astype(bf16), (b * value).astype(bf16)], axis=1)
            strict = jnp.where(row > col, b * mm_nt(key_low, key_low), 0.0)
            scores = jnp.where(row >= col, mm_nt(query_low, key_low), 0.0).astype(bf16)
            work.append((head, part, query_low, key_low, stacked, scores, strict))
    inverses = unit_lower_inverses([item[-1] for item in work], row, col)
    solved_all = {}
    for (head, part, query_low, key_low, stacked, scores, _), inverse in zip(work, inverses):
        inv_ref[head, part] = inverse
        solved_all[part, head] = (query_low, key_low, scores, mm(inverse, stacked))
    states = [state[head] for head in range(heads)]
    for part in range(rows // CHUNK):
        here = slice(part * CHUNK, (part + 1) * CHUNK)
        enters = [enter.astype(bf16) for enter in states]
        items = [solved_all[part, head] for head in range(heads)]
        freshes = [
            (solved[:, HEAD:] - mm(solved[:, :HEAD].astype(bf16), enter)).astype(bf16)
            for (_, _, _, solved), enter in zip(items, enters)
        ]
        states = [old + mm_tn(key_low, fresh) for old, (_, key_low, _, _), fresh in zip(states, items, freshes)]
        for head in range(heads):
            lanes = slice(head * HEAD, (head + 1) * HEAD)
            query_low, _, scores, _ = items[head]
            state_ref[head, part] = enters[head]
            mixed = mm(query_low, enters[head]) + mm(scores, freshes[head])
            mixed_ref[here, lanes] = mixed
            gate = pre_ref[here, 3 * width + head * HEAD : 3 * width + (head + 1) * HEAD].astype(f32)
            gate_act, _ = silu_parts(gate)
            normed = mixed * lax.rsqrt(jnp.mean(mixed * mixed, axis=-1, keepdims=True) + head_epsilon)
            z_ref[here, lanes] = (normed * gain_ref[...] * gate_act).astype(bf16)
    for head in range(heads):
        state[head] = states[head]


def mixer_forward(pre, taps, gain, heads):
    length, total = pre.shape
    width = heads * HEAD
    steps, parts = length // STEP, STEP // CHUNK
    return pl.pallas_call(
        functools.partial(forward_kernel, heads),
        grid=(steps,),
        in_specs=[
            pl.BlockSpec((STEP, total), lambda i: (i, 0)),
            pl.BlockSpec((3 * TAPS, width), lambda i: (0, 0)),
            pl.BlockSpec((1, HEAD), lambda i: (0, 0)),
        ],
        out_specs=[
            pl.BlockSpec((STEP, width), lambda i: (i, 0)),
            pl.BlockSpec((STEP, 3 * width), lambda i: (i, 0)),
            pl.BlockSpec((STEP, width), lambda i: (i, 0)),
            pl.BlockSpec((heads, parts, CHUNK, CHUNK), lambda i: (0, i, 0, 0)),
            pl.BlockSpec((heads, parts, HEAD, HEAD), lambda i: (0, i, 0, 0)),
        ],
        out_shape=[
            jax.ShapeDtypeStruct((length, width), bf16),
            jax.ShapeDtypeStruct((length, 3 * width), f32),
            jax.ShapeDtypeStruct((length, width), f32),
            jax.ShapeDtypeStruct((heads, steps * parts, CHUNK, CHUNK), bf16),
            jax.ShapeDtypeStruct((heads, steps * parts, HEAD, HEAD), bf16),
        ],
        scratch_shapes=[
            pltpu.VMEM((STEP + 8, 3 * width), f32),
            pltpu.VMEM((heads, HEAD, HEAD), f32),
        ],
        compiler_params=pltpu.CompilerParams(
            dimension_semantics=("arbitrary",), vmem_limit_bytes=VMEM_LIMIT
        ),
        cost_estimate=pl.CostEstimate(
            flops=2 * length * width * HEAD * 60, bytes_accessed=length * (total * 4 + width * 24), transcendentals=length * width * 8
        ),
    )(pre, taps, gain)


def backward_kernel(
    heads,
    pre_ref,
    conv_ref,
    mixed_ref,
    dz_ref,
    inv_ref,
    state_ref,
    taps_ref,
    gain_ref,
    dpre_ref,
    dtaps_ref,
    dgain_ref,
    later,
    dstate,
):
    step = pl.program_id(0)
    width = heads * HEAD
    rows = pre_ref.shape[0]
    count = rows // CHUNK

    @pl.when(step == 0)
    def _():
        later[rows : rows + 8, :] = jnp.zeros((8, 3 * width), f32)
        dstate[...] = jnp.zeros_like(dstate)
        dtaps_ref[...] = jnp.zeros_like(dtaps_ref)
        dgain_ref[...] = jnp.zeros_like(dgain_ref)

    @pl.when(step > 0)
    def _():
        later[rows : rows + 8, :] = later[0:8, :]

    row, col = chunk_indices()
    beta_all = jax.nn.sigmoid(pre_ref[:, 4 * width : 4 * width + BETA_PAD].astype(f32))
    beta_lane = lax.broadcasted_iota(jnp.int32, (CHUNK, BETA_PAD), 1)
    dbeta_all = [jnp.zeros((CHUNK, BETA_PAD), f32) for _ in range(count)]
    dgain = jnp.zeros((1, HEAD), f32)
    gain = gain_ref[...]
    every = [(part, head) for part in reversed(range(count)) for head in range(heads)]

    def of(ref, kind, at):
        part, head = at
        lanes = slice(kind * width + head * HEAD, kind * width + (head + 1) * HEAD)
        return ref[part * CHUNK : (part + 1) * CHUNK, lanes].astype(f32)

    betas = {(part, head): beta_all[part * CHUNK : (part + 1) * CHUNK, head : head + 1] for part, head in every}
    unit_queries, keys, query_lows, key_lows, scales, stacks = {}, {}, {}, {}, {}, {}
    for at in every:
        acts = [silu_parts(of(conv_ref, kind, at))[0] for kind in range(3)]
        scales[at] = [lax.rsqrt(jnp.sum(act * act, axis=-1, keepdims=True) + norm_epsilon) for act in acts[:2]]
        unit_queries[at], keys[at] = acts[0] * scales[at][0], acts[1] * scales[at][1]
        query_lows[at] = (unit_queries[at] * HEAD ** (-0.5)).astype(bf16)
        key_lows[at] = keys[at].astype(bf16)
        stacks[at] = jnp.concatenate([(betas[at] * keys[at]).astype(bf16), (betas[at] * acts[2]).astype(bf16)], axis=1)
    solved = {at: mm(inv_ref[at[1], at[0]], stacks[at]) for at in every}
    scores = {at: jnp.where(row >= col, mm_nt(query_lows[at], key_lows[at]), 0.0).astype(bf16) for at in every}
    weights = {at: solved[at][:, :HEAD].astype(bf16) for at in every}
    outs = {}
    for at in every:
        part, head = at
        here = slice(part * CHUNK, (part + 1) * CHUNK)
        gate = of(pre_ref, 3, at)
        gate_act, gate_sig = silu_parts(gate)
        mixed, dz = of(mixed_ref, 0, at), of(dz_ref, 0, at)
        root = lax.rsqrt(jnp.mean(mixed * mixed, axis=-1, keepdims=True) + head_epsilon)
        normed = mixed * root
        dgate = dz * normed * gain * (gate_sig * (1.0 + gate * (1.0 - gate_sig)))
        dpre_ref[here, 3 * width + head * HEAD : 3 * width + (head + 1) * HEAD] = dgate.astype(bf16)
        dgained = dz * gate_act
        dgain = dgain + jnp.sum(dgained * normed, axis=0, keepdims=True)
        dnormed = dgained * gain
        dmixed = root * (dnormed - normed * jnp.mean(dnormed * normed, axis=-1, keepdims=True))
        outs[at] = dmixed.astype(bf16)
    enters = {(part, head): state_ref[head, part] for part, head in every}
    fresh = {at: (solved[at][:, HEAD:] - mm(weights[at], enters[at])).astype(bf16) for at in every}
    within = {at: mm_tn(scores[at], outs[at]) for at in every}
    across = {at: mm_tn(query_lows[at], outs[at]) for at in every}
    leavings, dfresh = {}, {}
    states = [dstate[head] for head in range(heads)]
    for part in reversed(range(count)):
        for head in range(heads):
            leavings[part, head] = states[head].astype(bf16)
        for head in range(heads):
            at = (part, head)
            dfresh[at] = (within[at] + mm(key_lows[at], leavings[at])).astype(bf16)
        for head in range(heads):
            at = (part, head)
            states[head] = states[head] + across[at] - mm_tn(weights[at], dfresh[at])
    for head in range(heads):
        dstate[head] = states[head]
    dscores = {at: jnp.where(row >= col, mm_nt(outs[at], fresh[at]), 0.0).astype(bf16) for at in every}
    dweights = {at: (-mm_nt(dfresh[at], enters[at])).astype(bf16) for at in every}
    dxys = {
        at: mm_tn(inv_ref[at[1], at[0]], jnp.concatenate([dweights[at], dfresh[at]], axis=1)) for at in every
    }
    dqueries = {at: mm_nt(outs[at], enters[at]) + mm(dscores[at], key_lows[at]) for at in every}
    dkeys = {at: mm_tn(dscores[at], query_lows[at]) + mm_nt(fresh[at], leavings[at]) for at in every}
    dsystems = {
        at: jnp.where(row > col, -mm_nt(dxys[at].astype(bf16), solved[at].astype(bf16)), 0.0) for at in every
    }
    dsystem_lows = {at: dsystems[at].astype(bf16) for at in every}
    firsts = {at: mm(dsystem_lows[at], key_lows[at]) for at in every}
    seconds = {at: mm_tn(dsystem_lows[at], stacks[at][:, :HEAD]) for at in every}
    grams = {at: mm_nt(key_lows[at], key_lows[at]) for at in every}
    for at in every:
        part, head = at
        beta, dx, dy, key = betas[at], dxys[at][:, :HEAD], dxys[at][:, HEAD:], keys[at]
        dkey = dkeys[at] + beta * (firsts[at] + dx) + seconds[at]
        convs = [of(conv_ref, kind, at) for kind in range(3)]
        sigs = [jax.nn.sigmoid(conv) for conv in convs]
        dbeta = jnp.sum(dsystems[at] * grams[at] + dx * key + dy * (convs[2] * sigs[2]), axis=-1, keepdims=True)
        dbeta = dbeta * beta * (1.0 - beta)
        dbeta_all[part] = jnp.where(beta_lane == head, dbeta, dbeta_all[part])
        unit_query, dquery = unit_queries[at], dqueries[at] * HEAD ** (-0.5)
        dquery = scales[at][0] * (dquery - unit_query * jnp.sum(unit_query * dquery, axis=-1, keepdims=True))
        dkey = scales[at][1] * (dkey - key * jnp.sum(key * dkey, axis=-1, keepdims=True))
        for kind, grad in enumerate((dquery, dkey, beta * dy)):
            dconv = grad * (sigs[kind] * (1.0 + convs[kind] * (1.0 - sigs[kind])))
            lanes = slice(kind * width + head * HEAD, kind * width + (head + 1) * HEAD)
            later[part * CHUNK : (part + 1) * CHUNK, lanes] = dconv
    for part in range(count):
        dpre_ref[part * CHUNK : (part + 1) * CHUNK, 4 * width : 4 * width + BETA_PAD] = dbeta_all[part].astype(bf16)
    dgain_ref[...] += dgain
    for kind in range(3):
        for head in range(heads):
            lanes = slice(kind * width + head * HEAD, kind * width + (head + 1) * HEAD)
            source = pre_ref[:, lanes].astype(f32)
            total = jnp.zeros((rows, HEAD), f32)
            for tap in range(TAPS):
                at = kind * TAPS + tap
                shifted = later[TAPS - 1 - tap : TAPS - 1 - tap + rows, lanes]
                total = total + taps_ref[at : at + 1, head * HEAD : (head + 1) * HEAD] * shifted
                dtaps_ref[at : at + 1, head * HEAD : (head + 1) * HEAD] += jnp.sum(
                    source * shifted, axis=0, keepdims=True
                )
            dpre_ref[:, lanes] = total.astype(bf16)


def mixer_backward(pre, conv, mixed, dz, inverse, states, taps, gain, heads):
    length, total = pre.shape
    width = heads * HEAD
    steps, parts = length // STEP, STEP // CHUNK
    return pl.pallas_call(
        functools.partial(backward_kernel, heads),
        grid=(steps,),
        in_specs=[
            pl.BlockSpec((STEP, total), lambda i: (steps - 1 - i, 0)),
            pl.BlockSpec((STEP, 3 * width), lambda i: (steps - 1 - i, 0)),
            pl.BlockSpec((STEP, width), lambda i: (steps - 1 - i, 0)),
            pl.BlockSpec((STEP, width), lambda i: (steps - 1 - i, 0)),
            pl.BlockSpec((heads, parts, CHUNK, CHUNK), lambda i: (0, steps - 1 - i, 0, 0)),
            pl.BlockSpec((heads, parts, HEAD, HEAD), lambda i: (0, steps - 1 - i, 0, 0)),
            pl.BlockSpec((3 * TAPS, width), lambda i: (0, 0)),
            pl.BlockSpec((1, HEAD), lambda i: (0, 0)),
        ],
        out_specs=[
            pl.BlockSpec((STEP, total), lambda i: (steps - 1 - i, 0)),
            pl.BlockSpec((3 * TAPS, width), lambda i: (0, 0)),
            pl.BlockSpec((1, HEAD), lambda i: (0, 0)),
        ],
        out_shape=[
            jax.ShapeDtypeStruct((length, total), bf16),
            jax.ShapeDtypeStruct((3 * TAPS, width), f32),
            jax.ShapeDtypeStruct((1, HEAD), f32),
        ],
        scratch_shapes=[
            pltpu.VMEM((STEP + 8, 3 * width), f32),
            pltpu.VMEM((heads, HEAD, HEAD), f32),
        ],
        compiler_params=pltpu.CompilerParams(
            dimension_semantics=("arbitrary",), vmem_limit_bytes=VMEM_LIMIT
        ),
        cost_estimate=pl.CostEstimate(
            flops=2 * length * width * HEAD * 120, bytes_accessed=length * (total * 6 + width * 24), transcendentals=length * width * 8
        ),
    )(pre, conv, mixed, dz, inverse, states, taps, gain)


MESH = pl.DeviceIdType.MESH
TILE = 16
LANES = 128
LARGE_LIMIT = 60 * 1024 * 1024


def remote(source, target, send, receive, **where):
    return pltpu.make_async_remote_copy(
        src_ref=source,
        dst_ref=target,
        send_sem=send,
        recv_sem=receive,
        device_id=where,
        device_id_type=MESH,
    )


def when(condition, action):
    pl.when(condition)(action)


def greet(**where):
    pl.semaphore_signal(
        pltpu.get_barrier_semaphore(), inc=1, device_id=where, device_id_type=MESH
    )


def wait_greetings(count):
    pl.semaphore_wait(pltpu.get_barrier_semaphore(), count)


def plane():
    me = lax.axis_index("tensor")
    across = me + 1 - 2 * lax.rem(me, 2)
    along = lax.rem(me + 2, 4)
    return me, across, along


def chip_and_core():
    index = lax.axis_index("dp")
    return index // 2, lax.rem(index, 2)


def greet_line(chips):
    chip, core = chip_and_core()
    greet(dp=chip * 2 + 1 - core)
    when(chip > 0, lambda: greet(dp=(chip - 1) * 2 + core))
    when(chip < chips - 1, lambda: greet(dp=(chip + 1) * 2 + core))
    return 1 + jnp.where(chip > 0, 1, 0) + jnp.where(chip < chips - 1, 1, 0)


class PlaneGather:
    def __init__(self, own, full, send, receive):
        self.own, self.full, self.send, self.receive = own, full, send, receive
        self.me, self.across, self.along = plane()
        self.far = lax.rem(self.across + 2, 4)
        self.rows = own.shape[0]
        self.half = self.rows // 2

    def slot(self, block, half):
        start = pl.multiple_of(block * self.rows + half * self.half, self.half)
        return self.full.at[pl.ds(start, self.half)]

    def mine(self, half):
        return self.own.at[pl.ds(half * self.half, self.half)]

    def out(self, half, kind):
        where = self.across if kind == 0 else self.along
        at = 2 * kind + half
        return remote(
            self.mine(half), self.slot(self.me, half), self.send.at[at], self.receive.at[at], tensor=where
        )

    def arriving(self, half, kind):
        block = self.across if kind == 0 else self.along
        at = 2 * kind + half
        view = self.slot(block, half)
        return remote(view, view, self.send.at[at], self.receive.at[at], tensor=block)

    def passing(self, kind):
        view = self.slot(self.across if kind == 0 else self.along, kind)
        where = self.along if kind == 0 else self.across
        return remote(view, view, self.send.at[4 + kind], self.receive.at[4 + kind], tensor=where)

    def passed(self, kind):
        view = self.slot(self.far, kind)
        where = self.along if kind == 0 else self.across
        return remote(view, view, self.send.at[4 + kind], self.receive.at[4 + kind], tensor=where)

    def start(self, half):
        for kind in (half, 1 - half):
            self.out(half, kind).start()

    def relay(self, kind):
        self.arriving(kind, kind).wait_recv()
        self.passing(kind).start()

    def finish(self):
        for kind in (0, 1):
            self.arriving(1 - kind, kind).wait_recv()
        for kind in (0, 1):
            self.passed(kind).wait_recv()
            self.passing(kind).wait_send()
            for half in (0, 1):
                self.out(half, kind).wait_send()


class PlaneScatter:
    def __init__(self, part, first, second, stage, send, receive):
        self.part, self.first, self.second, self.stage = part, first, second, stage
        self.send, self.receive = send, receive
        self.me, self.across, self.along = plane()
        self.far = lax.rem(self.across + 2, 4)
        self.rows = part.shape[0] // 4
        self.half = self.rows // 2

    def start_of(self, block, half):
        return pl.multiple_of(block * self.rows + half * self.half, self.half)

    def view(self, block, half):
        return self.part.at[pl.ds(self.start_of(block, half), self.half)]

    def out(self, kind, order):
        where = self.across if kind == 0 else self.along
        at = 2 * kind + order
        return remote(
            self.view(self.far if order == 0 else where, kind),
            self.first.at[at],
            self.send.at[at],
            self.receive.at[at],
            tensor=where,
        )

    def over(self, kind):
        where = self.along if kind == 0 else self.across
        return remote(
            self.stage.at[kind], self.second.at[kind], self.send.at[4 + kind], self.receive.at[4 + kind], tensor=where
        )

    def start_far(self):
        for kind in (0, 1):
            self.out(kind, 0).start()

    def start_near(self, kind):
        self.out(kind, 1).start()

    def relay(self, kind):
        self.out(kind, 0).wait_recv()
        block = self.along if kind == 0 else self.across
        start = self.start_of(block, kind)

        def add(index, carry):
            at = pl.multiple_of(index * TILE, TILE)
            mine = self.part[pl.ds(pl.multiple_of(start + at, TILE), TILE), :].astype(f32)
            other = self.first[2 * kind, pl.ds(at, TILE), :].astype(f32)
            self.stage[kind, pl.ds(at, TILE), :] = (mine + other).astype(bf16)
            return carry

        lax.fori_loop(0, self.half // TILE, add, 0)
        self.over(kind).start()

    def ready(self, kind):
        self.out(kind, 1).wait_recv()
        self.over(kind).wait_recv()

    def tile(self, kind, at):
        start = self.start_of(self.me, kind)
        mine = self.part[pl.ds(pl.multiple_of(start + at, TILE), TILE), :].astype(f32)
        near = self.first[2 * kind + 1, pl.ds(at, TILE), :].astype(f32)
        return mine + near + self.second[kind, pl.ds(at, TILE), :].astype(f32)

    def finish(self):
        for kind in (0, 1):
            for order in (0, 1):
                self.out(kind, order).wait_send()
            self.over(kind).wait_send()


def plane_scatter_scratch(rows, columns):
    half = rows // 2
    return [
        pltpu.VMEM((4, half, columns), bf16),
        pltpu.VMEM((2, half, columns), bf16),
        pltpu.VMEM((2, half, columns), bf16),
        pltpu.SemaphoreType.DMA((6,)),
        pltpu.SemaphoreType.DMA((6,)),
    ]


def pieces_of(arrays, size):
    found = []
    for index, array in enumerate(arrays):
        rows, columns = array.shape[-2:]
        count = max(1, min(rows // 64, round(rows * columns / size)))
        while rows % count or (rows // count) % 16:
            count -= 1
        for piece in range(count):
            found.append((index, piece * (rows // count), rows // count))
    return found


PIECE = 64 * 2176


class LineGather:
    def __init__(self, chips, owns, fulls, sems):
        self.chips, self.owns, self.fulls = chips, owns, fulls
        self.pieces = pieces_of(owns, PIECE)
        self.right_send, self.right_receive, self.left_send, self.left_receive = sems[:4]
        self.core_send, self.core_receive, self.local = sems[4:]
        self.chip, self.core = chip_and_core()

    @staticmethod
    def scratch(chips, pieces, arrays):
        return [pltpu.SemaphoreType.DMA((chips, pieces)) for _ in range(6)] + [pltpu.SemaphoreType.DMA((arrays,))]

    def slot(self, piece, chip, core):
        index, start, rows = self.pieces[piece]
        return self.fulls[index].at[chip * 2 + core, pl.ds(start, rows)]

    def source(self, piece, away):
        index, start, rows = self.pieces[piece]
        return self.owns[index].at[pl.ds(start, rows)]

    def right(self, piece, away, chip):
        slot = self.slot(piece, chip, self.core)
        source = self.source(piece, 0) if away == 0 else slot
        to = (self.chip + 1) * 2 + self.core
        return remote(source, slot, self.right_send.at[away, piece], self.right_receive.at[away, piece], dp=to)

    def left(self, piece, away, chip):
        slot = self.slot(piece, chip, self.core)
        source = self.source(piece, 0) if away == 0 else slot
        to = (self.chip - 1) * 2 + self.core
        return remote(source, slot, self.left_send.at[away, piece], self.left_receive.at[away, piece], dp=to)

    def trade(self, piece, chip, own):
        slot = self.slot(piece, chip, self.core)
        source = self.source(piece, 0) if own else slot
        to = self.chip * 2 + 1 - self.core
        return remote(source, slot, self.core_send.at[chip, piece], self.core_receive.at[chip, piece], dp=to)

    def keep(self, index):
        return pltpu.make_async_copy(
            self.owns[index], self.fulls[index].at[self.chip * 2 + self.core], self.local.at[index]
        )

    def start(self):
        for piece in range(len(self.pieces)):
            when(self.chip < self.chips - 1, lambda: self.right(piece, 0, self.chip).start())
            when(self.chip > 0, lambda: self.left(piece, 0, self.chip).start())
        for piece in range(len(self.pieces)):
            self.trade(piece, self.chip, True).start()
        for index in range(len(self.owns)):
            self.keep(index).start()

    def step(self, away):
        for piece in range(len(self.pieces)):

            def from_left():
                chip = self.chip - away
                self.right(piece, away - 1, chip).wait_recv()
                if away < self.chips - 1:
                    when(self.chip < self.chips - 1, lambda: self.right(piece, away, chip).start())
                self.trade(piece, chip, False).start()

            def from_right():
                chip = self.chip + away
                self.left(piece, away - 1, chip).wait_recv()
                if away < self.chips - 1:
                    when(self.chip > 0, lambda: self.left(piece, away, chip).start())
                self.trade(piece, chip, False).start()

            when(self.chip >= away, from_left)
            when(self.chip + away < self.chips, from_right)

    def finish(self):
        for index in range(len(self.owns)):
            self.keep(index).wait()
        for piece in range(len(self.pieces)):
            for away in range(self.chips - 1):
                when(
                    (self.chip < self.chips - 1) & (self.chip >= away),
                    lambda: self.right(piece, away, self.chip - away).wait_send(),
                )
                when(
                    (self.chip > 0) & (self.chip + away < self.chips),
                    lambda: self.left(piece, away, self.chip + away).wait_send(),
                )
            for chip in range(self.chips):
                trade = remote(
                    self.slot(piece, chip, self.core),
                    self.slot(piece, chip, 1 - self.core),
                    self.core_send.at[chip, piece],
                    self.core_receive.at[chip, piece],
                    dp=self.chip * 2 + 1 - self.core,
                )
                trade.wait_send()
                trade.wait_recv()


def first_gather_kernel(chips, *refs):
    w_query, w_key, w_value, w_gate_out, w_beta, w_output, inputs, cotangent, mask, gain = refs[:10]
    w_gate, w_up, w_down = refs[10:13]
    inner_full, output_full, normed_full, grad_full, gate_up, down, grad = refs[13:20]
    inner, output, normed, gate_wide, up_wide, down_wide = refs[20:26]
    sems = refs[26:]
    width, hidden = w_query.shape[1], w_gate.shape[1]
    line = LineGather(chips, [inner, output], [inner_full, output_full], sems[:7])
    rows = [PlaneGather(normed, normed_full, *sems[7:9]), PlaneGather(grad, grad_full, *sems[9:11])]
    local = sems[11]
    keeps = [
        pltpu.make_async_copy(
            own, full.at[pl.ds(pl.multiple_of(each.me * each.rows, each.rows), each.rows)], local.at[at]
        )
        for at, (own, full, each) in enumerate(((normed, normed_full, rows[0]), (grad, grad_full, rows[1])))
    ]
    loads = [
        pltpu.make_async_copy(source, target, local.at[2 + at])
        for at, (source, target) in enumerate(((w_gate, gate_wide), (w_up, up_wide), (w_down, down_wide)))
    ]
    greetings = greet_line(chips)
    greet(tensor=rows[0].across)
    greet(tensor=rows[0].along)
    for kind, weight in enumerate((w_query, w_key, w_value, w_gate_out)):
        inner[:, kind * width : (kind + 1) * width] = weight[...].astype(bf16)
    inner[:, 4 * width :] = jnp.zeros((inner.shape[0], BETA_PAD), bf16)
    inner[:, 4 * width : 4 * width + w_beta.shape[1]] = w_beta[...].astype(bf16)
    output[...] = jnp.transpose(w_output[...]).astype(bf16)
    wait_greetings(2 + greetings)
    line.start()
    for load in loads:
        load.start()

    def norm(index, carry):
        here = pl.ds(pl.multiple_of(index * TILE, TILE), TILE)
        value = inputs[here, :].astype(f32)
        scale = lax.rsqrt(jnp.mean(value * value, axis=-1, keepdims=True) + norm_epsilon)
        normed[here, :] = (value * scale * gain[...]).astype(bf16)
        grad[here, :] = (cotangent[here, :].astype(f32) * mask[here, :]).astype(bf16)
        return carry

    lax.fori_loop(0, inputs.shape[0] // TILE, norm, 0)
    for each in rows:
        each.start(0)
        each.start(1)
    for keep in keeps:
        keep.start()
    for load in loads:
        load.wait()
    for kind, wide in enumerate((gate_wide, up_wide)):
        for tile in range(hidden // LANES):
            to = (2 * tile + kind) * LANES
            gate_up[:, to : to + LANES] = wide[:, tile * LANES : (tile + 1) * LANES].astype(bf16)
    down[...] = jnp.transpose(down_wide[...]).astype(bf16)
    rows[0].relay(0)
    rows[0].relay(1)
    line.step(1)
    rows[1].relay(0)
    rows[1].relay(1)
    for away in range(2, chips):
        line.step(away)
    for each in rows:
        each.finish()
    for keep in keeps:
        keep.wait()
    line.finish()


def ffn_kernel(normed, weight, middle, slopes):
    def block(index, carry):
        here = pl.ds(pl.multiple_of(index * 512, 512), 512)
        both = mm(normed[here, :], weight[...])
        gate, up_part = both[:, :LANES], both[:, LANES:]
        act, sig = silu_parts(gate)
        middle[here, :] = (act * up_part).astype(bf16)
        slopes[here, :LANES] = (up_part * sig * (1.0 + gate * (1.0 - sig))).astype(bf16)
        slopes[here, LANES:] = act.astype(bf16)
        return carry

    lax.fori_loop(0, normed.shape[0] // 512, block, 0, unroll=True)


def ffn(normed, gate_up):
    length, model = normed.shape
    hidden = gate_up.shape[1] // 2
    return pl.pallas_call(
        ffn_kernel,
        grid=(hidden // LANES,),
        in_specs=[
            pl.BlockSpec((length, model), lambda i: (0, 0)),
            pl.BlockSpec((model, 2 * LANES), lambda i: (0, i)),
        ],
        out_specs=[
            pl.BlockSpec((length, LANES), lambda i: (0, i)),
            pl.BlockSpec((length, 2 * LANES), lambda i: (0, i)),
        ],
        out_shape=[
            jax.ShapeDtypeStruct((length, hidden), bf16),
            jax.ShapeDtypeStruct((length, 2 * hidden), bf16),
        ],
        compiler_params=pltpu.CompilerParams(
            dimension_semantics=("arbitrary",), vmem_limit_bytes=VMEM_LIMIT
        ),
        cost_estimate=pl.CostEstimate(
            flops=4 * length * model * hidden, bytes_accessed=2 * (length * model + 2 * model * hidden), transcendentals=length * hidden
        ),
    )(normed, gate_up)


def ffn_backward_kernel(grad, weight, slopes, grad_both):
    grad_middle = mm(grad[...], weight[...])
    for tile in range(weight.shape[1] // LANES):
        part = grad_middle[:, tile * LANES : (tile + 1) * LANES]
        for kind in range(2):
            lanes = slice((2 * tile + kind) * LANES, (2 * tile + kind + 1) * LANES)
            grad_both[:, lanes] = (part * slopes[:, lanes].astype(f32)).astype(bf16)


def ffn_backward(grad, down, slopes):
    length, model = grad.shape
    hidden = down.shape[1]
    block = 512
    return pl.pallas_call(
        ffn_backward_kernel,
        grid=(length // block,),
        in_specs=[
            pl.BlockSpec((block, model), lambda i: (i, 0)),
            pl.BlockSpec((model, hidden), lambda i: (0, 0)),
            pl.BlockSpec((block, 2 * hidden), lambda i: (i, 0)),
        ],
        out_specs=pl.BlockSpec((block, 2 * hidden), lambda i: (i, 0)),
        out_shape=jax.ShapeDtypeStruct((length, 2 * hidden), bf16),
        compiler_params=pltpu.CompilerParams(
            dimension_semantics=("arbitrary",), vmem_limit_bytes=VMEM_LIMIT
        ),
        cost_estimate=pl.CostEstimate(
            flops=2 * length * model * hidden, bytes_accessed=2 * (length * model + model * hidden + 4 * length * hidden), transcendentals=0
        ),
    )(grad, down, slopes)


def finish_kernel(count, *refs):
    both, down = refs[:2]
    sources, gate_out, up_out, down_out = refs[2 : 2 + count], *refs[2 + count : 5 + count]
    targets, held, sems = refs[5 + count : 5 + 2 * count], refs[5 + 2 * count : 5 + 3 * count], refs[-1]
    loads = [
        pltpu.make_async_copy(source, here, sems.at[0, at]) for at, (source, here) in enumerate(zip(sources, held))
    ]
    stores = [
        pltpu.make_async_copy(here, target, sems.at[1, at]) for at, (here, target) in enumerate(zip(held, targets))
    ]
    for load in loads:
        load.start()
    for tile in range(gate_out.shape[1] // LANES):
        lanes = slice(tile * LANES, (tile + 1) * LANES)
        gate_out[:, lanes] = both[:, 2 * tile * LANES : (2 * tile + 1) * LANES].astype(f32)
        up_out[:, lanes] = both[:, (2 * tile + 1) * LANES : (2 * tile + 2) * LANES].astype(f32)
    for load, store in zip(loads, stores):
        load.wait()
        store.start()
    for tile in range(gate_out.shape[1] // LANES):
        lanes = slice(tile * LANES, (tile + 1) * LANES)
        down_out[lanes, :] = jnp.transpose(down[:, lanes].astype(f32))
    for store in stores:
        store.wait()


def finish(both, down, arrays):
    slab, hidden = down.shape
    return pl.pallas_call(
        functools.partial(finish_kernel, len(arrays)),
        in_specs=in_vmem(2) + anywhere(len(arrays)),
        out_specs=in_vmem(3) + anywhere(len(arrays)),
        out_shape=[
            jax.ShapeDtypeStruct((slab, hidden), f32),
            jax.ShapeDtypeStruct((slab, hidden), f32),
            jax.ShapeDtypeStruct((hidden, slab), f32),
        ]
        + [jax.ShapeDtypeStruct(array.shape, array.dtype) for array in arrays],
        scratch_shapes=[pltpu.VMEM(array.shape, array.dtype) for array in arrays]
        + [pltpu.SemaphoreType.DMA((2, len(arrays)))],
        compiler_params=pltpu.CompilerParams(vmem_limit_bytes=VMEM_LIMIT),
        cost_estimate=pl.CostEstimate(flops=0, bytes_accessed=40 * slab * hidden, transcendentals=0),
    )(both, down, *arrays)


def plain_ffn(normed, gate_up):
    gate, up_part = jnp.split(jnp.dot(normed, gate_up, preferred_element_type=f32), 2, axis=1)
    act, sig = silu_parts(gate)
    slopes = jnp.concatenate([up_part * sig * (1.0 + gate * (1.0 - sig)), act], axis=1)
    return (act * up_part).astype(bf16), slopes.astype(bf16)


def plain_ffn_backward(grad, down, slopes):
    grad_middle = jnp.dot(grad, down, preferred_element_type=f32)
    return (jnp.concatenate([grad_middle, grad_middle], axis=1) * slopes.astype(f32)).astype(bf16)


def plain_finish(both, down, arrays):
    gate, up_part = jnp.split(both.astype(f32), 2, axis=1)
    return gate, up_part, down.astype(f32).T, *arrays


def anywhere(count):
    return [pl.BlockSpec(memory_space=pl.ANY)] * count


def in_vmem(count):
    return [pl.BlockSpec(memory_space=pltpu.VMEM)] * count


def first_gather(w_query, w_key, w_value, w_gate_out, w_beta, w_output, inputs, cotangent, mask, gain, w_gate, w_up, w_down):
    shards = lax.axis_size("dp")
    rows, model = inputs.shape
    slab, width = w_query.shape
    hidden = w_gate.shape[1]
    inner = jax.ShapeDtypeStruct((slab, 4 * width + BETA_PAD), bf16)
    output = jax.ShapeDtypeStruct((slab, width), bf16)
    pieces = len(pieces_of([inner, output], PIECE))
    return pl.pallas_call(
        functools.partial(first_gather_kernel, shards // 2),
        in_specs=in_vmem(10) + anywhere(3),
        out_specs=anywhere(4) + in_vmem(3),
        out_shape=[
            jax.ShapeDtypeStruct((shards, *inner.shape), bf16),
            jax.ShapeDtypeStruct((shards, *output.shape), bf16),
            jax.ShapeDtypeStruct((4 * rows, model), bf16),
            jax.ShapeDtypeStruct((4 * rows, model), bf16),
            jax.ShapeDtypeStruct((slab, 2 * hidden), bf16),
            jax.ShapeDtypeStruct((slab, hidden), bf16),
            jax.ShapeDtypeStruct((rows, model), bf16),
        ],
        scratch_shapes=[
            pltpu.VMEM(inner.shape, bf16),
            pltpu.VMEM(output.shape, bf16),
            pltpu.VMEM((rows, model), bf16),
            pltpu.VMEM((slab, hidden), f32),
            pltpu.VMEM((slab, hidden), f32),
            pltpu.VMEM((hidden, slab), f32),
        ]
        + LineGather.scratch(shards // 2, pieces, 2)
        + [pltpu.SemaphoreType.DMA((6,)) for _ in range(4)]
        + [pltpu.SemaphoreType.DMA((5,))],
        compiler_params=pltpu.CompilerParams(
            collective_id=1, has_side_effects=True, vmem_limit_bytes=VMEM_LIMIT
        ),
        cost_estimate=pl.CostEstimate(flops=80_000_000_000, bytes_accessed=20_000_000, transcendentals=0),
    )(w_query, w_key, w_value, w_gate_out, w_beta, w_output, inputs, cotangent, mask, gain, w_gate, w_up, w_down)


def branch_kernel(z, weight, inputs, gain, resid, full, part, first, second, stage, low, s_send, s_recv, g_send, g_recv, local):
    scatter = PlaneScatter(part, first, second, stage, s_send, s_recv)
    gather = PlaneGather(low, full, g_send, g_recv)
    rows = scatter.rows
    slab = weight.shape[1]
    greet(tensor=scatter.across)
    greet(tensor=scatter.along)

    def compute(block):
        here = pl.ds(scatter.start_of(block, 0), rows)

        def column(index, carry):
            part[here, pl.ds(pl.multiple_of(index * slab, slab), slab)] = mm_nt(z[here, :], weight[index]).astype(bf16)
            return carry

        lax.fori_loop(0, weight.shape[0], column, 0)

    compute(scatter.far)
    wait_greetings(2)
    scatter.start_far()
    compute(scatter.across)
    scatter.start_near(0)
    compute(scatter.along)
    scatter.start_near(1)
    compute(scatter.me)
    scatter.relay(0)
    scatter.relay(1)
    for half in (0, 1):
        scatter.ready(half)

        def norm(index, carry):
            at = pl.multiple_of(index * TILE, TILE)
            here = pl.ds(pl.multiple_of(half * scatter.half + at, TILE), TILE)
            value = inputs[here, :].astype(f32) + scatter.tile(half, at)
            resid[here, :] = value
            scale = lax.rsqrt(jnp.mean(value * value, axis=-1, keepdims=True) + norm_epsilon)
            low[here, :] = (value * scale * gain[...]).astype(bf16)
            return carry

        lax.fori_loop(0, scatter.half // TILE, norm, 0)
        gather.start(half)
    keep = pltpu.make_async_copy(low, full.at[pl.ds(pl.multiple_of(gather.me * rows, rows), rows)], local.at[0])
    keep.start()
    gather.relay(0)
    gather.relay(1)
    scatter.finish()
    gather.finish()
    keep.wait()


def branch_and_norm(z, weight, inputs, gain):
    rows, model = inputs.shape
    return pl.pallas_call(
        branch_kernel,
        in_specs=in_vmem(4),
        out_specs=in_vmem(1) + anywhere(1),
        out_shape=[
            jax.ShapeDtypeStruct((rows, model), f32),
            jax.ShapeDtypeStruct((4 * rows, model), bf16),
        ],
        scratch_shapes=[pltpu.VMEM((4 * rows, model), bf16)]
        + plane_scatter_scratch(rows, model)[:3]
        + [pltpu.VMEM((rows, model), bf16)]
        + [pltpu.SemaphoreType.DMA((6,)) for _ in range(4)]
        + [pltpu.SemaphoreType.DMA((1,))],
        compiler_params=pltpu.CompilerParams(
            collective_id=2, has_side_effects=True, vmem_limit_bytes=VMEM_LIMIT
        ),
        cost_estimate=pl.CostEstimate(flops=50_000_000_000, bytes_accessed=20_000_000, transcendentals=0),
    )(z, weight, inputs, gain)


def norm_backward(value, grad, gain):
    scale = lax.rsqrt(jnp.mean(value * value, axis=-1, keepdims=True) + norm_epsilon)
    normed = value * scale
    inner = grad * gain
    return scale * (inner - normed * jnp.mean(inner * normed, axis=-1, keepdims=True)), grad * normed


class LineScatter:
    def __init__(self, chips, parts, stages, trades, arrived, sems):
        self.chips, self.parts, self.stages, self.trades, self.arrived = chips, parts, stages, trades, arrived
        self.pieces = pieces_of(parts, PIECE)
        self.right_send, self.right_receive, self.left_send, self.left_receive = sems[:4]
        self.core_send, self.core_receive, self.local = sems[4:]
        self.chip, self.core = chip_and_core()

    @staticmethod
    def scratch(chips, arrays):
        shapes = [array.shape[-2:] for array in arrays]
        pieces = len(pieces_of(arrays, PIECE))
        return (
            [pltpu.VMEM((chips, *shape), bf16) for shape in shapes]
            + [pltpu.VMEM((chips, *shape), bf16) for shape in shapes]
            + [pltpu.VMEM((chips + 1, *shape), bf16) for shape in shapes]
            + [pltpu.SemaphoreType.DMA((chips, pieces)) for _ in range(6)]
            + [pltpu.SemaphoreType.DMA((len(arrays), chips))]
        )

    def order(self):
        order = []
        for step in range(self.chips // 2):
            order += [self.chips - 1 - step, step]
        return order

    def trade(self, piece, dest):
        index, start, rows = self.pieces[piece]
        return remote(
            self.parts[index].at[dest * 2 + 1 - self.core, pl.ds(start, rows)],
            self.trades[index].at[dest, pl.ds(start, rows)],
            self.core_send.at[dest, piece],
            self.core_receive.at[dest, piece],
            dp=self.chip * 2 + 1 - self.core,
        )

    def load(self, index, dest):
        return pltpu.make_async_copy(
            self.parts[index].at[dest * 2 + self.core], self.stages[index].at[dest], self.local.at[index, dest]
        )

    def right(self, piece, dest):
        index, start, rows = self.pieces[piece]
        here = pl.ds(start, rows)
        return remote(
            self.stages[index].at[dest, here],
            self.arrived[index].at[dest, here],
            self.right_send.at[dest, piece],
            self.right_receive.at[dest, piece],
            dp=(self.chip + 1) * 2 + self.core,
        )

    def left_slot(self, dest, chip):
        return jnp.where(dest == chip, self.chips, dest)

    def left(self, piece, dest):
        index, start, rows = self.pieces[piece]
        here = pl.ds(start, rows)
        return remote(
            self.stages[index].at[dest, here],
            self.arrived[index].at[self.left_slot(dest, self.chip - 1), here],
            self.left_send.at[dest, piece],
            self.left_receive.at[dest, piece],
            dp=(self.chip - 1) * 2 + self.core,
        )

    def start(self):
        for dest in self.order():
            for index in range(len(self.parts)):
                self.load(index, dest).start()
            for piece in range(len(self.pieces)):
                self.trade(piece, dest).start()

    def add(self, piece, dest, slots, put=None):
        index, start, rows = self.pieces[piece]

        def tile(at, carry):
            here = pl.ds(pl.multiple_of(start + at * TILE, TILE), TILE)
            total = self.stages[index][dest, here, :].astype(f32) + self.trades[index][dest, here, :].astype(f32)
            for slot in slots:
                total = total + self.arrived[index][slot, here, :].astype(f32)
            if put is None:
                self.stages[index][dest, here, :] = total.astype(bf16)
            else:
                put[index](here, total)
            return carry

        lax.fori_loop(0, rows // TILE, tile, 0)

    def first_of(self, piece):
        return piece == 0 or self.pieces[piece - 1][0] != self.pieces[piece][0]

    def receive(self, piece, dest):
        if self.first_of(piece):
            self.load(self.pieces[piece][0], dest).wait()
        self.trade(piece, dest).wait_recv()

    def step(self, step, ends):
        to_right, to_left = self.chips - 1 - step, step

        def send_right(piece):
            self.receive(piece, to_right)
            if not ends:
                self.right(piece, to_right).wait_recv()
            self.add(piece, to_right, [] if ends else [to_right])
            self.right(piece, to_right).start()

        def send_left(piece):
            self.receive(piece, to_left)
            if not ends:
                self.left(piece, to_left).wait_recv()
            self.add(piece, to_left, [] if ends else [to_left])
            self.left(piece, to_left).start()

        count = len(self.pieces)
        if ends:
            when(self.chip == 0, lambda: [send_right(piece) for piece in range(count)] and None)
            when(self.chip == self.chips - 1, lambda: [send_left(piece) for piece in range(count)] and None)
            return
        inner_right = (self.chip > 0) & (to_right > self.chip)
        inner_left = (self.chip < self.chips - 1) & (to_left < self.chip)
        low = self.chip < self.chips // 2
        lead = 2
        for at in range(count + lead):
            early, late = at, at - lead
            if early < count:
                when(low & inner_right, functools.partial(send_right, early))
                when(jnp.logical_not(low) & inner_left, functools.partial(send_left, early))
            if late >= 0:
                when(low & inner_left, functools.partial(send_left, late))
                when(jnp.logical_not(low) & inner_right, functools.partial(send_right, late))

    def keep(self, outs, pieces):
        me = self.chip
        for piece in pieces:
            self.receive(piece, me)
            when(me > 0, lambda: self.right(piece, me).wait_recv())
            when(me < self.chips - 1, lambda: self.left(piece, me).wait_recv())
            when((me > 0) & (me < self.chips - 1), lambda: self.add(piece, me, [me, self.chips], outs))
            when(me == 0, lambda: self.add(piece, me, [self.chips], outs))
            when(me == self.chips - 1, lambda: self.add(piece, me, [me], outs))

    def finish(self):
        for piece in range(len(self.pieces)):
            for dest in range(self.chips):
                self.trade(piece, dest).wait_send()
                when(dest > self.chip, lambda: self.right(piece, dest).wait_send())
                when(dest < self.chip, lambda: self.left(piece, dest).wait_send())


def resid_kernel(
    slab, grad_far, weight_far, resid, grad_out, gain, grad_resid, full, dgain,
    part, first, second, stage, low, s_send, s_recv, g_send, g_recv, local, grad_both, weight, load_sems
):
    scatter = PlaneScatter(part, first, second, stage, s_send, s_recv)
    gather = PlaneGather(low, full, g_send, g_recv)
    rows = scatter.rows
    greet(tensor=scatter.across)
    greet(tensor=scatter.along)

    slabs = weight.shape[0] // slab
    order = (scatter.far, scatter.across, scatter.along, scatter.me)

    def rows_load(at):
        here = pl.ds(scatter.start_of(order[at], 0), rows)
        return pltpu.make_async_copy(grad_far.at[here], grad_both.at[here], load_sems.at[slabs + at])

    def slab_load(index):
        here = pl.ds(pl.multiple_of(index * slab, slab), slab)
        return pltpu.make_async_copy(weight_far.at[here], weight.at[here], load_sems.at[index])

    rows_load(0).start()
    for index in range(slabs):
        slab_load(index).start()
    for at in range(1, 4):
        rows_load(at).start()

    def compute(at):
        here = pl.ds(scatter.start_of(order[at], 0), rows)
        rows_load(at).wait()

        def column(index, carry):
            lanes = pl.ds(pl.multiple_of(index * slab, slab), slab)
            if at == 0:
                slab_load(index).wait()
            part[here, lanes] = mm_nt(grad_both[here, :], weight[lanes, :]).astype(bf16)
            return carry

        lax.fori_loop(0, slabs, column, 0)

    compute(0)
    wait_greetings(2)
    scatter.start_far()
    compute(1)
    scatter.start_near(0)
    compute(2)
    scatter.start_near(1)
    compute(3)
    dgain[...] = jnp.zeros_like(dgain)
    scatter.relay(0)
    scatter.relay(1)
    for half in (0, 1):
        scatter.ready(half)

        def norm(index, carry):
            at = pl.multiple_of(index * TILE, TILE)
            here = pl.ds(pl.multiple_of(half * scatter.half + at, TILE), TILE)
            back, gain_part = norm_backward(resid[here, :], scatter.tile(half, at), gain[...])
            value = grad_out[here, :].astype(f32) + back
            grad_resid[here, :] = value
            low[here, :] = value.astype(bf16)
            dgain[...] += jnp.sum(gain_part, axis=0, keepdims=True)
            return carry

        lax.fori_loop(0, scatter.half // TILE, norm, 0)
        gather.start(half)
    keep = pltpu.make_async_copy(low, full.at[pl.ds(pl.multiple_of(gather.me * rows, rows), rows)], local.at[0])
    keep.start()
    gather.relay(0)
    gather.relay(1)
    scatter.finish()
    gather.finish()
    keep.wait()


def resid_backward(grad_both, weight, resid, grad_out, gain):
    rows, model = resid.shape
    return pl.pallas_call(
        functools.partial(resid_kernel, 256),
        in_specs=anywhere(2) + in_vmem(3),
        out_specs=in_vmem(1) + anywhere(1) + in_vmem(1),
        out_shape=[
            jax.ShapeDtypeStruct((rows, model), f32),
            jax.ShapeDtypeStruct((4 * rows, model), bf16),
            jax.ShapeDtypeStruct((1, model), f32),
        ],
        scratch_shapes=[pltpu.VMEM((4 * rows, model), bf16)]
        + plane_scatter_scratch(rows, model)[:3]
        + [pltpu.VMEM((rows, model), bf16)]
        + [pltpu.SemaphoreType.DMA((6,)) for _ in range(4)]
        + [
            pltpu.SemaphoreType.DMA((1,)),
            pltpu.VMEM(grad_both.shape, bf16),
            pltpu.VMEM(weight.shape, bf16),
            pltpu.SemaphoreType.DMA((model // 256 + 4,)),
        ],
        compiler_params=pltpu.CompilerParams(
            collective_id=3, has_side_effects=True, vmem_limit_bytes=VMEM_LIMIT
        ),
        cost_estimate=pl.CostEstimate(flops=60_000_000_000, bytes_accessed=30_000_000, transcendentals=0),
    )(grad_both, weight, resid, grad_out, gain)


SMALL = 512


def last_kernel(chips, *refs):
    inner_part, output_part, weight, inner, dpre_far, middle_far, inputs_far, grad_resid_far, resid_far = refs[:9]
    mask, first_gain, ffn_dgain, head_dgain, dtaps = refs[9:14]
    query_out, key_out, value_out, gate_out, beta_out, output_out, input_grad, out = refs[14:22]
    first_out, ffn_out, head_out, taps_out = refs[22:26]
    refs = refs[26:]
    line = LineScatter(chips, [inner_part, output_part], refs[:2], refs[2:4], refs[4:6], refs[6:13])
    grad = PlaneScatter(*refs[13:19])
    ffn = PlaneScatter(*refs[19:25])
    turned, small, near, lined, dgain, small_send, small_receive, inner_slabs, down_slabs, slab_sems = refs[25:35]
    dpre, middle, inputs, grad_resid, resid, load_sems = refs[35:41]
    chip, core = line.chip, line.core
    slab = inner_part.shape[1]
    shards = 2 * chips
    sibling = chip * 2 + 1 - core
    greet(tensor=grad.across)
    greet(tensor=grad.along)
    greet(dp=sibling)
    for other in range(1, chips):
        greet(dp=lax.rem(chip + other, chips) * 2 + core)

    def stream(at, source, buffers, kind):
        return pltpu.make_async_copy(source.at[at], buffers.at[lax.rem(at, 2)], slab_sems.at[kind, lax.rem(at, 2)])

    def product(left, source, buffers, target, kind):
        def column(index, carry):
            when(index < shards - 1, lambda: stream(index + 1, source, buffers, kind).start())
            stream(index, source, buffers, kind).wait()
            lanes = pl.ds(pl.multiple_of(index * slab, slab), slab)
            target[:, lanes] = mm_nt(left[...], buffers[lax.rem(index, 2)]).astype(bf16)
            return carry

        lax.fori_loop(0, shards, column, 0)

    loads = [
        pltpu.make_async_copy(source, target, load_sems.at[at])
        for at, (source, target) in enumerate(
            (
                (dpre_far, dpre),
                (middle_far, middle),
                (inputs_far, inputs),
                (grad_resid_far, grad_resid),
                (resid_far, resid),
            )
        )
    ]
    wait_greetings(2 + chips)
    line.start()
    for load in loads[:2]:
        load.start()
    stream(0, inner, inner_slabs, 0).start()
    stream(0, weight, down_slabs, 1).start()
    for load in loads[2:]:
        load.start()
    dgain[...] = jnp.zeros_like(dgain)
    small[...] = jnp.zeros_like(small)
    line.step(0, True)
    loads[0].wait()
    product(dpre, inner, inner_slabs, grad.part, 0)
    grad.start_far()
    grad.start_near(0)
    grad.start_near(1)
    line.step(1, True)
    line.step(0, False)
    loads[1].wait()
    product(middle, weight, down_slabs, ffn.part, 1)
    grad.relay(0)
    grad.relay(1)
    ffn.start_far()
    ffn.start_near(0)
    ffn.start_near(1)
    for step in range(2, chips - 1):
        line.step(step, True)
    for step in range(1, chips - 1):
        line.step(step, False)
    for load in loads[2:]:
        load.wait()
    for half in (0, 1):
        grad.ready(half)

        def norm(index, carry):
            at = pl.multiple_of(index * TILE, TILE)
            here = pl.ds(pl.multiple_of(half * grad.half + at, TILE), TILE)
            back, gain_part = norm_backward(inputs[here, :].astype(f32), grad.tile(half, at), first_gain[...])
            input_grad[here, :] = grad_resid[here, :] + back
            dgain[...] += jnp.sum(gain_part, axis=0, keepdims=True)
            return carry

        lax.fori_loop(0, grad.half // TILE, norm, 0)
    model = dgain.shape[1]
    count = model // SMALL
    for row in range(count):
        lanes = slice(row * SMALL, (row + 1) * SMALL)
        small[0, row : row + 1, :] = dgain[:, lanes]
        small[0, count + row : count + row + 1, :] = ffn_dgain[:, lanes]
    small[0, 2 * count : 2 * count + 1, 0:HEAD] = head_dgain[...]
    small[0, 16 : 16 + 3 * TAPS, :] = dtaps[...]

    def hop(at):
        where = (dict(tensor=grad.across), dict(tensor=grad.along), dict(dp=sibling))[at]
        return remote(small.at[at], near.at[at], small_send.at[at], small_receive.at[at], **where)

    def hopped(at):
        hop(at).wait()
        if at < 2:
            small[at + 1, 0:16, :] = small[at, 0:16, :] + near[at, 0:16, :]
            small[at + 1, 16:32, :] = small[at, 16:32, :]
        else:
            small[3] = small[2] + near[2]

    def tell(other):
        to = lax.rem(chip + other, chips)
        return remote(
            small.at[3], lined.at[chip], small_send.at[2 + other], small_receive.at[2 + other], dp=to * 2 + core
        )

    def put_inner(here, total):
        width = query_out.shape[1]
        for kind, target in enumerate((query_out, key_out, value_out, gate_out)):
            target[here, :] = total[:, kind * width : (kind + 1) * width]
        beta_out[here, :] = total[:, 4 * width : 4 * width + beta_out.shape[1]]

    def put_output(here, total):
        turned[here, :] = total

    puts = [put_inner, put_output]
    hop(0).start()
    ffn.relay(0)
    ffn.relay(1)
    hopped(0)
    hop(1).start()
    pieces = len(line.pieces)
    line.keep(puts, range(0, pieces - 3))
    hopped(1)
    hop(2).start()
    for half in (0, 1):
        ffn.ready(half)

        def finish_rows(index, carry):
            at = pl.multiple_of(index * TILE, TILE)
            here = pl.ds(pl.multiple_of(half * ffn.half + at, TILE), TILE)
            out[here, :] = ((resid[here, :] + ffn.tile(half, at)) * mask[here, :]).astype(bf16)
            return carry

        lax.fori_loop(0, ffn.half // TILE, finish_rows, 0)
    hopped(2)
    lined[chip] = small[3]
    for other in range(1, chips):
        tell(other).start()
    line.keep(puts, range(pieces - 3, pieces))
    output_out[...] = jnp.transpose(turned[...])
    for other in range(1, chips):
        tell(other).wait()
    total = lined[0]
    for other in range(1, chips):
        total = total + lined[other]
    for row in range(count):
        lanes = slice(row * SMALL, (row + 1) * SMALL)
        first_out[:, lanes] = total[row : row + 1, :]
        ffn_out[:, lanes] = total[count + row : count + row + 1, :]
    head_out[...] = total[2 * count : 2 * count + 1, 0:HEAD]
    for kind in range(3):
        taps_out[kind] = total[16 + kind * TAPS : 16 + (kind + 1) * TAPS, :]
    grad.finish()
    ffn.finish()
    line.finish()


def last_scatter(
    inner_part, output_part, weight, inner, dpre, middle, inputs, grad_resid, resid, mask, gain, ffn_dgain, head_dgain, dtaps
):
    chips = lax.axis_size("dp") // 2
    rows, model = inputs.shape
    slab, width = output_part.shape[1:]
    arrays = [inner_part, output_part]
    shape = jax.ShapeDtypeStruct
    return pl.pallas_call(
        functools.partial(last_kernel, chips),
        in_specs=anywhere(9) + in_vmem(5),
        out_specs=in_vmem(12),
        out_shape=[shape((slab, width), f32)] * 4
        + [
            shape((slab, width // HEAD), f32),
            shape((width, slab), f32),
            shape((rows, model), f32),
            shape((rows, model), bf16),
            shape((1, model), f32),
            shape((1, model), f32),
            shape((1, HEAD), f32),
            shape((3, TAPS, dtaps.shape[1]), f32),
        ],
        scratch_shapes=LineScatter.scratch(chips, arrays)
        + [pltpu.VMEM((4 * rows, model), bf16)]
        + plane_scatter_scratch(rows, model)
        + [pltpu.VMEM((4 * rows, model), bf16)]
        + plane_scatter_scratch(rows, model)
        + [
            pltpu.VMEM((slab, width), f32),
            pltpu.VMEM((4, 32, SMALL), f32),
            pltpu.VMEM((3, 32, SMALL), f32),
            pltpu.VMEM((chips, 32, SMALL), f32),
            pltpu.VMEM((1, model), f32),
            pltpu.SemaphoreType.DMA((2 + chips,)),
            pltpu.SemaphoreType.DMA((2 + chips,)),
            pltpu.VMEM((2, *inner.shape[1:]), bf16),
            pltpu.VMEM((2, *weight.shape[1:]), bf16),
            pltpu.SemaphoreType.DMA((2, 2)),
            pltpu.VMEM(dpre.shape, bf16),
            pltpu.VMEM(middle.shape, bf16),
            pltpu.VMEM((rows, model), bf16),
            pltpu.VMEM((rows, model), f32),
            pltpu.VMEM((rows, model), f32),
            pltpu.SemaphoreType.DMA((5,)),
        ],
        compiler_params=pltpu.CompilerParams(
            collective_id=4, has_side_effects=True, vmem_limit_bytes=LARGE_LIMIT
        ),
        cost_estimate=pl.CostEstimate(flops=80_000_000_000, bytes_accessed=20_000_000, transcendentals=0),
    )(inner_part, output_part, weight, inner, dpre, middle, inputs, grad_resid, resid, mask, gain, ffn_dgain, head_dgain, dtaps)


def rms_norm(values, gain):
    return (
        values * lax.rsqrt(jnp.mean(values * values, axis=-1, keepdims=True) + norm_epsilon) * gain
    )


def gather(values, axis):
    return lax.all_gather(values, axis, axis=0, tiled=True)


def scatter(values, axis):
    return lax.psum_scatter(values, axis, scatter_dimension=0, tiled=True)


def plain_first_gather(
    w_query, w_key, w_value, w_gate_out, w_beta, w_output, inputs, cotangent, mask, gain, w_gate, w_up, w_down
):
    shards = lax.axis_size("dp")
    padded = jnp.pad(w_beta, ((0, 0), (0, BETA_PAD - w_beta.shape[1])))
    inner = jnp.concatenate([w_query, w_key, w_value, w_gate_out, padded], axis=1).astype(bf16)
    output = w_output.T.astype(bf16)
    grad = (cotangent.astype(f32) * mask).astype(bf16)
    return (
        gather(inner, "dp").reshape(shards, *inner.shape),
        gather(output, "dp").reshape(shards, *output.shape),
        gather(rms_norm(inputs.astype(f32), gain[0]).astype(bf16), "tensor"),
        gather(grad, "tensor"),
        jnp.concatenate([w_gate, w_up], axis=1).astype(bf16),
        w_down.T.astype(bf16),
        grad,
    )


def plain_branch_and_norm(z, weight, inputs, gain):
    branch = mm_nt(z, weight.reshape(-1, z.shape[1])).astype(bf16)
    resid = inputs.astype(f32) + scatter(branch, "tensor").astype(f32)
    return resid, gather(rms_norm(resid, gain[0]).astype(bf16), "tensor")


def plain_resid_backward(grad_both, weight, resid, grad_out, gain):
    part = mm_nt(grad_both, weight).astype(bf16)
    back, gain_part = norm_backward(resid, scatter(part, "tensor").astype(f32), gain)
    value = grad_out.astype(f32) + back
    return value, gather(value.astype(bf16), "tensor"), jnp.sum(gain_part, axis=0, keepdims=True)


def plain_last_scatter(
    inner_part, output_part, weight, inner, dpre, middle, inputs, grad_resid, resid, mask, gain, ffn_dgain, head_dgain, dtaps
):
    grad_part = mm_nt(dpre, inner.reshape(-1, inner.shape[2])).astype(bf16)
    inner, output = (
        scatter(part.reshape(-1, part.shape[-1]), "dp").astype(f32) for part in (inner_part, output_part)
    )
    width = output.shape[1]
    back, gain_part = norm_backward(inputs.astype(f32), scatter(grad_part, "tensor").astype(f32), gain)
    ffn_part = mm_nt(middle, weight.reshape(-1, weight.shape[2])).astype(bf16)
    out = ((resid + scatter(ffn_part, "tensor").astype(f32)) * mask).astype(bf16)
    gains = (jnp.sum(gain_part, axis=0, keepdims=True), ffn_dgain, head_dgain)
    return (
        *(inner[:, kind * width : (kind + 1) * width] for kind in range(4)),
        inner[:, 4 * width : 4 * width + width // HEAD],
        output.T,
        grad_resid + back,
        out,
        *lax.psum(gains, ("dp", "tensor")),
        lax.psum(dtaps, "dp").reshape(3, TAPS, -1),
    )


def body(
    inputs,
    cotangent,
    lengths,
    norm_gain,
    w_query,
    w_key,
    w_value,
    w_gate_out,
    w_beta,
    conv_weight,
    out_norm_gain,
    w_output,
    ffn_norm_gain,
    w_gate,
    w_up,
    w_down,
):
    tensor_count = lax.axis_size("tensor")
    shards = lax.axis_size("dp")
    kernels = tensor_count == 4 and shards == 8
    rows, model = inputs.shape
    length = rows * tensor_count
    width = w_query.shape[1]
    heads = width // HEAD
    hidden = w_gate.shape[1]
    slab = w_query.shape[0]
    taps = conv_weight.reshape(3 * TAPS, width)
    first_gain, head_gain = norm_gain.reshape(1, model), out_norm_gain.reshape(1, HEAD)
    ffn_gain = ffn_norm_gain.reshape(1, model)

    positions = lax.axis_index("tensor") * rows + jnp.arange(rows, dtype=jnp.int32)
    mask = (positions < lengths[0]).astype(f32)[:, None]
    inner, full_output, normed, grad_full, gate_up, down, grad_out = (
        first_gather if kernels else plain_first_gather
    )(w_query, w_key, w_value, w_gate_out, w_beta, w_output, inputs, cotangent, mask, first_gain, w_gate, w_up, w_down)
    gate_up = gather(gate_up, "dp")
    down = gather(down, "dp")

    pre = jnp.dot(normed, inner.reshape(model, -1), preferred_element_type=f32).astype(bf16)
    z, conv, mixed, inverse, states = mixer_forward(pre, taps, head_gain, heads)
    resid, normed2 = (branch_and_norm if kernels else plain_branch_and_norm)(z, full_output, inputs, ffn_gain)
    middle, slopes = (ffn if kernels else plain_ffn)(normed2, gate_up)
    down_part = mm_tn(grad_full, middle).astype(bf16)
    down, down_part = lax.optimization_barrier((down, down_part))
    down_total = scatter(down_part, "dp")
    grad_both = (ffn_backward if kernels else plain_ffn_backward)(grad_full, down, slopes)
    grad_both, both_part = lax.optimization_barrier((grad_both, mm_tn(normed2, grad_both).astype(bf16)))
    both_total = scatter(both_part, "dp")
    grad_resid, grad_resid_full, ffn_dgain = (resid_backward if kernels else plain_resid_backward)(
        grad_both, gate_up, resid, grad_out, ffn_gain
    )
    dz = jnp.dot(grad_resid_full, full_output.reshape(model, width), preferred_element_type=f32).astype(bf16)
    dpre, dtaps, head_dgain = mixer_backward(pre, conv, mixed, dz, inverse, states, taps, head_gain, heads)
    output_grad = mm_tn(grad_resid_full, z).astype(bf16).reshape(shards, slab, width)
    inner_grad = mm_tn(normed, dpre).astype(bf16).reshape(shards, slab, -1)
    results = (last_scatter if kernels else plain_last_scatter)(
        inner_grad,
        output_grad,
        down.reshape(shards, slab, hidden),
        inner,
        dpre,
        middle,
        inputs,
        grad_resid,
        resid,
        mask,
        first_gain,
        ffn_dgain,
        head_dgain,
        dtaps,
    )
    gate_total, up_total, down_total, *results = (finish if kernels else plain_finish)(
        both_total, down_total, results
    )
    query_total, key_total, value_total, gate_out_total, beta_total, output_total, input_grad, output = results[:8]
    first_total, ffn_total, head_total, taps_total = results[8:]
    return (
        output,
        input_grad,
        first_total[0],
        query_total,
        key_total,
        value_total,
        gate_out_total,
        beta_total,
        taps_total,
        head_total[0],
        output_total,
        ffn_total[0],
        gate_total,
        up_total,
        down_total,
    )


def solution(mesh):
    rows = P(("dp", "tensor"), None)
    split = P("dp", "tensor")
    turned = P("tensor", "dp")
    taps = P(None, None, "tensor")
    return jax.shard_map(
        body,
        mesh=mesh,
        in_specs=(rows, rows, P("dp"), P(), split, split, split, split, split, taps, P(), turned, P(), split, split, turned),
        out_specs=(rows, rows, P(), split, split, split, split, split, taps, P(), turned, P(), split, split, turned),
        check_vma=False,
    )
```

time: 1850 us -> 595 us (0.32)
  waiting for transfers between devices: 716 us -> 23.2 us
  Pallas kernels: 0 us -> 477 us
  other arithmetic: 443 us -> 0.67 us
  matrix products: 442 us -> 67.4 us
  local copies, waits for them, and re-layouts: 134 us -> 3.72 us
  blocking collectives: 84.2 us -> 0 us
    pallas_call x0 -> x9, Pallas kernels: none -> 477 us  [the longest x1 115 us: last_scatter(): pl.pallas_call(functools.partial(last_kernel, chips), in_specs=anywhere(9...]
    all_gather x12 -> x2, waiting for transfers between devices: 417 us -> 22.4 us  [gather(): return lax.all_gather(values, axis, axis=0, tiled=True)]
    dot_general x127 -> x6, matrix products: 430 us -> 67.4 us  [the longest x4 48.5 us: mm_tn(): lax.dot_general(a, b, (((0,), (0,)), ((), ())), preferred_element_type=f32)]
    another operation x7 -> x0, other arithmetic: 326 us -> none  [the longest x5 320 us: delta_rule(): lax.linalg.triangular_solve(system, stacked, left_side=True, lower=True,...]
    reduce_scatter x12 -> x2, waiting for transfers between devices: 296 us -> 0.04 us  [scatter(): return lax.psum_scatter(values, axis, scatter_dimension=0, tiled=True)]
    psum x2 -> x0, blocking collectives: 69.6 us -> none  [the longest x1 40.1 us: body(): lax.psum((first_gain_grad, ffn_gain_grad, head_gain_grad), ('dp', 'tensor'))]
    reshape x15 -> x1, local copies, waits for them, and re-layouts: 54.7 us -> 0.63 us  [body(): taps = conv_weight.reshape(3 * TAPS, width)]
    reduce_sum x11 -> x0, other arithmetic: 36 us -> none  [the longest x1 10.1 us: short_conv(): total = total + taps[offset] * padded[offset:offset + length]]
  transfers between devices with their start and end apart: 25 -> 4, of which waited for: 19 -> 1; matrix products, arithmetic and copies ran while one was open for 52% -> 12% of each run, Pallas kernels for 0% -> 63%
where the time goes in v1:
time: 595 us; the launch traced here: 587 us
  Pallas kernels  477 us (80%)
  matrix products  67.4 us (11%)
  waiting for transfers between devices  23.2 us (4%)
  between operations  14.8 us (2%)
    pallas_call x1, Pallas kernels, last_scatter(): pl.pallas_call(functools.partial(last_kernel, chips), in_specs=anywhere(9...  115 us
    pallas_call x1, Pallas kernels, first_gather(): pl.pallas_call(functools.partial(first_gather_kernel, shards // 2), in_sp...  101 us
    pallas_call x1, Pallas kernels, resid_backward(): pl.pallas_call(functools.partial(resid_kernel, 256), in_specs=anywhere(2)...  84.8 us
    pallas_call x1, Pallas kernels, branch_and_norm(): pl.pallas_call(branch_kernel, in_specs=in_vmem(4), out_specs=in_vmem(1) +...  80.4 us
    dot_general x4, matrix products, mm_tn(): lax.dot_general(a, b, (((0,), (0,)), ((), ())), preferred_element_type=f32)  48.5 us
    pallas_call x1, Pallas kernels, mixer_backward(): pl.pallas_call(functools.partial(backward_kernel, heads), grid=(steps,),...  36 us
    all_gather x2, waiting for transfers between devices, gather(): return lax.all_gather(values, axis, axis=0, tiled=True)  22.4 us
    pallas_call x1, Pallas kernels, ffn(): pl.pallas_call(ffn_kernel, grid=(hidden // LANES,), in_specs=[pl.BlockSpe...  19.8 us
  transfers between devices with their start and end apart: 4, of which 1 were waited for; matrix products, arithmetic and copies ran while one was open for 12% of the time, Pallas kernels for 63%

profile of v1, /device:TPU:0, one launch (start us, length us, event | category | flops | bytes accessed | tf_op | source)
XLA Modules:
  0.0 587.3 jit_solution(5067636857818929044)
XLA Ops:
  7.2 0.0 all-gather.5.cloned.1.call-start
  7.9 1.5 copy.31.refs_4_
  9.4 0.7 fusion.refs_8_.refs_9_
  10.0 0.0 copy-start
  10.0 100.6 %shard_map.271 = (bf16[8,256,2176]{2,1,0:T(8,128)(2,1)}, bf16[8,256,512]{2,1,0:T(8,128)(2,1)}, bf16[1024,2048]{1,0:T(8,128)(2,1)}, bf16[1024,2048]{1,0:T(8,128)(...) custom-call(f32[256,512]{1,0:T(8,128)} %refs_0_.1, f32[256,512]{1,0:T(8,128)} %refs_1_.1, ...), custom_call_target="tpu_custom_call" | custom-call | flops 80000000000 | bytes 20000000 | tf_op jit(solution)/shard_map/pallas_call | solution.py:869
  110.6 0.0 all-gather.5.cloned.1.call-update
  110.6 0.0 all-gather.3.cloned.1.call-start
  110.7 0.7 all-gather.3.cloned.1.call-update
  111.4 0.0 reduce-scatter.5.cloned.1.call-start
  111.4 0.0 copy-done
  111.5 0.6 reshape.72.taps_ref
  112.1 15.6 %convolution_convert_fusion.3.pre_ref = bf16[1024,2176]{1,0:T(8,128)(2,1)} fusion(bf16[1024,2048]{1,0:T(8,128)(2,1)} %get-tuple-element.70, bf16[2048,2176]{1,0:T(8,128)(2,1)} %bitcast.35), kind=kOutput, calls=%fused_computation.3 | convolution fusion | flops 9129033728 | bytes 17563648 | tf_op jit(solution)/shard_map/dot_general | solution.py:1564
  127.7 18.4 %shard_map.272 = (bf16[1024,512]{1,0:T(8,128)(2,1)}, f32[1024,1536]{1,0:T(8,128)}, f32[1024,512]{1,0:T(8,128)}, bf16[4,8,128,128]{3,2,1,0:T(8,128)(2,1)}, bf16[4,8,128,128]{3,2,1,0:T(8,128)(2,1)}) custom-call(bf16[1024,2176]{1,0:T(8,128)(2,1)} %convolution_convert_fusion.3.pre_ref, f32[12,512]{1,0:T(8,128)} %reshape.72.taps_ref, f32[1,128]{1,0:T(1,128)} %bitcast.32), custom_call_target="tpu_custom_call" | custom-call | flops 8053063680 | bytes 21495808 | tf_op jit(solution)/shard_map/pallas_call | solution.py:136
  146.1 80.4 %shard_map.273 = (f32[256,2048]{1,0:T(8,128)}, bf16[1024,2048]{1,0:T(8,128)(2,1)}) custom-call(bf16[1024,512]{1,0:T(8,128)(2,1)} %get-tuple-element.72.z, bf16[8,256,512]{2,1,0:T(8,128)(2,1)} %get-tuple-element.73.weight, bf16[256,2048]{1,0:T(8,128)(2,1)} %refs_6_.3, f32[1,2048]{1,0:T(1,128)} %bitcast.26), custom_call_target="tpu_custom_call" | custom-call | flops 49999998976 | bytes 20000000 | tf_op jit(solution)/shard_map/pallas_call | solution.py:952
  226.6 0.0 all-gather.5.cloned.1.call-done.weight.weight_far
  226.6 0.0 copy-start.2
  226.6 19.8 %shard_map.274 = (bf16[1024,1408]{1,0:T(8,128)(2,1)}, bf16[1024,2816]{1,0:T(8,128)(2,1)}) custom-call(bf16[1024,2048]{1,0:T(8,128)(2,1)} %get-tuple-element.74.normed, bf16[2048,2816]{1,0:T(8,128)(2,1)} %all-gather.5.cloned.1.call-done.weight.weight_far), custom_call_target="tpu_custom_call" | custom-call | flops 11811160064 | bytes 15728640 | tf_op jit(solution)/shard_map/pallas_call | solution.py:735
  246.5 0.0 copy-done.2
  246.5 10.6 %convolution_convert_fusion.2 = bf16[2048,1408]{1,0:T(8,128)(2,1)} fusion(bf16[1024,2048]{1,0:T(8,128)(2,1)S(1)} %copy-done.2, bf16[1024,1408]{1,0:T(8,128)(2,1)} %get-tuple-element.76.refs_5_), kind=kOutput, calls=%fused_computation.2 | convolution fusion | flops 5908463616 | bytes 12845056 | tf_op jit(solution)/shard_map/dot_general | solution.py:30
  257.1 22.4 %all-gather.3.cloned.1.call-done.weight = bf16[2048,1408]{1,0:T(8,128)(2,1)} async-done(((bf16[256,1408]{1,0:T(8,128)(2,1)}), bf16[2048,1408]{1,0:T(8,128)(2,1)}) %all-gather.3.cloned.1.call-update) | async-done | bytes 5767184 | tf_op jit(solution)/shard_map/all_gather | solution.py:1463
  279.4 0.0 reduce-scatter.5.cloned.1.call-update
  279.5 0.0 reduce-scatter.3.cloned.1.call-start
  279.5 0.0 copy-start.5
  279.5 12.9 %shard_map.275.grad_far = bf16[1024,2816]{1,0:T(8,128)(2,1)} custom-call(bf16[1024,2048]{1,0:T(8,128)(2,1)} %get-tuple-element.68.grad, bf16[2048,1408]{1,0:T(8,128)(2,1)} %all-gather.3.cloned.1.call-done.weight, bf16[1024,2816]{1,0:T(8,128)(2,1)} %get-tuple-element.78.slopes), custom_call_target="tpu_custom_call" | custom-call | flops 5905580032 | bytes 21495808 | tf_op jit(solution)/shard_map/pallas_call | solution.py:772
  292.5 0.0 copy-done.5
  292.5 17.3 %convolution_convert_fusion.1 = bf16[2048,2816]{1,0:T(8,128)(2,1)} fusion(bf16[1024,2048]{1,0:T(8,128)(2,1)S(1)} %copy-done.5, bf16[1024,2816]{1,0:T(8,128)(2,1)} %shard_map.275.grad_far), kind=kOutput, calls=%fused_computation.1 | convolution fusion | flops 11816927232 | bytes 21495808 | tf_op jit(solution)/shard_map/dot_general | solution.py:30
  309.7 0.0 reduce-scatter.3.cloned.1.call-update
  309.8 0.0 copy-start.4
  309.8 84.8 %shard_map.276 = (f32[256,2048]{1,0:T(8,128)}, bf16[1024,2048]{1,0:T(8,128)(2,1)}, f32[1,2048]{1,0:T(1,128)}) custom-call(bf16[1024,2816]{1,0:T(8,128)(2,1)} %shard_map.275.grad_far, bf16[2048,2816]{1,0:T(8,128)(2,1)} %all-gather.5.cloned.1.call-done.weight.weight_far, f32[256,2048]{1,0:T(8,128)} %get-tuple-element.84.resid.refs_8_, ...), custom_call_target="tpu_custom_call" | custom-call | flops 60000002048 | bytes 30000000 | tf_op jit(solution)/shard_map/pallas_call | solution.py:1206
  394.6 0.0 copy-done.4
  394.6 0.0 copy-start.1
  394.6 0.0 copy-start.3
  394.6 6.2 %convolution_convert_fusion.4 = bf16[2048,512]{1,0:T(8,128)(2,1)} fusion(bf16[1024,2048]{1,0:T(8,128)(2,1)} %get-tuple-element.86, bf16[1024,512]{1,0:T(8,128)(2,1)S(1)} %copy-done.4), kind=kOutput, calls=%fused_computation.4 | convolution fusion | flops 2148532224 | bytes 7340032 | tf_op jit(solution)/shard_map/dot_general | solution.py:30
  400.8 0.0 copy-done.1
  400.8 0.0 copy-done.3
  400.8 3.3 convolution_convert_fusion.5.dz_ref
  404.1 0.0 copy-start.6
  404.1 36.0 %shard_map.277 = (bf16[1024,2176]{1,0:T(8,128)(2,1)}, f32[12,512]{1,0:T(8,128)}, f32[1,128]{1,0:T(1,128)}) custom-call(bf16[1024,2176]{1,0:T(8,128)(2,1)} %convolution_convert_fusion.3.pre_ref, f32[1024,1536]{1,0:T(8,128)} %get-tuple-element.81.conv_ref, f32[1024,512]{1,0:T(8,128)} %get-tuple-element.82.mixed_ref, ...), custom_call_target="tpu_custom_call" | custom-call | flops 16106127360 | bytes 25952256 | tf_op jit(solution)/shard_map/pallas_call | solution.py:313
  440.1 0.0 copy-done.6
  440.1 14.4 %convolution_convert_fusion = bf16[2048,2176]{1,0:T(8,128)(2,1)} fusion(bf16[1024,2048]{1,0:T(8,128)(2,1)S(1)} %copy-done.6, bf16[1024,2176]{1,0:T(8,128)(2,1)} %get-tuple-element.89.refs_4_), kind=kOutput, calls=%fused_computation | convolution fusion | flops 9131261952 | bytes 17563648 | tf_op jit(solution)/shard_map/dot_general | solution.py:30
  454.5 115.5 %shard_map.278 = (f32[256,512]{1,0:T(8,128)}, f32[256,512]{1,0:T(8,128)}, f32[256,512]{1,0:T(8,128)}, f32[256,512]{1,0:T(8,128)}, f32[256,4]{1,0:T(8,128)}, /*in...) custom-call(bf16[8,256,2176]{2,1,0:T(8,128)(2,1)} %bitcast.36, ...), custom_call_target="tpu_custom_call" | custom-call | flops 80000000000 | bytes 20000000 | tf_op jit(solution)/shard_map/pallas_call | solution.py:1411
  570.0 0.0 reduce-scatter.5.cloned.1.call-done.refs_1_
  570.0 0.0 reduce-scatter.3.cloned.1.call-done.refs_0_
  570.1 8.9 %shard_map.279 = (f32[256,1408]{1,0:T(8,128)}, f32[256,1408]{1,0:T(8,128)}, f32[1408,256]{1,0:T(8,128)}, f32[256,512]{1,0:T(8,128)}, f32[256,512]{1,0:T(8,128)},...) custom-call(bf16[256,2816]{1,0:T(8,128)(2,1)} %reduce-scatter.3.clon, ...), custom_call_target="tpu_custom_call" | custom-call | bytes 14417920 | tf_op jit(solution)/shard_map/pallas_call | solution.py:819
  579.0 1.6 copy.32
Async XLA Ops:
  7.2 219.4 %all-gather.5.cloned.1.call-start = ((), (), s32[]{:S(2)}) async-start(), calls=%async_computation.3 | async-start | bytes 12976128 | tf_op jit(solution)/shard_map/all_gather | solution.py:1463
  10.0 101.4 %copy-start = (f32[3,4,512]{2,1,0:T(4,128)S(1)}, f32[3,4,512]{2,1,0:T(4,128)}, u32[]{:S(2)}) copy-start(f32[3,4,512]{2,1,0:T(4,128)} %param.25) | copy-start | bytes 73732
  110.6 168.8 %all-gather.3.cloned.1.call-start = ((), (), s32[]{:S(2)}) async-start(), calls=%async_computation.2 | async-start | bytes 6488064 | tf_op jit(solution)/shard_map/all_gather | solution.py:1463
  111.4 458.6 %reduce-scatter.5.cloned.1.call-start = ((), (), s32[]{:S(2)}) async-start(), calls=%async_computation.5 | async-start | bytes 6488064 | tf_op jit(solution)/shard_map/reduce_scatter | solution.py:1467
  226.6 19.8 %copy-start.2 = (bf16[1024,2048]{1,0:T(8,128)(2,1)S(1)}, bf16[1024,2048]{1,0:T(8,128)(2,1)}, u32[]{:S(2)}) copy-start(bf16[1024,2048]{1,0:T(8,128)(2,1)} %get-tuple-element.68.grad) | copy-start | bytes 12582916
  279.5 290.6 %reduce-scatter.3.cloned.1.call-start = ((), (), s32[]{:S(2)}) async-start(), calls=%async_computation.4 | async-start | bytes 12976128 | tf_op jit(solution)/shard_map/reduce_scatter | solution.py:1467
  279.5 13.0 %copy-start.5 = (bf16[1024,2048]{1,0:T(8,128)(2,1)S(1)}, bf16[1024,2048]{1,0:T(8,128)(2,1)}, u32[]{:S(2)}) copy-start(bf16[1024,2048]{1,0:T(8,128)(2,1)} %get-tuple-element.74.normed) | copy-start | bytes 12582916
  309.8 84.8 %copy-start.4 = (bf16[1024,512]{1,0:T(8,128)(2,1)S(1)}, bf16[1024,512]{1,0:T(8,128)(2,1)}, u32[]{:S(2)}) copy-start(bf16[1024,512]{1,0:T(8,128)(2,1)} %get-tuple-element.72.z) | copy-start | bytes 3145732
  394.6 6.2 %copy-start.1 = (bf16[8,256,512]{2,1,0:T(8,128)(2,1)S(1)}, bf16[8,256,512]{2,1,0:T(8,128)(2,1)}, u32[]{:S(2)}) copy-start(bf16[8,256,512]{2,1,0:T(8,128)(2,1)} %get-tuple-element.73.weight) | copy-start | bytes 6291460
  394.6 6.2 %copy-start.3 = (bf16[1024,2048]{1,0:T(8,128)(2,1)S(1)}, bf16[1024,2048]{1,0:T(8,128)(2,1)}, u32[]{:S(2)}) copy-start(bf16[1024,2048]{1,0:T(8,128)(2,1)} %get-tuple-element.86) | copy-start | bytes 12582916
  404.1 36.0 %copy-start.6 = (bf16[1024,2048]{1,0:T(8,128)(2,1)S(1)}, bf16[1024,2048]{1,0:T(8,128)(2,1)}, u32[]{:S(2)}) copy-start(bf16[1024,2048]{1,0:T(8,128)(2,1)} %get-tuple-element.70) | copy-start | bytes 12582916
Sparse Core Ops, SparseCore 0:
  110.8 108.2 all-gather.4
  220.7 58.7 all-gather.2
  281.7 63.5 reduce-scatter.4
  347.5 118.0 reduce-scatter.2

commit v2 on v1

--- a/solution.py
+++ b/solution.py
@@ -12,7 +12,7 @@
 CHUNK = 128
 STEP = 256
 TAPS = 4
-BETA_PAD = 128
+BETA_PAD = 16
 VMEM_LIMIT = 56 * 1024 * 1024
 f32 = jnp.float32
 bf16 = jnp.bfloat16
@@ -55,7 +55,7 @@
 
 
 def forward_kernel(
-    heads, pre_ref, taps_ref, gain_ref, z_ref, conv_ref, mixed_ref, inv_ref, state_ref, hist, state
+    heads, pre_ref, beta_ref, taps_ref, gain_ref, z_ref, conv_ref, mixed_ref, inv_ref, state_ref, hist, state
 ):
     step = pl.program_id(0)
     width = heads * HEAD
@@ -72,7 +72,7 @@
 
     hist[8 : 8 + rows, :] = pre_ref[:, 0 : 3 * width].astype(f32)
     row, col = chunk_indices()
-    beta_all = jax.nn.sigmoid(pre_ref[:, 4 * width : 4 * width + BETA_PAD].astype(f32))
+    beta_all = jax.nn.sigmoid(beta_ref[...])
     work = []
     for head in range(heads):
         parts = []
@@ -129,7 +129,7 @@
         state[head] = states[head]
 
 
-def mixer_forward(pre, taps, gain, heads):
+def mixer_forward(pre, beta, taps, gain, heads):
     length, total = pre.shape
     width = heads * HEAD
     steps, parts = length // STEP, STEP // CHUNK
@@ -138,6 +138,7 @@
         grid=(steps,),
         in_specs=[
             pl.BlockSpec((STEP, total), lambda i: (i, 0)),
+            pl.BlockSpec((STEP, BETA_PAD), lambda i: (i, 0)),
             pl.BlockSpec((3 * TAPS, width), lambda i: (0, 0)),
             pl.BlockSpec((1, HEAD), lambda i: (0, 0)),
         ],
@@ -165,12 +166,14 @@
         cost_estimate=pl.CostEstimate(
             flops=2 * length * width * HEAD * 60, bytes_accessed=length * (total * 4 + width * 24), transcendentals=length * width * 8
         ),
-    )(pre, taps, gain)
+    )(pre, beta, taps, gain)
 
 
 def backward_kernel(
     heads,
     pre_ref,
+    beta_ref,
+    source_ref,
     conv_ref,
     mixed_ref,
     dz_ref,
@@ -179,6 +182,8 @@
     taps_ref,
     gain_ref,
     dpre_ref,
+    dbeta_ref,
+    dsource_ref,
     dtaps_ref,
     dgain_ref,
     later,
@@ -195,13 +200,14 @@
         dstate[...] = jnp.zeros_like(dstate)
         dtaps_ref[...] = jnp.zeros_like(dtaps_ref)
         dgain_ref[...] = jnp.zeros_like(dgain_ref)
+        dsource_ref[...] = jnp.zeros_like(dsource_ref)
 
     @pl.when(step > 0)
     def _():
         later[rows : rows + 8, :] = later[0:8, :]
 
     row, col = chunk_indices()
-    beta_all = jax.nn.sigmoid(pre_ref[:, 4 * width : 4 * width + BETA_PAD].astype(f32))
+    beta_all = jax.nn.sigmoid(beta_ref[...])
     beta_lane = lax.broadcasted_iota(jnp.int32, (CHUNK, BETA_PAD), 1)
     dbeta_all = [jnp.zeros((CHUNK, BETA_PAD), f32) for _ in range(count)]
     dgain = jnp.zeros((1, HEAD), f32)
@@ -289,7 +295,10 @@
             lanes = slice(kind * width + head * HEAD, kind * width + (head + 1) * HEAD)
             later[part * CHUNK : (part + 1) * CHUNK, lanes] = dconv
     for part in range(count):
-        dpre_ref[part * CHUNK : (part + 1) * CHUNK, 4 * width : 4 * width + BETA_PAD] = dbeta_all[part].astype(bf16)
+        here = slice(part * CHUNK, (part + 1) * CHUNK)
+        dbeta_low = dbeta_all[part].astype(bf16)
+        dbeta_ref[here, :] = dbeta_low
+        dsource_ref[...] += mm_tn(dbeta_low, source_ref[here, :])
     dgain_ref[...] += dgain
     for kind in range(3):
         for head in range(heads):
@@ -306,8 +315,9 @@
             dpre_ref[:, lanes] = total.astype(bf16)
 
 
-def mixer_backward(pre, conv, mixed, dz, inverse, states, taps, gain, heads):
+def mixer_backward(pre, beta, source, conv, mixed, dz, inverse, states, taps, gain, heads):
     length, total = pre.shape
+    model = source.shape[1]
     width = heads * HEAD
     steps, parts = length // STEP, STEP // CHUNK
     return pl.pallas_call(
@@ -315,6 +325,8 @@
         grid=(steps,),
         in_specs=[
             pl.BlockSpec((STEP, total), lambda i: (steps - 1 - i, 0)),
+            pl.BlockSpec((STEP, BETA_PAD), lambda i: (steps - 1 - i, 0)),
+            pl.BlockSpec((STEP, model), lambda i: (steps - 1 - i, 0)),
             pl.BlockSpec((STEP, 3 * width), lambda i: (steps - 1 - i, 0)),
             pl.BlockSpec((STEP, width), lambda i: (steps - 1 - i, 0)),
             pl.BlockSpec((STEP, width), lambda i: (steps - 1 - i, 0)),
@@ -325,11 +337,15 @@
         ],
         out_specs=[
             pl.BlockSpec((STEP, total), lambda i: (steps - 1 - i, 0)),
+            pl.BlockSpec((STEP, BETA_PAD), lambda i: (steps - 1 - i, 0)),
+            pl.BlockSpec((BETA_PAD, model), lambda i: (0, 0)),
             pl.BlockSpec((3 * TAPS, width), lambda i: (0, 0)),
             pl.BlockSpec((1, HEAD), lambda i: (0, 0)),
         ],
         out_shape=[
             jax.ShapeDtypeStruct((length, total), bf16),
+            jax.ShapeDtypeStruct((length, BETA_PAD), bf16),
+            jax.ShapeDtypeStruct((BETA_PAD, model), f32),
             jax.ShapeDtypeStruct((3 * TAPS, width), f32),
             jax.ShapeDtypeStruct((1, HEAD), f32),
         ],
@@ -341,9 +357,9 @@
             dimension_semantics=("arbitrary",), vmem_limit_bytes=VMEM_LIMIT
         ),
         cost_estimate=pl.CostEstimate(
-            flops=2 * length * width * HEAD * 120, bytes_accessed=length * (total * 6 + width * 24), transcendentals=length * width * 8
+            flops=1_000_000, bytes_accessed=1_000_000, transcendentals=0
         ),
-    )(pre, conv, mixed, dz, inverse, states, taps, gain)
+    )(pre, beta, source, conv, mixed, dz, inverse, states, taps, gain)
 
 
 MESH = pl.DeviceIdType.MESH
@@ -443,11 +459,21 @@
         self.arriving(kind, kind).wait_recv()
         self.passing(kind).start()
 
+    def near(self, kind):
+        self.arriving(1 - kind, kind).wait_recv()
+
+    def diagonal(self):
+        self.passed(0).wait_recv()
+        self.passed(1).wait_recv()
+
     def finish(self):
+        self.near(0)
+        self.near(1)
+        self.diagonal()
+        self.sent()
+
+    def sent(self):
         for kind in (0, 1):
-            self.arriving(1 - kind, kind).wait_recv()
-        for kind in (0, 1):
-            self.passed(kind).wait_recv()
             self.passing(kind).wait_send()
             for half in (0, 1):
                 self.out(half, kind).wait_send()
@@ -650,11 +676,11 @@
 def first_gather_kernel(chips, *refs):
     w_query, w_key, w_value, w_gate_out, w_beta, w_output, inputs, cotangent, mask, gain = refs[:10]
     w_gate, w_up, w_down = refs[10:13]
-    inner_full, output_full, normed_full, grad_full, gate_up, down, grad = refs[13:20]
-    inner, output, normed, gate_wide, up_wide, down_wide = refs[20:26]
-    sems = refs[26:]
+    inner_full, output_full, beta_full, normed_full, grad_full, gate_up, down, grad = refs[13:21]
+    inner, output, normed, gate_wide, up_wide, down_wide = refs[21:27]
+    sems = refs[27:]
     width, hidden = w_query.shape[1], w_gate.shape[1]
-    line = LineGather(chips, [inner, output], [inner_full, output_full], sems[:7])
+    line = LineGather(chips, [inner, output, w_beta], [inner_full, output_full, beta_full], sems[:7])
     rows = [PlaneGather(normed, normed_full, *sems[7:9]), PlaneGather(grad, grad_full, *sems[9:11])]
     local = sems[11]
     keeps = [
@@ -672,8 +698,6 @@
     greet(tensor=rows[0].along)
     for kind, weight in enumerate((w_query, w_key, w_value, w_gate_out)):
         inner[:, kind * width : (kind + 1) * width] = weight[...].astype(bf16)
-    inner[:, 4 * width :] = jnp.zeros((inner.shape[0], BETA_PAD), bf16)
-    inner[:, 4 * width : 4 * width + w_beta.shape[1]] = w_beta[...].astype(bf16)
     output[...] = jnp.transpose(w_output[...]).astype(bf16)
     wait_greetings(2 + greetings)
     line.start()
@@ -863,16 +887,17 @@
     rows, model = inputs.shape
     slab, width = w_query.shape
     hidden = w_gate.shape[1]
-    inner = jax.ShapeDtypeStruct((slab, 4 * width + BETA_PAD), bf16)
+    inner = jax.ShapeDtypeStruct((slab, 4 * width), bf16)
     output = jax.ShapeDtypeStruct((slab, width), bf16)
-    pieces = len(pieces_of([inner, output], PIECE))
+    pieces = len(pieces_of([inner, output, w_beta], PIECE))
     return pl.pallas_call(
         functools.partial(first_gather_kernel, shards // 2),
         in_specs=in_vmem(10) + anywhere(3),
-        out_specs=anywhere(4) + in_vmem(3),
+        out_specs=anywhere(5) + in_vmem(3),
         out_shape=[
             jax.ShapeDtypeStruct((shards, *inner.shape), bf16),
             jax.ShapeDtypeStruct((shards, *output.shape), bf16),
+            jax.ShapeDtypeStruct((shards, *w_beta.shape), bf16),
             jax.ShapeDtypeStruct((4 * rows, model), bf16),
             jax.ShapeDtypeStruct((4 * rows, model), bf16),
             jax.ShapeDtypeStruct((slab, 2 * hidden), bf16),
@@ -887,7 +912,7 @@
             pltpu.VMEM((slab, hidden), f32),
             pltpu.VMEM((hidden, slab), f32),
         ]
-        + LineGather.scratch(shards // 2, pieces, 2)
+        + LineGather.scratch(shards // 2, pieces, 3)
         + [pltpu.SemaphoreType.DMA((6,)) for _ in range(4)]
         + [pltpu.SemaphoreType.DMA((5,))],
         compiler_params=pltpu.CompilerParams(
@@ -1127,17 +1152,17 @@
 
 
 def resid_kernel(
-    slab, grad_far, weight_far, resid, grad_out, gain, grad_resid, full, dgain,
-    part, first, second, stage, low, s_send, s_recv, g_send, g_recv, local, grad_both, weight, load_sems
+    slab, grad_far, weight_far, z_far, out_weight_far, resid, grad_out, gain, grad_resid, dgain, dz, output_grad,
+    part, first, second, stage, low, full, total, s_send, s_recv, g_send, g_recv,
+    grad_both, weight, z, out_weight, load_sems
 ):
     scatter = PlaneScatter(part, first, second, stage, s_send, s_recv)
     gather = PlaneGather(low, full, g_send, g_recv)
     rows = scatter.rows
+    slabs = weight.shape[0] // slab
+    order = (scatter.far, scatter.across, scatter.along, scatter.me)
     greet(tensor=scatter.across)
     greet(tensor=scatter.along)
-
-    slabs = weight.shape[0] // slab
-    order = (scatter.far, scatter.across, scatter.along, scatter.me)
 
     def rows_load(at):
         here = pl.ds(scatter.start_of(order[at], 0), rows)
@@ -1147,11 +1172,17 @@
         here = pl.ds(pl.multiple_of(index * slab, slab), slab)
         return pltpu.make_async_copy(weight_far.at[here], weight.at[here], load_sems.at[index])
 
-    rows_load(0).start()
-    for index in range(slabs):
-        slab_load(index).start()
-    for at in range(1, 4):
+    late_loads = [
+        pltpu.make_async_copy(z_far, z, load_sems.at[slabs + 4]),
+        pltpu.make_async_copy(out_weight_far, out_weight, load_sems.at[slabs + 5]),
+    ]
+    for at in range(4):
         rows_load(at).start()
+        if at == 0:
+            for index in range(slabs):
+                slab_load(index).start()
+    for load in late_loads:
+        load.start()
 
     def compute(at):
         here = pl.ds(scatter.start_of(order[at], 0), rows)
@@ -1192,41 +1223,72 @@
 
         lax.fori_loop(0, scatter.half // TILE, norm, 0)
         gather.start(half)
-    keep = pltpu.make_async_copy(low, full.at[pl.ds(pl.multiple_of(gather.me * rows, rows), rows)], local.at[0])
-    keep.start()
+    for load in late_loads:
+        load.wait()
+
+    def use(block, left, fresh=False):
+        here = pl.ds(pl.multiple_of(block * rows, rows), rows)
+        dz[here, :] = mm(left[...], out_weight[...]).astype(bf16)
+
+        def column(index, carry):
+            lanes = pl.ds(pl.multiple_of(index * slab, slab), slab)
+            product = mm_tn(left[:, lanes], z[here, :])
+            total[lanes, :] = product if fresh else total[lanes, :] + product
+            return carry
+
+        lax.fori_loop(0, slabs, column, 0)
+
+    def block_of(block):
+        return full.at[pl.ds(pl.multiple_of(block * rows, rows), rows)]
+
     gather.relay(0)
     gather.relay(1)
+    use(scatter.me, low, True)
+    gather.near(0)
+    use(scatter.across, block_of(scatter.across))
+    gather.near(1)
+    use(scatter.along, block_of(scatter.along))
+
+    gather.diagonal()
+    use(scatter.far, block_of(scatter.far))
+    output_grad[...] = total[...].astype(bf16)
+    gather.sent()
     scatter.finish()
-    gather.finish()
-    keep.wait()
-
-
-def resid_backward(grad_both, weight, resid, grad_out, gain):
+
+
+def resid_backward(grad_both, weight, z, out_weight, resid, grad_out, gain):
     rows, model = resid.shape
+    width = z.shape[1]
     return pl.pallas_call(
         functools.partial(resid_kernel, 256),
-        in_specs=anywhere(2) + in_vmem(3),
-        out_specs=in_vmem(1) + anywhere(1) + in_vmem(1),
+        in_specs=anywhere(4) + in_vmem(3),
+        out_specs=in_vmem(4),
         out_shape=[
             jax.ShapeDtypeStruct((rows, model), f32),
-            jax.ShapeDtypeStruct((4 * rows, model), bf16),
             jax.ShapeDtypeStruct((1, model), f32),
+            jax.ShapeDtypeStruct((4 * rows, width), bf16),
+            jax.ShapeDtypeStruct((model, width), bf16),
         ],
         scratch_shapes=[pltpu.VMEM((4 * rows, model), bf16)]
         + plane_scatter_scratch(rows, model)[:3]
-        + [pltpu.VMEM((rows, model), bf16)]
+        + [
+            pltpu.VMEM((rows, model), bf16),
+            pltpu.VMEM((4 * rows, model), bf16),
+            pltpu.VMEM((model, width), f32),
+        ]
         + [pltpu.SemaphoreType.DMA((6,)) for _ in range(4)]
         + [
-            pltpu.SemaphoreType.DMA((1,)),
-            pltpu.VMEM(grad_both.shape, bf16),
+            pltpu.VMEM((4 * rows, weight.shape[1]), bf16),
             pltpu.VMEM(weight.shape, bf16),
-            pltpu.SemaphoreType.DMA((model // 256 + 4,)),
+            pltpu.VMEM(z.shape, bf16),
+            pltpu.VMEM(out_weight.shape, bf16),
+            pltpu.SemaphoreType.DMA((model // 256 + 6,)),
         ],
         compiler_params=pltpu.CompilerParams(
-            collective_id=3, has_side_effects=True, vmem_limit_bytes=VMEM_LIMIT
+            collective_id=3, has_side_effects=True, vmem_limit_bytes=LARGE_LIMIT
         ),
-        cost_estimate=pl.CostEstimate(flops=60_000_000_000, bytes_accessed=30_000_000, transcendentals=0),
-    )(grad_both, weight, resid, grad_out, gain)
+        cost_estimate=pl.CostEstimate(flops=1_000_000, bytes_accessed=1_000_000, transcendentals=0),
+    )(grad_both, weight, z, out_weight, resid, grad_out, gain)
 
 
 SMALL = 512
@@ -1234,7 +1296,8 @@
 
 def last_kernel(chips, *refs):
     inner_part, output_part, weight, inner, dpre_far, middle_far, inputs_far, grad_resid_far, resid_far = refs[:9]
-    mask, first_gain, ffn_dgain, head_dgain, dtaps = refs[9:14]
+    mask, first_gain, ffn_dgain, head_dgain, dtaps, dbeta, beta, beta_part = refs[9:17]
+    refs = refs[3:]
     query_out, key_out, value_out, gate_out, beta_out, output_out, input_grad, out = refs[14:22]
     first_out, ffn_out, head_out, taps_out = refs[22:26]
     refs = refs[26:]
@@ -1256,12 +1319,15 @@
     def stream(at, source, buffers, kind):
         return pltpu.make_async_copy(source.at[at], buffers.at[lax.rem(at, 2)], slab_sems.at[kind, lax.rem(at, 2)])
 
-    def product(left, source, buffers, target, kind):
+    def product(left, source, buffers, target, kind, extra=None):
         def column(index, carry):
             when(index < shards - 1, lambda: stream(index + 1, source, buffers, kind).start())
             stream(index, source, buffers, kind).wait()
             lanes = pl.ds(pl.multiple_of(index * slab, slab), slab)
-            target[:, lanes] = mm_nt(left[...], buffers[lax.rem(index, 2)]).astype(bf16)
+            total = mm_nt(left[...], buffers[lax.rem(index, 2)])
+            if extra is not None:
+                total = total + mm(extra[0][...], extra[1][index])
+            target[:, lanes] = total.astype(bf16)
             return carry
 
         lax.fori_loop(0, shards, column, 0)
@@ -1290,21 +1356,21 @@
     small[...] = jnp.zeros_like(small)
     line.step(0, True)
     loads[0].wait()
-    product(dpre, inner, inner_slabs, grad.part, 0)
+    product(dpre, inner, inner_slabs, grad.part, 0, (dbeta, beta))
     grad.start_far()
     grad.start_near(0)
     grad.start_near(1)
     line.step(1, True)
-    line.step(0, False)
     loads[1].wait()
     product(middle, weight, down_slabs, ffn.part, 1)
+    for step in range(2, chips - 1):
+        line.step(step, True)
+    line.step(0, False)
     grad.relay(0)
     grad.relay(1)
     ffn.start_far()
     ffn.start_near(0)
     ffn.start_near(1)
-    for step in range(2, chips - 1):
-        line.step(step, True)
     for step in range(1, chips - 1):
         line.step(step, False)
     for load in loads[2:]:
@@ -1329,6 +1395,11 @@
         small[0, count + row : count + row + 1, :] = ffn_dgain[:, lanes]
     small[0, 2 * count : 2 * count + 1, 0:HEAD] = head_dgain[...]
     small[0, 16 : 16 + 3 * TAPS, :] = dtaps[...]
+    heads = beta_out.shape[0]
+    for head in range(heads):
+        for row in range(count):
+            at = 32 + head * count + row
+            small[0, at : at + 1, :] = beta_part[head : head + 1, row * SMALL : (row + 1) * SMALL]
 
     def hop(at):
         where = (dict(tensor=grad.across), dict(tensor=grad.along), dict(dp=sibling))[at]
@@ -1338,7 +1409,7 @@
         hop(at).wait()
         if at < 2:
             small[at + 1, 0:16, :] = small[at, 0:16, :] + near[at, 0:16, :]
-            small[at + 1, 16:32, :] = small[at, 16:32, :]
+            small[at + 1, 16:, :] = small[at, 16:, :]
         else:
             small[3] = small[2] + near[2]
 
@@ -1352,7 +1423,6 @@
         width = query_out.shape[1]
         for kind, target in enumerate((query_out, key_out, value_out, gate_out)):
             target[here, :] = total[:, kind * width : (kind + 1) * width]
-        beta_out[here, :] = total[:, 4 * width : 4 * width + beta_out.shape[1]]
 
     def put_output(here, total):
         turned[here, :] = total
@@ -1393,6 +1463,12 @@
         first_out[:, lanes] = total[row : row + 1, :]
         ffn_out[:, lanes] = total[count + row : count + row + 1, :]
     head_out[...] = total[2 * count : 2 * count + 1, 0:HEAD]
+    summed = small.at[0]
+    summed[...] = total
+    mine = (chip * 2 + core) * slab
+    lanes = pl.ds(pl.multiple_of(lax.rem(mine, SMALL), slab), slab)
+    for head in range(heads):
+        beta_out[head : head + 1, :] = summed[pl.ds(32 + head * count + mine // SMALL, 1), lanes]
     for kind in range(3):
         taps_out[kind] = total[16 + kind * TAPS : 16 + (kind + 1) * TAPS, :]
     grad.finish()
@@ -1401,7 +1477,8 @@
 
 
 def last_scatter(
-    inner_part, output_part, weight, inner, dpre, middle, inputs, grad_resid, resid, mask, gain, ffn_dgain, head_dgain, dtaps
+    inner_part, output_part, weight, inner, dpre, middle, inputs, grad_resid, resid, mask, gain, ffn_dgain, head_dgain, dtaps,
+    dbeta, beta, beta_part
 ):
     chips = lax.axis_size("dp") // 2
     rows, model = inputs.shape
@@ -1410,11 +1487,11 @@
     shape = jax.ShapeDtypeStruct
     return pl.pallas_call(
         functools.partial(last_kernel, chips),
-        in_specs=anywhere(9) + in_vmem(5),
+        in_specs=anywhere(9) + in_vmem(8),
         out_specs=in_vmem(12),
         out_shape=[shape((slab, width), f32)] * 4
         + [
-            shape((slab, width // HEAD), f32),
+            shape((width // HEAD, slab), f32),
             shape((width, slab), f32),
             shape((rows, model), f32),
             shape((rows, model), bf16),
@@ -1430,9 +1507,9 @@
         + plane_scatter_scratch(rows, model)
         + [
             pltpu.VMEM((slab, width), f32),
-            pltpu.VMEM((4, 32, SMALL), f32),
-            pltpu.VMEM((3, 32, SMALL), f32),
-            pltpu.VMEM((chips, 32, SMALL), f32),
+            pltpu.VMEM((4, 48, SMALL), f32),
+            pltpu.VMEM((3, 48, SMALL), f32),
+            pltpu.VMEM((chips, 48, SMALL), f32),
             pltpu.VMEM((1, model), f32),
             pltpu.SemaphoreType.DMA((2 + chips,)),
             pltpu.SemaphoreType.DMA((2 + chips,)),
@@ -1449,8 +1526,8 @@
         compiler_params=pltpu.CompilerParams(
             collective_id=4, has_side_effects=True, vmem_limit_bytes=LARGE_LIMIT
         ),
-        cost_estimate=pl.CostEstimate(flops=80_000_000_000, bytes_accessed=20_000_000, transcendentals=0),
-    )(inner_part, output_part, weight, inner, dpre, middle, inputs, grad_resid, resid, mask, gain, ffn_dgain, head_dgain, dtaps)
+        cost_estimate=pl.CostEstimate(flops=1_000_000, bytes_accessed=1_000_000, transcendentals=0),
+    )(inner_part, output_part, weight, inner, dpre, middle, inputs, grad_resid, resid, mask, gain, ffn_dgain, head_dgain, dtaps, dbeta, beta, beta_part)
 
 
 def rms_norm(values, gain):
@@ -1471,13 +1548,13 @@
     w_query, w_key, w_value, w_gate_out, w_beta, w_output, inputs, cotangent, mask, gain, w_gate, w_up, w_down
 ):
     shards = lax.axis_size("dp")
-    padded = jnp.pad(w_beta, ((0, 0), (0, BETA_PAD - w_beta.shape[1])))
-    inner = jnp.concatenate([w_query, w_key, w_value, w_gate_out, padded], axis=1).astype(bf16)
+    inner = jnp.concatenate([w_query, w_key, w_value, w_gate_out], axis=1).astype(bf16)
     output = w_output.T.astype(bf16)
     grad = (cotangent.astype(f32) * mask).astype(bf16)
     return (
         gather(inner, "dp").reshape(shards, *inner.shape),
         gather(output, "dp").reshape(shards, *output.shape),
+        gather(w_beta, "dp").reshape(shards, *w_beta.shape),
         gather(rms_norm(inputs.astype(f32), gain[0]).astype(bf16), "tensor"),
         gather(grad, "tensor"),
         jnp.concatenate([w_gate, w_up], axis=1).astype(bf16),
@@ -1492,17 +1569,24 @@
     return resid, gather(rms_norm(resid, gain[0]).astype(bf16), "tensor")
 
 
-def plain_resid_backward(grad_both, weight, resid, grad_out, gain):
+def plain_resid_backward(grad_both, weight, z, out_weight, resid, grad_out, gain):
     part = mm_nt(grad_both, weight).astype(bf16)
     back, gain_part = norm_backward(resid, scatter(part, "tensor").astype(f32), gain)
     value = grad_out.astype(f32) + back
-    return value, gather(value.astype(bf16), "tensor"), jnp.sum(gain_part, axis=0, keepdims=True)
+    full = gather(value.astype(bf16), "tensor")
+    dgain = jnp.sum(gain_part, axis=0, keepdims=True)
+    return value, dgain, mm(full, out_weight).astype(bf16), mm_tn(full, z).astype(bf16)
 
 
 def plain_last_scatter(
-    inner_part, output_part, weight, inner, dpre, middle, inputs, grad_resid, resid, mask, gain, ffn_dgain, head_dgain, dtaps
+    inner_part, output_part, weight, inner, dpre, middle, inputs, grad_resid, resid, mask, gain, ffn_dgain, head_dgain, dtaps,
+    dbeta, beta, beta_part
 ):
-    grad_part = mm_nt(dpre, inner.reshape(-1, inner.shape[2])).astype(bf16)
+    beta = beta.transpose(1, 0, 2).reshape(BETA_PAD, -1)
+    grad_part = (mm_nt(dpre, inner.reshape(-1, inner.shape[2])) + mm(dbeta, beta)).astype(bf16)
+    slab = inner_part.shape[1]
+    beta_total = lax.psum(beta_part[: output_part.shape[2] // HEAD], "dp")
+    beta_total = lax.dynamic_slice_in_dim(beta_total, lax.axis_index("dp") * slab, slab, axis=1)
     inner, output = (
         scatter(part.reshape(-1, part.shape[-1]), "dp").astype(f32) for part in (inner_part, output_part)
     )
@@ -1513,7 +1597,7 @@
     gains = (jnp.sum(gain_part, axis=0, keepdims=True), ffn_dgain, head_dgain)
     return (
         *(inner[:, kind * width : (kind + 1) * width] for kind in range(4)),
-        inner[:, 4 * width : 4 * width + width // HEAD],
+        beta_total,
         output.T,
         grad_resid + back,
         out,
@@ -1555,14 +1639,16 @@
 
     positions = lax.axis_index("tensor") * rows + jnp.arange(rows, dtype=jnp.int32)
     mask = (positions < lengths[0]).astype(f32)[:, None]
-    inner, full_output, normed, grad_full, gate_up, down, grad_out = (
+    beta_rows = jnp.pad(w_beta.T, ((0, BETA_PAD - w_beta.shape[1]), (0, 0))).astype(bf16)
+    inner, full_output, full_beta, normed, grad_full, gate_up, down, grad_out = (
         first_gather if kernels else plain_first_gather
-    )(w_query, w_key, w_value, w_gate_out, w_beta, w_output, inputs, cotangent, mask, first_gain, w_gate, w_up, w_down)
+    )(w_query, w_key, w_value, w_gate_out, beta_rows, w_output, inputs, cotangent, mask, first_gain, w_gate, w_up, w_down)
     gate_up = gather(gate_up, "dp")
     down = gather(down, "dp")
 
     pre = jnp.dot(normed, inner.reshape(model, -1), preferred_element_type=f32).astype(bf16)
-    z, conv, mixed, inverse, states = mixer_forward(pre, taps, head_gain, heads)
+    beta_pre = mm_nt(normed, full_beta.transpose(1, 0, 2).reshape(BETA_PAD, model))
+    z, conv, mixed, inverse, states = mixer_forward(pre, beta_pre, taps, head_gain, heads)
     resid, normed2 = (branch_and_norm if kernels else plain_branch_and_norm)(z, full_output, inputs, ffn_gain)
     middle, slopes = (ffn if kernels else plain_ffn)(normed2, gate_up)
     down_part = mm_tn(grad_full, middle).astype(bf16)
@@ -1571,12 +1657,13 @@
     grad_both = (ffn_backward if kernels else plain_ffn_backward)(grad_full, down, slopes)
     grad_both, both_part = lax.optimization_barrier((grad_both, mm_tn(normed2, grad_both).astype(bf16)))
     both_total = scatter(both_part, "dp")
-    grad_resid, grad_resid_full, ffn_dgain = (resid_backward if kernels else plain_resid_backward)(
-        grad_both, gate_up, resid, grad_out, ffn_gain
+    grad_resid, ffn_dgain, dz, output_grad = (resid_backward if kernels else plain_resid_backward)(
+        grad_both, gate_up, z, full_output.reshape(model, width), resid, grad_out, ffn_gain
     )
-    dz = jnp.dot(grad_resid_full, full_output.reshape(model, width), preferred_element_type=f32).astype(bf16)
-    dpre, dtaps, head_dgain = mixer_backward(pre, conv, mixed, dz, inverse, states, taps, head_gain, heads)
-    output_grad = mm_tn(grad_resid_full, z).astype(bf16).reshape(shards, slab, width)
+    dpre, dbeta, beta_part, dtaps, head_dgain = mixer_backward(
+        pre, beta_pre, normed, conv, mixed, dz, inverse, states, taps, head_gain, heads
+    )
+    output_grad = output_grad.reshape(shards, slab, width)
     inner_grad = mm_tn(normed, dpre).astype(bf16).reshape(shards, slab, -1)
     results = (last_scatter if kernels else plain_last_scatter)(
         inner_grad,
@@ -1593,6 +1680,9 @@
         ffn_dgain,
         head_dgain,
         dtaps,
+        dbeta,
+        full_beta,
+        beta_part,
     )
     gate_total, up_total, down_total, *results = (finish if kernels else plain_finish)(
         both_total, down_total, results
@@ -1607,7 +1697,7 @@
         key_total,
         value_total,
         gate_out_total,
-        beta_total,
+        beta_total.T,
         taps_total,
         head_total[0],
         output_total,

time: 595 us -> 576 us (0.968)
  matrix products: 67.4 us -> 58.7 us
    dot_general x4 -> x3, matrix products: 48.5 us -> 40.9 us  [mm_tn(): lax.dot_general(a, b, (((0,), (0,)), ((), ())), preferred_element_type=f32)]
    pallas_call x1, Pallas kernels: 36 us -> 29.3 us  [mixer_backward(): pl.pallas_call(functools.partial(backward_kernel, heads), grid=(steps,),...]
  transfers between devices with their start and end apart: 4 -> 4, of which waited for: 1 -> 1; matrix products, arithmetic and copies ran while one was open for 12% -> 11% of each run, Pallas kernels for 63% -> 64%
where the time goes in v2:
time: 576 us; the launch traced here: 572 us
  Pallas kernels  474 us (82%)
  matrix products  58.7 us (10%)
  waiting for transfers between devices  20.5 us (4%)
  between operations  14.7 us (3%)
    pallas_call x1, Pallas kernels, last_scatter(): pl.pallas_call(functools.partial(last_kernel, chips), in_specs=anywhere(9...  119 us
    pallas_call x1, Pallas kernels, first_gather(): pl.pallas_call(functools.partial(first_gather_kernel, shards // 2), in_sp...  96.9 us
    pallas_call x1, Pallas kernels, resid_backward(): pl.pallas_call(functools.partial(resid_kernel, 256), in_specs=anywhere(4)...  88.4 us
    pallas_call x1, Pallas kernels, branch_and_norm(): pl.pallas_call(branch_kernel, in_specs=in_vmem(4), out_specs=in_vmem(1) +...  80.6 us
    dot_general x3, matrix products, mm_tn(): lax.dot_general(a, b, (((0,), (0,)), ((), ())), preferred_element_type=f32)  40.9 us
    pallas_call x1, Pallas kernels, mixer_backward(): pl.pallas_call(functools.partial(backward_kernel, heads), grid=(steps,),...  29.3 us
    all_gather x2, waiting for transfers between devices, gather(): return lax.all_gather(values, axis, axis=0, tiled=True)  19.7 us
    pallas_call x1, Pallas kernels, ffn(): pl.pallas_call(ffn_kernel, grid=(hidden // LANES,), in_specs=[pl.BlockSpe...  19.5 us
  transfers between devices with their start and end apart: 4, of which 1 were waited for; matrix products, arithmetic and copies ran while one was open for 11% of the time, Pallas kernels for 64%

profile of v2, /device:TPU:0, one launch (start us, length us, event | category | flops | bytes accessed | tf_op | source)
XLA Modules:
  0.0 572.3 jit_solution(3761203590615055606)
XLA Ops:
  7.2 0.0 all-gather.5.cloned.1.call-start
  7.9 0.7 convert_bitcast_fusion
  8.6 0.6 pad.5.refs_4_
  9.2 0.7 fusion.refs_8_.refs_9_
  9.8 0.0 copy-start.2
  9.9 96.9 %shard_map.271 = (bf16[8,256,2048]{2,1,0:T(8,128)(2,1)}, bf16[8,256,512]{2,1,0:T(8,128)(2,1)}, bf16[8,16,256]{2,1,0:T(8,128)(2,1)}, bf16[1024,2048]{1,0:T(8,128)...) custom-call(f32[256,512]{1,0:T(8,128)} %refs_0_.1, ...), custom_call_target="tpu_custom_call" | custom-call | flops 80000000000 | bytes 20000000 | tf_op jit(solution)/shard_map/pallas_call | solution.py:893
  106.8 0.0 all-gather.5.cloned.1.call-update
  106.8 0.0 all-gather.3.cloned.1.call-start
  106.9 0.7 all-gather.3.cloned.1.call-update
  107.6 0.0 reduce-scatter.5.cloned.1.call-start
  107.6 0.0 copy-done.2
  107.6 0.6 reshape.76.taps_ref
  108.3 0.0 copy-start
  108.3 1.0 copy.37
  109.3 4.5 fusion.1.beta_ref
  113.7 0.0 copy-done
  113.7 13.3 %convolution_convert_fusion.3.pre_ref = bf16[1024,2048]{1,0:T(8,128)(2,1)} fusion(bf16[1024,2048]{1,0:T(8,128)(2,1)S(1)} %copy-done, bf16[2048,2048]{1,0:T(8,128)(2,1)} %bitcast.29), kind=kOutput, calls=%fused_computation.3 | convolution fusion | flops 8592031744 | bytes 16777216 | tf_op jit(solution)/shard_map/dot_general | solution.py:1649
  127.0 18.4 %shard_map.272 = (bf16[1024,512]{1,0:T(8,128)(2,1)}, f32[1024,1536]{1,0:T(8,128)}, f32[1024,512]{1,0:T(8,128)}, bf16[4,8,128,128]{3,2,1,0:T(8,128)(2,1)}, bf16[4,8,128,128]{3,2,1,0:T(8,128)(2,1)}) custom-call(bf16[1024,2048]{1,0:T(8,128)(2,1)} %convolution_convert_fusion.3.pre_ref, f32[1024,16]{1,0:T(8,128)} %fusion.1.beta_ref, f32[12,512]{1,0:T(8,128)} %reshape.76.taps_ref, ...), custom_call_target="tpu_custom_call" | custom-call | flops 8053063680 | bytes 20971520 | tf_op jit(solution)/shard_map/pallas_call | solution.py:136
  145.4 80.6 %shard_map.273 = (f32[256,2048]{1,0:T(8,128)}, bf16[1024,2048]{1,0:T(8,128)(2,1)}) custom-call(bf16[1024,512]{1,0:T(8,128)(2,1)} %get-tuple-element.77.z.z_far, bf16[8,256,512]{2,1,0:T(8,128)(2,1)} %get-tuple-element.78.weight, bf16[256,2048]{1,0:T(8,128)(2,1)} %refs_6_.3, f32[1,2048]{1,0:T(1,128)} %bitcast.36), custom_call_target="tpu_custom_call" | custom-call | flops 49999998976 | bytes 20000000 | tf_op jit(solution)/shard_map/pallas_call | solution.py:977
  226.1 0.0 all-gather.5.cloned.1.call-done.weight.weight_far
  226.1 0.0 copy-start.3
  226.1 19.5 %shard_map.274 = (bf16[1024,1408]{1,0:T(8,128)(2,1)}, bf16[1024,2816]{1,0:T(8,128)(2,1)}) custom-call(bf16[1024,2048]{1,0:T(8,128)(2,1)} %get-tuple-element.79.normed, bf16[2048,2816]{1,0:T(8,128)(2,1)} %all-gather.5.cloned.1.call-done.weight.weight_far), custom_call_target="tpu_custom_call" | custom-call | flops 11811160064 | bytes 15728640 | tf_op jit(solution)/shard_map/pallas_call | solution.py:759
  245.6 0.0 copy-done.3
  245.6 10.3 %convolution_convert_fusion.2 = bf16[2048,1408]{1,0:T(8,128)(2,1)} fusion(bf16[1024,2048]{1,0:T(8,128)(2,1)S(1)} %copy-done.3, bf16[1024,1408]{1,0:T(8,128)(2,1)} %get-tuple-element.81.refs_5_), kind=kOutput, calls=%fused_computation.2 | convolution fusion | flops 5908463616 | bytes 12845056 | tf_op jit(solution)/shard_map/dot_general | solution.py:30
  255.9 19.7 %all-gather.3.cloned.1.call-done.weight = bf16[2048,1408]{1,0:T(8,128)(2,1)} async-done(((bf16[256,1408]{1,0:T(8,128)(2,1)}), bf16[2048,1408]{1,0:T(8,128)(2,1)}) %all-gather.3.cloned.1.call-update) | async-done | bytes 5767184 | tf_op jit(solution)/shard_map/all_gather | solution.py:1540
  275.6 0.0 reduce-scatter.5.cloned.1.call-update
  275.6 0.3 reduce-scatter.3.cloned.1.call-start
  275.9 0.0 copy-start.4
  275.9 13.0 %shard_map.275.grad_far = bf16[1024,2816]{1,0:T(8,128)(2,1)} custom-call(bf16[1024,2048]{1,0:T(8,128)(2,1)} %get-tuple-element.72.grad, bf16[2048,1408]{1,0:T(8,128)(2,1)} %all-gather.3.cloned.1.call-done.weight, bf16[1024,2816]{1,0:T(8,128)(2,1)} %get-tuple-element.83.slopes), custom_call_target="tpu_custom_call" | custom-call | flops 5905580032 | bytes 21495808 | tf_op jit(solution)/shard_map/pallas_call | solution.py:796
  288.9 0.0 copy-done.4
  288.9 17.3 %convolution_convert_fusion = bf16[2048,2816]{1,0:T(8,128)(2,1)} fusion(bf16[1024,2048]{1,0:T(8,128)(2,1)S(1)} %copy-done.4, bf16[1024,2816]{1,0:T(8,128)(2,1)} %shard_map.275.grad_far), kind=kOutput, calls=%fused_computation | convolution fusion | flops 11816927232 | bytes 21495808 | tf_op jit(solution)/shard_map/dot_general | solution.py:30
  306.1 0.0 reduce-scatter.3.cloned.1.call-update
  306.2 88.4 %shard_map.276 = (f32[256,2048]{1,0:T(8,128)}, f32[1,2048]{1,0:T(1,128)}, bf16[1024,512]{1,0:T(8,128)(2,1)}, bf16[2048,512]{1,0:T(8,128)(2,1)}) custom-call(bf16[1024,2816]{1,0:T(8,128)(2,1)} %shard_map.275.grad_far, bf16[2048,2816]{1,0:T(8,128)(2,1)} %all-gather.5.cloned.1.call-done.weight.weight_far, bf16[1024,512]{1,0:T(8,128)(2,1)} %get-tuple-element.77.z.z_far, ...), custom_call_target="tpu_custom_call" | custom-call | flops 1000000 | bytes 1000000 | tf_op jit(solution)/shard_map/pallas_call | solution.py:1262
  394.6 0.0 copy-start.1
  394.6 29.3 %shard_map.277 = (bf16[1024,2048]{1,0:T(8,128)(2,1)}, bf16[1024,16]{1,0:T(8,128)(2,1)}, f32[16,2048]{1,0:T(8,128)}, f32[12,512]{1,0:T(8,128)}, f32[1,128]{1,0:T(1,128)}) custom-call(bf16[1024,2048]{1,0:T(8,128)(2,1)} %convolution_convert_fusion.3.pre_ref, f32[1024,16]{1,0:T(8,128)} %fusion.1.beta_ref, bf16[1024,2048]{1,0:T(8,128)(2,1)} %get-tuple-element.74.source_ref, ...), custom_call_target="tpu_custom_call" | custom-call | flops 1000000 | bytes 1000000 | tf_op jit(solution)/shard_map/pallas_call | solution.py:323
  423.9 0.0 copy-done.1
  423.9 13.3 %convolution_convert_fusion.1 = bf16[2048,2048]{1,0:T(8,128)(2,1)} fusion(bf16[1024,2048]{1,0:T(8,128)(2,1)S(1)} %copy-done.1, bf16[1024,2048]{1,0:T(8,128)(2,1)} %get-tuple-element.94.refs_4_), kind=kOutput, calls=%fused_computation.1 | convolution fusion | flops 8594128896 | bytes 16777216 | tf_op jit(solution)/shard_map/dot_general | solution.py:30
  437.2 119.4 %shard_map.278 = (f32[256,512]{1,0:T(8,128)}, f32[256,512]{1,0:T(8,128)}, f32[256,512]{1,0:T(8,128)}, f32[256,512]{1,0:T(8,128)}, f32[4,256]{1,0:T(4,128)}, /*in...) custom-call(bf16[8,256,2048]{2,1,0:T(8,128)(2,1)} %bitcast.30, ...), custom_call_target="tpu_custom_call" | custom-call | flops 1000000 | bytes 1000000 | tf_op jit(solution)/shard_map/pallas_call | solution.py:1488
  556.7 0.0 reduce-scatter.5.cloned.1.call-done.refs_1_
  556.7 0.0 reduce-scatter.3.cloned.1.call-done.refs_0_
  556.7 8.8 %shard_map.279 = (f32[256,1408]{1,0:T(8,128)}, f32[256,1408]{1,0:T(8,128)}, f32[1408,256]{1,0:T(8,128)}, f32[256,512]{1,0:T(8,128)}, f32[256,512]{1,0:T(8,128)},...) custom-call(bf16[256,2816]{1,0:T(8,128)(2,1)} %reduce-scatter.3.clon, ...), custom_call_target="tpu_custom_call" | custom-call | bytes 14417920 | tf_op jit(solution)/shard_map/pallas_call | solution.py:843
Async XLA Ops:
  7.2 218.9 %all-gather.5.cloned.1.call-start = ((), (), s32[]{:S(2)}) async-start(), calls=%async_computation.3 | async-start | bytes 12976128 | tf_op jit(solution)/shard_map/all_gather | solution.py:1540
  9.8 97.8 %copy-start.2 = (f32[3,4,512]{2,1,0:T(4,128)S(1)}, f32[3,4,512]{2,1,0:T(4,128)}, u32[]{:S(2)}) copy-start(f32[3,4,512]{2,1,0:T(4,128)} %param.25) | copy-start | bytes 73732
  106.8 168.8 %all-gather.3.cloned.1.call-start = ((), (), s32[]{:S(2)}) async-start(), calls=%async_computation.2 | async-start | bytes 6488064 | tf_op jit(solution)/shard_map/all_gather | solution.py:1540
  107.6 449.1 %reduce-scatter.5.cloned.1.call-start = ((), (), s32[]{:S(2)}) async-start(), calls=%async_computation.5 | async-start | bytes 6488064 | tf_op jit(solution)/shard_map/reduce_scatter | solution.py:1544
  108.3 5.5 copy-start
  226.1 19.5 %copy-start.3 = (bf16[1024,2048]{1,0:T(8,128)(2,1)S(1)}, bf16[1024,2048]{1,0:T(8,128)(2,1)}, u32[]{:S(2)}) copy-start(bf16[1024,2048]{1,0:T(8,128)(2,1)} %get-tuple-element.72.grad) | copy-start | bytes 12582916
  275.6 281.1 %reduce-scatter.3.cloned.1.call-start = ((), (), s32[]{:S(2)}) async-start(), calls=%async_computation.4 | async-start | bytes 12976128 | tf_op jit(solution)/shard_map/reduce_scatter | solution.py:1544
  275.9 13.0 %copy-start.4 = (bf16[1024,2048]{1,0:T(8,128)(2,1)S(1)}, bf16[1024,2048]{1,0:T(8,128)(2,1)}, u32[]{:S(2)}) copy-start(bf16[1024,2048]{1,0:T(8,128)(2,1)} %get-tuple-element.79.normed) | copy-start | bytes 12582916
  394.6 29.3 %copy-start.1 = (bf16[1024,2048]{1,0:T(8,128)(2,1)S(1)}, bf16[1024,2048]{1,0:T(8,128)(2,1)}, u32[]{:S(2)}) copy-start(bf16[1024,2048]{1,0:T(8,128)(2,1)} %get-tuple-element.74.source_ref) | copy-start | bytes 12582916
Sparse Core Ops, SparseCore 0:
  106.9 108.2 all-gather.4
  216.8 58.7 all-gather.2
  277.9 63.5 reduce-scatter.4
  343.7 131.3 reduce-scatter.2

commit v3 on v2

--- a/solution.py
+++ b/solution.py
@@ -364,6 +364,7 @@
 
 MESH = pl.DeviceIdType.MESH
 TILE = 16
+BOTH_LAST = 512
 LANES = 128
 LARGE_LIMIT = 60 * 1024 * 1024
 
@@ -780,19 +781,23 @@
     )(normed, gate_up)
 
 
-def ffn_backward_kernel(grad, weight, slopes, grad_both):
+def ffn_backward_kernel(grad, weight, slopes, low, high):
+    split = low.shape[1] // LANES
     grad_middle = mm(grad[...], weight[...])
     for tile in range(weight.shape[1] // LANES):
         part = grad_middle[:, tile * LANES : (tile + 1) * LANES]
         for kind in range(2):
-            lanes = slice((2 * tile + kind) * LANES, (2 * tile + kind + 1) * LANES)
-            grad_both[:, lanes] = (part * slopes[:, lanes].astype(f32)).astype(bf16)
+            at = 2 * tile + kind
+            target, to = (low, at) if at < split else (high, at - split)
+            slope = slopes[:, at * LANES : (at + 1) * LANES].astype(f32)
+            target[:, to * LANES : (to + 1) * LANES] = (part * slope).astype(bf16)
 
 
 def ffn_backward(grad, down, slopes):
     length, model = grad.shape
     hidden = down.shape[1]
     block = 512
+    widths = (2 * hidden - BOTH_LAST, BOTH_LAST)
     return pl.pallas_call(
         ffn_backward_kernel,
         grid=(length // block,),
@@ -801,8 +806,8 @@
             pl.BlockSpec((model, hidden), lambda i: (0, 0)),
             pl.BlockSpec((block, 2 * hidden), lambda i: (i, 0)),
         ],
-        out_specs=pl.BlockSpec((block, 2 * hidden), lambda i: (i, 0)),
-        out_shape=jax.ShapeDtypeStruct((length, 2 * hidden), bf16),
+        out_specs=[pl.BlockSpec((block, width), lambda i: (i, 0)) for width in widths],
+        out_shape=[jax.ShapeDtypeStruct((length, width), bf16) for width in widths],
         compiler_params=pltpu.CompilerParams(
             dimension_semantics=("arbitrary",), vmem_limit_bytes=VMEM_LIMIT
         ),
@@ -813,48 +818,60 @@
 
 
 def finish_kernel(count, *refs):
-    both, down = refs[:2]
-    sources, gate_out, up_out, down_out = refs[2 : 2 + count], *refs[2 + count : 5 + count]
-    targets, held, sems = refs[5 + count : 5 + 2 * count], refs[5 + 2 * count : 5 + 3 * count], refs[-1]
+    sources, targets, held, sems = refs[:count], refs[count : 2 * count], refs[2 * count : 3 * count], refs[-1]
+    kept, outs = held[:3], refs[3 * count : 3 * count + 3]
     loads = [
         pltpu.make_async_copy(source, here, sems.at[0, at]) for at, (source, here) in enumerate(zip(sources, held))
     ]
     stores = [
-        pltpu.make_async_copy(here, target, sems.at[1, at]) for at, (here, target) in enumerate(zip(held, targets))
+        pltpu.make_async_copy(here, target, sems.at[1, at])
+        for at, (here, target) in enumerate(zip((*outs, *held[3:]), targets))
     ]
     for load in loads:
         load.start()
+    low, high, down = kept
+    gate_out, up_out, down_out = outs
+    split = low.shape[1] // LANES
+    for load in loads[:3]:
+        load.wait()
     for tile in range(gate_out.shape[1] // LANES):
-        lanes = slice(tile * LANES, (tile + 1) * LANES)
-        gate_out[:, lanes] = both[:, 2 * tile * LANES : (2 * tile + 1) * LANES].astype(f32)
-        up_out[:, lanes] = both[:, (2 * tile + 1) * LANES : (2 * tile + 2) * LANES].astype(f32)
-    for load, store in zip(loads, stores):
+        for kind, target in enumerate((gate_out, up_out)):
+            at = 2 * tile + kind
+            source, start = (low, at) if at < split else (high, at - split)
+            target[:, tile * LANES : (tile + 1) * LANES] = source[:, start * LANES : (start + 1) * LANES].astype(f32)
+    stores[0].start()
+    stores[1].start()
+    for load, store in zip(loads[3:], stores[3:]):
         load.wait()
         store.start()
     for tile in range(gate_out.shape[1] // LANES):
         lanes = slice(tile * LANES, (tile + 1) * LANES)
         down_out[lanes, :] = jnp.transpose(down[:, lanes].astype(f32))
+    stores[2].start()
     for store in stores:
         store.wait()
 
 
-def finish(both, down, arrays):
+def finish(low, high, down, arrays):
     slab, hidden = down.shape
+    sources = [low, high, down, *arrays]
+    count = len(sources)
+    outs = [
+        jax.ShapeDtypeStruct((slab, hidden), f32),
+        jax.ShapeDtypeStruct((slab, hidden), f32),
+        jax.ShapeDtypeStruct((hidden, slab), f32),
+    ]
     return pl.pallas_call(
-        functools.partial(finish_kernel, len(arrays)),
-        in_specs=in_vmem(2) + anywhere(len(arrays)),
-        out_specs=in_vmem(3) + anywhere(len(arrays)),
-        out_shape=[
-            jax.ShapeDtypeStruct((slab, hidden), f32),
-            jax.ShapeDtypeStruct((slab, hidden), f32),
-            jax.ShapeDtypeStruct((hidden, slab), f32),
-        ]
-        + [jax.ShapeDtypeStruct(array.shape, array.dtype) for array in arrays],
-        scratch_shapes=[pltpu.VMEM(array.shape, array.dtype) for array in arrays]
-        + [pltpu.SemaphoreType.DMA((2, len(arrays)))],
+        functools.partial(finish_kernel, count),
+        in_specs=anywhere(count),
+        out_specs=anywhere(count),
+        out_shape=outs + [jax.ShapeDtypeStruct(array.shape, array.dtype) for array in arrays],
+        scratch_shapes=[pltpu.VMEM(array.shape, array.dtype) for array in sources]
+        + [pltpu.VMEM(out.shape, f32) for out in outs]
+        + [pltpu.SemaphoreType.DMA((2, count))],
         compiler_params=pltpu.CompilerParams(vmem_limit_bytes=VMEM_LIMIT),
         cost_estimate=pl.CostEstimate(flops=0, bytes_accessed=40 * slab * hidden, transcendentals=0),
-    )(both, down, *arrays)
+    )(*sources)
 
 
 def plain_ffn(normed, gate_up):
@@ -866,11 +883,12 @@
 
 def plain_ffn_backward(grad, down, slopes):
     grad_middle = jnp.dot(grad, down, preferred_element_type=f32)
-    return (jnp.concatenate([grad_middle, grad_middle], axis=1) * slopes.astype(f32)).astype(bf16)
-
-
-def plain_finish(both, down, arrays):
-    gate, up_part = jnp.split(both.astype(f32), 2, axis=1)
+    both = (jnp.concatenate([grad_middle, grad_middle], axis=1) * slopes.astype(f32)).astype(bf16)
+    return both[:, :-BOTH_LAST], both[:, -BOTH_LAST:]
+
+
+def plain_finish(low, high, down, arrays):
+    gate, up_part = jnp.split(jnp.concatenate([low.astype(f32), high], axis=1), 2, axis=1)
     return gate, up_part, down.astype(f32).T, *arrays
 
 
@@ -1098,7 +1116,7 @@
             self.load(self.pieces[piece][0], dest).wait()
         self.trade(piece, dest).wait_recv()
 
-    def step(self, step, ends):
+    def step(self, step, ends, turns=(0, 1)):
         to_right, to_left = self.chips - 1 - step, step
 
         def send_right(piece):
@@ -1126,10 +1144,10 @@
         lead = 2
         for at in range(count + lead):
             early, late = at, at - lead
-            if early < count:
+            if 0 in turns and early < count:
                 when(low & inner_right, functools.partial(send_right, early))
                 when(jnp.logical_not(low) & inner_left, functools.partial(send_left, early))
-            if late >= 0:
+            if 1 in turns and late >= 0:
                 when(low & inner_left, functools.partial(send_left, late))
                 when(jnp.logical_not(low) & inner_right, functools.partial(send_right, late))
 
@@ -1152,32 +1170,42 @@
 
 
 def resid_kernel(
-    slab, grad_far, weight_far, z_far, out_weight_far, resid, grad_out, gain, grad_resid, dgain, dz, output_grad,
+    chips, slab, low_far, high_far, weight_far, z_far, out_weight_far, resid, grad_out, gain, high_part,
+    grad_resid, dgain, dz, output_grad, high_out,
     part, first, second, stage, low, full, total, s_send, s_recv, g_send, g_recv,
-    grad_both, weight, z, out_weight, load_sems
+    grad_both, weight, z, out_weight, load_sems, *rest
 ):
     scatter = PlaneScatter(part, first, second, stage, s_send, s_recv)
     gather = PlaneGather(low, full, g_send, g_recv)
+    line = LineScatter(chips, [high_part], rest[:1], rest[1:2], rest[2:3], rest[3:])
     rows = scatter.rows
+    split = low_far.shape[1]
     slabs = weight.shape[0] // slab
     order = (scatter.far, scatter.across, scatter.along, scatter.me)
+    greetings = greet_line(chips)
     greet(tensor=scatter.across)
     greet(tensor=scatter.along)
 
-    def rows_load(at):
+    def rows_loads(at):
         here = pl.ds(scatter.start_of(order[at], 0), rows)
-        return pltpu.make_async_copy(grad_far.at[here], grad_both.at[here], load_sems.at[slabs + at])
+        return [
+            pltpu.make_async_copy(far.at[here], grad_both.at[here, lanes], load_sems.at[slabs + 2 * at + which])
+            for which, (far, lanes) in enumerate(
+                ((low_far, pl.ds(0, split)), (high_far, pl.ds(split, grad_both.shape[1] - split)))
+            )
+        ]
 
     def slab_load(index):
         here = pl.ds(pl.multiple_of(index * slab, slab), slab)
         return pltpu.make_async_copy(weight_far.at[here], weight.at[here], load_sems.at[index])
 
     late_loads = [
-        pltpu.make_async_copy(z_far, z, load_sems.at[slabs + 4]),
-        pltpu.make_async_copy(out_weight_far, out_weight, load_sems.at[slabs + 5]),
+        pltpu.make_async_copy(z_far, z, load_sems.at[slabs + 8]),
+        pltpu.make_async_copy(out_weight_far, out_weight, load_sems.at[slabs + 9]),
     ]
     for at in range(4):
-        rows_load(at).start()
+        for load in rows_loads(at):
+            load.start()
         if at == 0:
             for index in range(slabs):
                 slab_load(index).start()
@@ -1186,7 +1214,8 @@
 
     def compute(at):
         here = pl.ds(scatter.start_of(order[at], 0), rows)
-        rows_load(at).wait()
+        for load in rows_loads(at):
+            load.wait()
 
         def column(index, carry):
             lanes = pl.ds(pl.multiple_of(index * slab, slab), slab)
@@ -1198,16 +1227,20 @@
         lax.fori_loop(0, slabs, column, 0)
 
     compute(0)
-    wait_greetings(2)
+    wait_greetings(2 + greetings)
     scatter.start_far()
+    line.start()
     compute(1)
     scatter.start_near(0)
     compute(2)
     scatter.start_near(1)
+    line.step(0, True)
     compute(3)
     dgain[...] = jnp.zeros_like(dgain)
     scatter.relay(0)
     scatter.relay(1)
+    for step in range(1, chips - 1):
+        line.step(step, True)
     for half in (0, 1):
         scatter.ready(half)
 
@@ -1223,6 +1256,8 @@
 
         lax.fori_loop(0, scatter.half // TILE, norm, 0)
         gather.start(half)
+        if half == 0:
+            line.step(0, False, (0,))
     for load in late_loads:
         load.wait()
 
@@ -1243,31 +1278,42 @@
 
     gather.relay(0)
     gather.relay(1)
+    line.step(0, False, (1,))
+    for step in range(1, chips - 1):
+        line.step(step, False)
     use(scatter.me, low, True)
     gather.near(0)
     use(scatter.across, block_of(scatter.across))
     gather.near(1)
     use(scatter.along, block_of(scatter.along))
 
+    def put(here, total):
+        high_out[here, :] = total
+
+    line.keep([put], range(len(line.pieces)))
     gather.diagonal()
     use(scatter.far, block_of(scatter.far))
     output_grad[...] = total[...].astype(bf16)
     gather.sent()
     scatter.finish()
-
-
-def resid_backward(grad_both, weight, z, out_weight, resid, grad_out, gain):
+    line.finish()
+
+
+def resid_backward(grad_low, grad_high, weight, z, out_weight, resid, grad_out, gain, high_part):
+    chips = lax.axis_size("dp") // 2
     rows, model = resid.shape
     width = z.shape[1]
+    slab, columns = high_part.shape[1:]
     return pl.pallas_call(
-        functools.partial(resid_kernel, 256),
-        in_specs=anywhere(4) + in_vmem(3),
-        out_specs=in_vmem(4),
+        functools.partial(resid_kernel, chips, 256),
+        in_specs=anywhere(5) + in_vmem(3) + anywhere(1),
+        out_specs=in_vmem(5),
         out_shape=[
             jax.ShapeDtypeStruct((rows, model), f32),
             jax.ShapeDtypeStruct((1, model), f32),
             jax.ShapeDtypeStruct((4 * rows, width), bf16),
             jax.ShapeDtypeStruct((model, width), bf16),
+            jax.ShapeDtypeStruct((slab, columns), f32),
         ],
         scratch_shapes=[pltpu.VMEM((4 * rows, model), bf16)]
         + plane_scatter_scratch(rows, model)[:3]
@@ -1282,13 +1328,14 @@
             pltpu.VMEM(weight.shape, bf16),
             pltpu.VMEM(z.shape, bf16),
             pltpu.VMEM(out_weight.shape, bf16),
-            pltpu.SemaphoreType.DMA((model // 256 + 6,)),
-        ],
+            pltpu.SemaphoreType.DMA((model // 256 + 10,)),
+        ]
+        + LineScatter.scratch(chips, [high_part]),
         compiler_params=pltpu.CompilerParams(
             collective_id=3, has_side_effects=True, vmem_limit_bytes=LARGE_LIMIT
         ),
         cost_estimate=pl.CostEstimate(flops=1_000_000, bytes_accessed=1_000_000, transcendentals=0),
-    )(grad_both, weight, z, out_weight, resid, grad_out, gain)
+    )(grad_low, grad_high, weight, z, out_weight, resid, grad_out, gain, high_part)
 
 
 SMALL = 512
@@ -1569,13 +1616,14 @@
     return resid, gather(rms_norm(resid, gain[0]).astype(bf16), "tensor")
 
 
-def plain_resid_backward(grad_both, weight, z, out_weight, resid, grad_out, gain):
-    part = mm_nt(grad_both, weight).astype(bf16)
+def plain_resid_backward(grad_low, grad_high, weight, z, out_weight, resid, grad_out, gain, high_part):
+    part = mm_nt(jnp.concatenate([grad_low, grad_high], axis=1), weight).astype(bf16)
     back, gain_part = norm_backward(resid, scatter(part, "tensor").astype(f32), gain)
     value = grad_out.astype(f32) + back
     full = gather(value.astype(bf16), "tensor")
+    high = scatter(high_part.reshape(-1, high_part.shape[2]), "dp").astype(f32)
     dgain = jnp.sum(gain_part, axis=0, keepdims=True)
-    return value, dgain, mm(full, out_weight).astype(bf16), mm_tn(full, z).astype(bf16)
+    return value, dgain, mm(full, out_weight).astype(bf16), mm_tn(full, z).astype(bf16), high
 
 
 def plain_last_scatter(
@@ -1654,11 +1702,20 @@
     down_part = mm_tn(grad_full, middle).astype(bf16)
     down, down_part = lax.optimization_barrier((down, down_part))
     down_total = scatter(down_part, "dp")
-    grad_both = (ffn_backward if kernels else plain_ffn_backward)(grad_full, down, slopes)
-    grad_both, both_part = lax.optimization_barrier((grad_both, mm_tn(normed2, grad_both).astype(bf16)))
-    both_total = scatter(both_part, "dp")
-    grad_resid, ffn_dgain, dz, output_grad = (resid_backward if kernels else plain_resid_backward)(
-        grad_both, gate_up, z, full_output.reshape(model, width), resid, grad_out, ffn_gain
+    grad_low, grad_high = (ffn_backward if kernels else plain_ffn_backward)(grad_full, down, slopes)
+    low_part, high_part = mm_tn(normed2, grad_low).astype(bf16), mm_tn(normed2, grad_high).astype(bf16)
+    grad_low, grad_high, low_part = lax.optimization_barrier((grad_low, grad_high, low_part))
+    low_total = scatter(low_part, "dp")
+    grad_resid, ffn_dgain, dz, output_grad, high_total = (resid_backward if kernels else plain_resid_backward)(
+        grad_low,
+        grad_high,
+        gate_up,
+        z,
+        full_output.reshape(model, width),
+        resid,
+        grad_out,
+        ffn_gain,
+        high_part.reshape(shards, slab, -1),
     )
     dpre, dbeta, beta_part, dtaps, head_dgain = mixer_backward(
         pre, beta_pre, normed, conv, mixed, dz, inverse, states, taps, head_gain, heads
@@ -1685,7 +1742,7 @@
         beta_part,
     )
     gate_total, up_total, down_total, *results = (finish if kernels else plain_finish)(
-        both_total, down_total, results
+        low_total, high_total, down_total, results
     )
     query_total, key_total, value_total, gate_out_total, beta_total, output_total, input_grad, output = results[:8]
     first_total, ffn_total, head_total, taps_total = results[8:]

time: 576 us -> 588 us (1.021)
  Pallas kernels: 474 us -> 482 us
    dot_general x3 -> x4, matrix products: 40.9 us -> 44.3 us  [mm_tn(): lax.dot_general(a, b, (((0,), (0,)), ((), ())), preferred_element_type=f32)]
  transfers between devices with their start and end apart: 4 -> 4, of which waited for: 1 -> 1; matrix products, arithmetic and copies ran while one was open for 11% -> 11% of each run, Pallas kernels for 64% -> 65%
where the time goes in v3:
time: 588 us; the launch traced here: 584 us
  Pallas kernels  482 us (82%)
  matrix products  62.1 us (11%)
  waiting for transfers between devices  20.4 us (3%)
  between operations  14.7 us (2%)
    pallas_call x1, Pallas kernels, last_scatter(): pl.pallas_call(functools.partial(last_kernel, chips), in_specs=anywhere(9...  122 us
    pallas_call x1, Pallas kernels, first_gather(): pl.pallas_call(functools.partial(first_gather_kernel, shards // 2), in_sp...  96.9 us
    pallas_call x1, Pallas kernels, resid_backward(): pl.pallas_call(functools.partial(resid_kernel, chips, 256), in_specs=anyw...  96 us
    pallas_call x1, Pallas kernels, branch_and_norm(): pl.pallas_call(branch_kernel, in_specs=in_vmem(4), out_specs=in_vmem(1) +...  80.7 us
    dot_general x4, matrix products, mm_tn(): lax.dot_general(a, b, (((0,), (0,)), ((), ())), preferred_element_type=f32)  44.3 us
    pallas_call x1, Pallas kernels, mixer_backward(): pl.pallas_call(functools.partial(backward_kernel, heads), grid=(steps,),...  28.6 us
    all_gather x2, waiting for transfers between devices, gather(): return lax.all_gather(values, axis, axis=0, tiled=True)  19.6 us
    pallas_call x1, Pallas kernels, ffn(): pl.pallas_call(ffn_kernel, grid=(hidden // LANES,), in_specs=[pl.BlockSpe...  19.4 us
  transfers between devices with their start and end apart: 4, of which 1 were waited for; matrix products, arithmetic and copies ran while one was open for 11% of the time, Pallas kernels for 65%

profile of v3, /device:TPU:0, one launch (start us, length us, event | category | flops | bytes accessed | tf_op | source)
XLA Modules:
  0.0 584.1 jit_solution(8677067314145336848)
XLA Ops:
  7.2 0.0 all-gather.5.cloned.1.call-start
  7.9 0.7 convert_bitcast_fusion
  8.6 0.6 pad.5.refs_4_
  9.2 0.7 fusion.refs_8_.refs_9_
  9.8 0.0 copy-start.3
  9.8 96.9 %shard_map.271 = (bf16[8,256,2048]{2,1,0:T(8,128)(2,1)}, bf16[8,256,512]{2,1,0:T(8,128)(2,1)}, bf16[8,16,256]{2,1,0:T(8,128)(2,1)}, bf16[1024,2048]{1,0:T(8,128)...) custom-call(f32[256,512]{1,0:T(8,128)} %refs_0_.1, ...), custom_call_target="tpu_custom_call" | custom-call | flops 80000000000 | bytes 20000000 | tf_op jit(solution)/shard_map/pallas_call | solution.py:911
  106.8 0.0 all-gather.5.cloned.1.call-update
  106.8 0.0 all-gather.3.cloned.1.call-start
  106.9 0.7 all-gather.3.cloned.1.call-update
  107.6 0.0 reduce-scatter.5.cloned.1.call-start
  107.6 0.0 copy-done.3
  107.6 0.6 reshape.79.taps_ref
  108.3 0.0 copy-start
  108.3 1.0 copy.37
  109.3 4.5 fusion.1.beta_ref
  113.7 0.0 copy-done
  113.7 13.3 %convolution_convert_fusion.3.pre_ref = bf16[1024,2048]{1,0:T(8,128)(2,1)} fusion(bf16[1024,2048]{1,0:T(8,128)(2,1)S(1)} %copy-done, bf16[2048,2048]{1,0:T(8,128)(2,1)} %bitcast.32), kind=kOutput, calls=%fused_computation.3 | convolution fusion | flops 8592031744 | bytes 16777216 | tf_op jit(solution)/shard_map/dot_general | solution.py:1697
  127.0 18.4 %shard_map.272 = (bf16[1024,512]{1,0:T(8,128)(2,1)}, f32[1024,1536]{1,0:T(8,128)}, f32[1024,512]{1,0:T(8,128)}, bf16[4,8,128,128]{3,2,1,0:T(8,128)(2,1)}, bf16[4,8,128,128]{3,2,1,0:T(8,128)(2,1)}) custom-call(bf16[1024,2048]{1,0:T(8,128)(2,1)} %convolution_convert_fusion.3.pre_ref, f32[1024,16]{1,0:T(8,128)} %fusion.1.beta_ref, f32[12,512]{1,0:T(8,128)} %reshape.79.taps_ref, ...), custom_call_target="tpu_custom_call" | custom-call | flops 8053063680 | bytes 20971520 | tf_op jit(solution)/shard_map/pallas_call | solution.py:136
  145.4 80.7 %shard_map.273 = (f32[256,2048]{1,0:T(8,128)}, bf16[1024,2048]{1,0:T(8,128)(2,1)}) custom-call(bf16[1024,512]{1,0:T(8,128)(2,1)} %get-tuple-element.81.z.z_far, bf16[8,256,512]{2,1,0:T(8,128)(2,1)} %get-tuple-element.82.weight, bf16[256,2048]{1,0:T(8,128)(2,1)} %refs_6_.3, f32[1,2048]{1,0:T(1,128)} %bitcast.40), custom_call_target="tpu_custom_call" | custom-call | flops 49999998976 | bytes 20000000 | tf_op jit(solution)/shard_map/pallas_call | solution.py:995
  226.1 0.0 all-gather.5.cloned.1.call-done.weight.weight_far
  226.1 0.0 copy-start.4
  226.1 19.4 %shard_map.274 = (bf16[1024,1408]{1,0:T(8,128)(2,1)}, bf16[1024,2816]{1,0:T(8,128)(2,1)}) custom-call(bf16[1024,2048]{1,0:T(8,128)(2,1)} %get-tuple-element.83.normed, bf16[2048,2816]{1,0:T(8,128)(2,1)} %all-gather.5.cloned.1.call-done.weight.weight_far), custom_call_target="tpu_custom_call" | custom-call | flops 11811160064 | bytes 15728640 | tf_op jit(solution)/shard_map/pallas_call | solution.py:760
  245.5 0.0 copy-done.4
  245.5 10.5 %convolution_convert_fusion.2 = bf16[2048,1408]{1,0:T(8,128)(2,1)} fusion(bf16[1024,2048]{1,0:T(8,128)(2,1)S(1)} %copy-done.4, bf16[1024,1408]{1,0:T(8,128)(2,1)} %get-tuple-element.85.refs_5_), kind=kOutput, calls=%fused_computation.2 | convolution fusion | flops 5908463616 | bytes 12845056 | tf_op jit(solution)/shard_map/dot_general | solution.py:30
  256.0 19.6 %all-gather.3.cloned.1.call-done.weight = bf16[2048,1408]{1,0:T(8,128)(2,1)} async-done(((bf16[256,1408]{1,0:T(8,128)(2,1)}), bf16[2048,1408]{1,0:T(8,128)(2,1)}) %all-gather.3.cloned.1.call-update) | async-done | bytes 5767184 | tf_op jit(solution)/shard_map/all_gather | solution.py:1587
  275.6 0.0 reduce-scatter.5.cloned.1.call-update
  275.6 0.3 reduce-scatter.3.cloned.1.call-start
  275.9 0.0 copy-start.5
  275.9 12.9 %shard_map.275 = (bf16[1024,2304]{1,0:T(8,128)(2,1)}, bf16[1024,512]{1,0:T(8,128)(2,1)}) custom-call(bf16[1024,2048]{1,0:T(8,128)(2,1)} %get-tuple-element.76.grad, bf16[2048,1408]{1,0:T(8,128)(2,1)} %all-gather.3.cloned.1.call-done.weight, bf16[1024,2816]{1,0:T(8,128)(2,1)} %get-tuple-element.87.slopes), custom_call_target="tpu_custom_call" | custom-call | flops 5905580032 | bytes 21495808 | tf_op jit(solution)/shard_map/pallas_call | solution.py:801
  288.8 0.0 copy-done.5
  288.8 14.6 %convolution_convert_fusion = bf16[2048,2304]{1,0:T(8,128)(2,1)} fusion(bf16[1024,2048]{1,0:T(8,128)(2,1)S(1)} %copy-done.5, bf16[1024,2304]{1,0:T(8,128)(2,1)} %get-tuple-element.91.low_far), kind=kOutput, calls=%fused_computation | convolution fusion | flops 9668395008 | bytes 18350080 | tf_op jit(solution)/shard_map/dot_general | solution.py:30
  303.4 0.0 copy-start.2
  303.4 0.0 reduce-scatter.3.cloned.1.call-update
  303.4 1.2 copy-done.2
  304.6 5.9 %convolution_convert_fusion.4 = bf16[2048,512]{1,0:T(8,128)(2,1)} fusion(bf16[1024,2048]{1,0:T(8,128)(2,1)} %get-tuple-element.83.normed, bf16[1024,512]{1,0:T(8,128)(2,1)S(1)} %copy-done.2), kind=kOutput, calls=%fused_computation.4 | convolution fusion | flops 2148532224 | bytes 7340032 | tf_op jit(solution)/shard_map/dot_general | solution.py:30
  310.5 96.0 %shard_map.276 = (f32[256,2048]{1,0:T(8,128)}, f32[1,2048]{1,0:T(1,128)}, bf16[1024,512]{1,0:T(8,128)(2,1)}, bf16[2048,512]{1,0:T(8,128)(2,1)}, f32[256,512]{1,0:T(8,128)}) custom-call(bf16[1024,2304]{1,0:T(8,128)(2,1)} %get-tuple-element.91.low_far, bf16[1024,512]{1,0:T(8,128)(2,1)} %get-tuple-element.92.high_far, ...), custom_call_target="tpu_custom_call" | custom-call | flops 1000000 | bytes 1000000 | tf_op jit(solution)/shard_map/pallas_call | solution.py:1307
  406.5 0.0 copy-start.1
  406.5 28.6 %shard_map.277 = (bf16[1024,2048]{1,0:T(8,128)(2,1)}, bf16[1024,16]{1,0:T(8,128)(2,1)}, f32[16,2048]{1,0:T(8,128)}, f32[12,512]{1,0:T(8,128)}, f32[1,128]{1,0:T(1,128)}) custom-call(bf16[1024,2048]{1,0:T(8,128)(2,1)} %convolution_convert_fusion.3.pre_ref, f32[1024,16]{1,0:T(8,128)} %fusion.1.beta_ref, bf16[1024,2048]{1,0:T(8,128)(2,1)} %get-tuple-element.78.source_ref, ...), custom_call_target="tpu_custom_call" | custom-call | flops 1000000 | bytes 1000000 | tf_op jit(solution)/shard_map/pallas_call | solution.py:323
  435.1 0.0 copy-done.1
  435.2 13.4 %convolution_convert_fusion.1 = bf16[2048,2048]{1,0:T(8,128)(2,1)} fusion(bf16[1024,2048]{1,0:T(8,128)(2,1)S(1)} %copy-done.1, bf16[1024,2048]{1,0:T(8,128)(2,1)} %get-tuple-element.102.refs_4_), kind=kOutput, calls=%fused_computation.1 | convolution fusion | flops 8594128896 | bytes 16777216 | tf_op jit(solution)/shard_map/dot_general | solution.py:30
  448.5 121.9 %shard_map.278 = (f32[256,512]{1,0:T(8,128)}, f32[256,512]{1,0:T(8,128)}, f32[256,512]{1,0:T(8,128)}, f32[256,512]{1,0:T(8,128)}, f32[4,256]{1,0:T(4,128)}, /*in...) custom-call(bf16[8,256,2048]{2,1,0:T(8,128)(2,1)} %bitcast.33, ...), custom_call_target="tpu_custom_call" | custom-call | flops 1000000 | bytes 1000000 | tf_op jit(solution)/shard_map/pallas_call | solution.py:1535
  570.5 0.0 reduce-scatter.5.cloned.1.call-done.refs_2_
  570.5 0.0 reduce-scatter.3.cloned.1.call-done.refs_0_
  570.5 6.8 %shard_map.279 = (f32[256,1408]{1,0:T(8,128)}, f32[256,1408]{1,0:T(8,128)}, f32[1408,256]{1,0:T(8,128)}, f32[256,512]{1,0:T(8,128)}, f32[256,512]{1,0:T(8,128)},...) custom-call(bf16[256,2304]{1,0:T(8,128)(2,1)} %reduce-scatter.3.clon, ...), custom_call_target="tpu_custom_call" | custom-call | bytes 14417920 | tf_op jit(solution)/shard_map/pallas_call | solution.py:864
Async XLA Ops:
  7.2 218.9 %all-gather.5.cloned.1.call-start = ((), (), s32[]{:S(2)}) async-start(), calls=%async_computation.3 | async-start | bytes 12976128 | tf_op jit(solution)/shard_map/all_gather | solution.py:1587
  9.8 97.8 %copy-start.3 = (f32[3,4,512]{2,1,0:T(4,128)S(1)}, f32[3,4,512]{2,1,0:T(4,128)}, u32[]{:S(2)}) copy-start(f32[3,4,512]{2,1,0:T(4,128)} %param.25) | copy-start | bytes 73732
  106.8 168.8 %all-gather.3.cloned.1.call-start = ((), (), s32[]{:S(2)}) async-start(), calls=%async_computation.2 | async-start | bytes 6488064 | tf_op jit(solution)/shard_map/all_gather | solution.py:1587
  107.6 462.9 %reduce-scatter.5.cloned.1.call-start = ((), (), s32[]{:S(2)}) async-start(), calls=%async_computation.5 | async-start | bytes 6488064 | tf_op jit(solution)/shard_map/reduce_scatter | solution.py:1591
  108.3 5.5 copy-start
  226.1 19.4 %copy-start.4 = (bf16[1024,2048]{1,0:T(8,128)(2,1)S(1)}, bf16[1024,2048]{1,0:T(8,128)(2,1)}, u32[]{:S(2)}) copy-start(bf16[1024,2048]{1,0:T(8,128)(2,1)} %get-tuple-element.76.grad) | copy-start | bytes 12582916
  275.6 294.9 %reduce-scatter.3.cloned.1.call-start = ((), (), s32[]{:S(2)}) async-start(), calls=%async_computation.4 | async-start | bytes 10616832 | tf_op jit(solution)/shard_map/reduce_scatter | solution.py:1591
  275.9 12.9 %copy-start.5 = (bf16[1024,2048]{1,0:T(8,128)(2,1)S(1)}, bf16[1024,2048]{1,0:T(8,128)(2,1)}, u32[]{:S(2)}) copy-start(bf16[1024,2048]{1,0:T(8,128)(2,1)} %get-tuple-element.83.normed) | copy-start | bytes 12582916
  303.4 1.2 copy-start.2
  406.5 28.7 %copy-start.1 = (bf16[1024,2048]{1,0:T(8,128)(2,1)S(1)}, bf16[1024,2048]{1,0:T(8,128)(2,1)}, u32[]{:S(2)}) copy-start(bf16[1024,2048]{1,0:T(8,128)(2,1)} %get-tuple-element.78.source_ref) | copy-start | bytes 12582916
Sparse Core Ops, SparseCore 0:
  106.9 108.2 all-gather.4
  216.9 58.7 all-gather.2
  277.9 73.4 reduce-scatter.4
  353.6 96.9 reduce-scatter.2

commit v4 on v3

--- a/solution.py
+++ b/solution.py
@@ -1181,7 +1181,7 @@
     rows = scatter.rows
     split = low_far.shape[1]
     slabs = weight.shape[0] // slab
-    order = (scatter.far, scatter.across, scatter.along, scatter.me)
+    order = (scatter.far, scatter.along, scatter.across, scatter.me)
     greetings = greet_line(chips)
     greet(tensor=scatter.across)
     greet(tensor=scatter.along)
@@ -1206,36 +1206,36 @@
     for at in range(4):
         for load in rows_loads(at):
             load.start()
-        if at == 0:
+        if at == 1:
             for index in range(slabs):
                 slab_load(index).start()
     for load in late_loads:
         load.start()
 
-    def compute(at):
-        here = pl.ds(scatter.start_of(order[at], 0), rows)
-        for load in rows_loads(at):
-            load.wait()
+    def compute(blocks, first):
+        start = pl.multiple_of(scatter.start_of(jnp.minimum(order[blocks[0]], order[blocks[1]]), 0), rows)
+        here = pl.ds(start, 2 * rows)
+        for at in blocks:
+            for load in rows_loads(at):
+                load.wait()
 
         def column(index, carry):
             lanes = pl.ds(pl.multiple_of(index * slab, slab), slab)
-            if at == 0:
+            if first:
                 slab_load(index).wait()
             part[here, lanes] = mm_nt(grad_both[here, :], weight[lanes, :]).astype(bf16)
             return carry
 
         lax.fori_loop(0, slabs, column, 0)
 
-    compute(0)
+    compute((0, 1), True)
     wait_greetings(2 + greetings)
     scatter.start_far()
+    scatter.start_near(1)
     line.start()
-    compute(1)
+    compute((2, 3), False)
     scatter.start_near(0)
-    compute(2)
-    scatter.start_near(1)
     line.step(0, True)
-    compute(3)
     dgain[...] = jnp.zeros_like(dgain)
     scatter.relay(0)
     scatter.relay(1)
@@ -1366,15 +1366,22 @@
     def stream(at, source, buffers, kind):
         return pltpu.make_async_copy(source.at[at], buffers.at[lax.rem(at, 2)], slab_sems.at[kind, lax.rem(at, 2)])
 
-    def product(left, source, buffers, target, kind, extra=None):
+    rows = inputs.shape[0]
+
+    def product(left, source, buffers, each, kind, mine, extra=None):
+        pair = each.me // 2
+        here = pl.ds(pl.multiple_of((pair if mine else 1 - pair) * 2 * rows, 2 * rows), 2 * rows)
+
         def column(index, carry):
-            when(index < shards - 1, lambda: stream(index + 1, source, buffers, kind).start())
+            def following():
+                stream(lax.rem(index + 1, shards), source, buffers, kind).start()
+
+            when(index < (shards - 1 if mine else shards), following)
             stream(index, source, buffers, kind).wait()
-            lanes = pl.ds(pl.multiple_of(index * slab, slab), slab)
-            total = mm_nt(left[...], buffers[lax.rem(index, 2)])
+            total = mm_nt(left[here, :], buffers[lax.rem(index, 2)])
             if extra is not None:
-                total = total + mm(extra[0][...], extra[1][index])
-            target[:, lanes] = total.astype(bf16)
+                total = total + mm(extra[0][here, :], extra[1][index])
+            each.part[here, pl.ds(pl.multiple_of(index * slab, slab), slab)] = total.astype(bf16)
             return carry
 
         lax.fori_loop(0, shards, column, 0)
@@ -1403,21 +1410,24 @@
     small[...] = jnp.zeros_like(small)
     line.step(0, True)
     loads[0].wait()
-    product(dpre, inner, inner_slabs, grad.part, 0, (dbeta, beta))
+    product(dpre, inner, inner_slabs, grad, 0, False, (dbeta, beta))
     grad.start_far()
-    grad.start_near(0)
     grad.start_near(1)
     line.step(1, True)
+    product(dpre, inner, inner_slabs, grad, 0, True, (dbeta, beta))
+    grad.start_near(0)
+    line.step(0, False, (0,))
     loads[1].wait()
-    product(middle, weight, down_slabs, ffn.part, 1)
+    product(middle, weight, down_slabs, ffn, 1, False)
     for step in range(2, chips - 1):
         line.step(step, True)
-    line.step(0, False)
     grad.relay(0)
     grad.relay(1)
     ffn.start_far()
+    ffn.start_near(1)
+    product(middle, weight, down_slabs, ffn, 1, True)
     ffn.start_near(0)
-    ffn.start_near(1)
+    line.step(0, False, (1,))
     for step in range(1, chips - 1):
         line.step(step, False)
     for load in loads[2:]:

time: 588 us -> 580 us (0.986)
  Pallas kernels: 482 us -> 472 us
    pallas_call x1, Pallas kernels: 122 us -> 106 us  [last_scatter(): pl.pallas_call(functools.partial(last_kernel, chips), in_specs=anywhere(9...]
    pallas_call x1, Pallas kernels: 96 us -> 103 us  [resid_backward(): pl.pallas_call(functools.partial(resid_kernel, chips, 256), in_specs=anyw...]
  transfers between devices with their start and end apart: 4 -> 4, of which waited for: 1 -> 1; matrix products, arithmetic and copies ran while one was open for 11% -> 11% of each run, Pallas kernels for 65% -> 64%
where the time goes in v4:
time: 580 us; the launch traced here: 575 us
  Pallas kernels  472 us (81%)
  matrix products  62.1 us (11%)
  waiting for transfers between devices  20.4 us (4%)
  between operations  14.7 us (3%)
    pallas_call x1, Pallas kernels, last_scatter(): pl.pallas_call(functools.partial(last_kernel, chips), in_specs=anywhere(9...  106 us
    pallas_call x1, Pallas kernels, resid_backward(): pl.pallas_call(functools.partial(resid_kernel, chips, 256), in_specs=anyw...  103 us
    pallas_call x1, Pallas kernels, first_gather(): pl.pallas_call(functools.partial(first_gather_kernel, shards // 2), in_sp...  96.9 us
    pallas_call x1, Pallas kernels, branch_and_norm(): pl.pallas_call(branch_kernel, in_specs=in_vmem(4), out_specs=in_vmem(1) +...  80.7 us
    dot_general x4, matrix products, mm_tn(): lax.dot_general(a, b, (((0,), (0,)), ((), ())), preferred_element_type=f32)  44.3 us
    pallas_call x1, Pallas kernels, mixer_backward(): pl.pallas_call(functools.partial(backward_kernel, heads), grid=(steps,),...  28.8 us
    all_gather x2, waiting for transfers between devices, gather(): return lax.all_gather(values, axis, axis=0, tiled=True)  19.6 us
    pallas_call x1, Pallas kernels, ffn(): pl.pallas_call(ffn_kernel, grid=(hidden // LANES,), in_specs=[pl.BlockSpe...  19.4 us
  transfers between devices with their start and end apart: 4, of which 1 were waited for; matrix products, arithmetic and copies ran while one was open for 11% of the time, Pallas kernels for 64%

profile of v4, /device:TPU:0, one launch (start us, length us, event | category | flops | bytes accessed | tf_op | source)
XLA Modules:
  0.0 574.8 jit_solution(4513528682820899904)
XLA Ops:
  7.2 0.0 all-gather.5.cloned.1.call-start
  7.9 0.7 convert_bitcast_fusion
  8.6 0.6 pad.5.refs_4_
  9.2 0.7 fusion.refs_8_.refs_9_
  9.8 0.0 copy-start.3
  9.8 96.9 %shard_map.271 = (bf16[8,256,2048]{2,1,0:T(8,128)(2,1)}, bf16[8,256,512]{2,1,0:T(8,128)(2,1)}, bf16[8,16,256]{2,1,0:T(8,128)(2,1)}, bf16[1024,2048]{1,0:T(8,128)...) custom-call(f32[256,512]{1,0:T(8,128)} %refs_0_.1, ...), custom_call_target="tpu_custom_call" | custom-call | flops 80000000000 | bytes 20000000 | tf_op jit(solution)/shard_map/pallas_call | solution.py:911
  106.8 0.0 all-gather.5.cloned.1.call-update
  106.8 0.0 all-gather.3.cloned.1.call-start
  106.9 0.7 all-gather.3.cloned.1.call-update
  107.6 0.0 reduce-scatter.5.cloned.1.call-start
  107.6 0.0 copy-done.3
  107.6 0.6 reshape.79.taps_ref
  108.3 0.0 copy-start
  108.3 1.0 copy.37
  109.3 4.5 fusion.1.beta_ref
  113.7 0.0 copy-done
  113.7 13.3 %convolution_convert_fusion.3.pre_ref = bf16[1024,2048]{1,0:T(8,128)(2,1)} fusion(bf16[1024,2048]{1,0:T(8,128)(2,1)S(1)} %copy-done, bf16[2048,2048]{1,0:T(8,128)(2,1)} %bitcast.32), kind=kOutput, calls=%fused_computation.3 | convolution fusion | flops 8592031744 | bytes 16777216 | tf_op jit(solution)/shard_map/dot_general | solution.py:1707
  127.0 18.4 %shard_map.272 = (bf16[1024,512]{1,0:T(8,128)(2,1)}, f32[1024,1536]{1,0:T(8,128)}, f32[1024,512]{1,0:T(8,128)}, bf16[4,8,128,128]{3,2,1,0:T(8,128)(2,1)}, bf16[4,8,128,128]{3,2,1,0:T(8,128)(2,1)}) custom-call(bf16[1024,2048]{1,0:T(8,128)(2,1)} %convolution_convert_fusion.3.pre_ref, f32[1024,16]{1,0:T(8,128)} %fusion.1.beta_ref, f32[12,512]{1,0:T(8,128)} %reshape.79.taps_ref, ...), custom_call_target="tpu_custom_call" | custom-call | flops 8053063680 | bytes 20971520 | tf_op jit(solution)/shard_map/pallas_call | solution.py:136
  145.4 80.7 %shard_map.273 = (f32[256,2048]{1,0:T(8,128)}, bf16[1024,2048]{1,0:T(8,128)(2,1)}) custom-call(bf16[1024,512]{1,0:T(8,128)(2,1)} %get-tuple-element.81.z.z_far, bf16[8,256,512]{2,1,0:T(8,128)(2,1)} %get-tuple-element.82.weight, bf16[256,2048]{1,0:T(8,128)(2,1)} %refs_6_.3, f32[1,2048]{1,0:T(1,128)} %bitcast.40), custom_call_target="tpu_custom_call" | custom-call | flops 49999998976 | bytes 20000000 | tf_op jit(solution)/shard_map/pallas_call | solution.py:995
  226.1 0.0 all-gather.5.cloned.1.call-done.weight.weight_far
  226.1 0.0 copy-start.4
  226.1 19.4 %shard_map.274 = (bf16[1024,1408]{1,0:T(8,128)(2,1)}, bf16[1024,2816]{1,0:T(8,128)(2,1)}) custom-call(bf16[1024,2048]{1,0:T(8,128)(2,1)} %get-tuple-element.83.normed, bf16[2048,2816]{1,0:T(8,128)(2,1)} %all-gather.5.cloned.1.call-done.weight.weight_far), custom_call_target="tpu_custom_call" | custom-call | flops 11811160064 | bytes 15728640 | tf_op jit(solution)/shard_map/pallas_call | solution.py:760
  245.5 0.0 copy-done.4
  245.5 10.5 %convolution_convert_fusion.2 = bf16[2048,1408]{1,0:T(8,128)(2,1)} fusion(bf16[1024,2048]{1,0:T(8,128)(2,1)S(1)} %copy-done.4, bf16[1024,1408]{1,0:T(8,128)(2,1)} %get-tuple-element.85.refs_5_), kind=kOutput, calls=%fused_computation.2 | convolution fusion | flops 5908463616 | bytes 12845056 | tf_op jit(solution)/shard_map/dot_general | solution.py:30
  256.0 19.6 %all-gather.3.cloned.1.call-done.weight = bf16[2048,1408]{1,0:T(8,128)(2,1)} async-done(((bf16[256,1408]{1,0:T(8,128)(2,1)}), bf16[2048,1408]{1,0:T(8,128)(2,1)}) %all-gather.3.cloned.1.call-update) | async-done | bytes 5767184 | tf_op jit(solution)/shard_map/all_gather | solution.py:1597
  275.6 0.0 reduce-scatter.5.cloned.1.call-update
  275.6 0.3 reduce-scatter.3.cloned.1.call-start
  275.9 0.0 copy-start.5
  275.9 12.9 %shard_map.275 = (bf16[1024,2304]{1,0:T(8,128)(2,1)}, bf16[1024,512]{1,0:T(8,128)(2,1)}) custom-call(bf16[1024,2048]{1,0:T(8,128)(2,1)} %get-tuple-element.76.grad, bf16[2048,1408]{1,0:T(8,128)(2,1)} %all-gather.3.cloned.1.call-done.weight, bf16[1024,2816]{1,0:T(8,128)(2,1)} %get-tuple-element.87.slopes), custom_call_target="tpu_custom_call" | custom-call | flops 5905580032 | bytes 21495808 | tf_op jit(solution)/shard_map/pallas_call | solution.py:801
  288.8 0.0 copy-done.5
  288.8 14.6 %convolution_convert_fusion = bf16[2048,2304]{1,0:T(8,128)(2,1)} fusion(bf16[1024,2048]{1,0:T(8,128)(2,1)S(1)} %copy-done.5, bf16[1024,2304]{1,0:T(8,128)(2,1)} %get-tuple-element.91.low_far), kind=kOutput, calls=%fused_computation | convolution fusion | flops 9668395008 | bytes 18350080 | tf_op jit(solution)/shard_map/dot_general | solution.py:30
  303.4 0.0 copy-start.2
  303.4 0.0 reduce-scatter.3.cloned.1.call-update
  303.4 1.2 copy-done.2
  304.6 5.9 %convolution_convert_fusion.4 = bf16[2048,512]{1,0:T(8,128)(2,1)} fusion(bf16[1024,2048]{1,0:T(8,128)(2,1)} %get-tuple-element.83.normed, bf16[1024,512]{1,0:T(8,128)(2,1)S(1)} %copy-done.2), kind=kOutput, calls=%fused_computation.4 | convolution fusion | flops 2148532224 | bytes 7340032 | tf_op jit(solution)/shard_map/dot_general | solution.py:30
  310.5 102.9 %shard_map.276 = (f32[256,2048]{1,0:T(8,128)}, f32[1,2048]{1,0:T(1,128)}, bf16[1024,512]{1,0:T(8,128)(2,1)}, bf16[2048,512]{1,0:T(8,128)(2,1)}, f32[256,512]{1,0:T(8,128)}) custom-call(bf16[1024,2304]{1,0:T(8,128)(2,1)} %get-tuple-element.91.low_far, bf16[1024,512]{1,0:T(8,128)(2,1)} %get-tuple-element.92.high_far, ...), custom_call_target="tpu_custom_call" | custom-call | flops 1000000 | bytes 1000000 | tf_op jit(solution)/shard_map/pallas_call | solution.py:1307
  413.5 0.0 copy-start.1
  413.5 28.8 %shard_map.277 = (bf16[1024,2048]{1,0:T(8,128)(2,1)}, bf16[1024,16]{1,0:T(8,128)(2,1)}, f32[16,2048]{1,0:T(8,128)}, f32[12,512]{1,0:T(8,128)}, f32[1,128]{1,0:T(1,128)}) custom-call(bf16[1024,2048]{1,0:T(8,128)(2,1)} %convolution_convert_fusion.3.pre_ref, f32[1024,16]{1,0:T(8,128)} %fusion.1.beta_ref, bf16[1024,2048]{1,0:T(8,128)(2,1)} %get-tuple-element.78.source_ref, ...), custom_call_target="tpu_custom_call" | custom-call | flops 1000000 | bytes 1000000 | tf_op jit(solution)/shard_map/pallas_call | solution.py:323
  442.2 0.0 copy-done.1
  442.2 13.4 %convolution_convert_fusion.1 = bf16[2048,2048]{1,0:T(8,128)(2,1)} fusion(bf16[1024,2048]{1,0:T(8,128)(2,1)S(1)} %copy-done.1, bf16[1024,2048]{1,0:T(8,128)(2,1)} %get-tuple-element.102.refs_4_), kind=kOutput, calls=%fused_computation.1 | convolution fusion | flops 8594128896 | bytes 16777216 | tf_op jit(solution)/shard_map/dot_general | solution.py:30
  455.6 105.6 %shard_map.278 = (f32[256,512]{1,0:T(8,128)}, f32[256,512]{1,0:T(8,128)}, f32[256,512]{1,0:T(8,128)}, f32[256,512]{1,0:T(8,128)}, f32[4,256]{1,0:T(4,128)}, /*in...) custom-call(bf16[8,256,2048]{2,1,0:T(8,128)(2,1)} %bitcast.33, ...), custom_call_target="tpu_custom_call" | custom-call | flops 1000000 | bytes 1000000 | tf_op jit(solution)/shard_map/pallas_call | solution.py:1545
  561.2 0.0 reduce-scatter.5.cloned.1.call-done.refs_2_
  561.2 0.0 reduce-scatter.3.cloned.1.call-done.refs_0_
  561.3 6.8 %shard_map.279 = (f32[256,1408]{1,0:T(8,128)}, f32[256,1408]{1,0:T(8,128)}, f32[1408,256]{1,0:T(8,128)}, f32[256,512]{1,0:T(8,128)}, f32[256,512]{1,0:T(8,128)},...) custom-call(bf16[256,2304]{1,0:T(8,128)(2,1)} %reduce-scatter.3.clon, ...), custom_call_target="tpu_custom_call" | custom-call | bytes 14417920 | tf_op jit(solution)/shard_map/pallas_call | solution.py:864
Async XLA Ops:
  7.2 218.9 %all-gather.5.cloned.1.call-start = ((), (), s32[]{:S(2)}) async-start(), calls=%async_computation.3 | async-start | bytes 12976128 | tf_op jit(solution)/shard_map/all_gather | solution.py:1597
  9.8 97.8 %copy-start.3 = (f32[3,4,512]{2,1,0:T(4,128)S(1)}, f32[3,4,512]{2,1,0:T(4,128)}, u32[]{:S(2)}) copy-start(f32[3,4,512]{2,1,0:T(4,128)} %param.25) | copy-start | bytes 73732
  106.8 168.8 %all-gather.3.cloned.1.call-start = ((), (), s32[]{:S(2)}) async-start(), calls=%async_computation.2 | async-start | bytes 6488064 | tf_op jit(solution)/shard_map/all_gather | solution.py:1597
  107.6 453.7 %reduce-scatter.5.cloned.1.call-start = ((), (), s32[]{:S(2)}) async-start(), calls=%async_computation.5 | async-start | bytes 6488064 | tf_op jit(solution)/shard_map/reduce_scatter | solution.py:1601
  108.3 5.5 copy-start
  226.1 19.4 %copy-start.4 = (bf16[1024,2048]{1,0:T(8,128)(2,1)S(1)}, bf16[1024,2048]{1,0:T(8,128)(2,1)}, u32[]{:S(2)}) copy-start(bf16[1024,2048]{1,0:T(8,128)(2,1)} %get-tuple-element.76.grad) | copy-start | bytes 12582916
  275.6 285.6 %reduce-scatter.3.cloned.1.call-start = ((), (), s32[]{:S(2)}) async-start(), calls=%async_computation.4 | async-start | bytes 10616832 | tf_op jit(solution)/shard_map/reduce_scatter | solution.py:1601
  275.9 12.9 %copy-start.5 = (bf16[1024,2048]{1,0:T(8,128)(2,1)S(1)}, bf16[1024,2048]{1,0:T(8,128)(2,1)}, u32[]{:S(2)}) copy-start(bf16[1024,2048]{1,0:T(8,128)(2,1)} %get-tuple-element.83.normed) | copy-start | bytes 12582916
  303.4 1.2 copy-start.2
  413.5 28.8 %copy-start.1 = (bf16[1024,2048]{1,0:T(8,128)(2,1)S(1)}, bf16[1024,2048]{1,0:T(8,128)(2,1)}, u32[]{:S(2)}) copy-start(bf16[1024,2048]{1,0:T(8,128)(2,1)} %get-tuple-element.78.source_ref) | copy-start | bytes 12582916
Sparse Core Ops, SparseCore 0:
  106.9 108.2 all-gather.4
  216.9 58.7 all-gather.2
  277.9 71.6 reduce-scatter.4
  351.8 96.9 reduce-scatter.2

commit v5 on v4

--- a/solution.py
+++ b/solution.py
@@ -1181,7 +1181,7 @@
     rows = scatter.rows
     split = low_far.shape[1]
     slabs = weight.shape[0] // slab
-    order = (scatter.far, scatter.along, scatter.across, scatter.me)
+    order = (scatter.far, scatter.across, scatter.along, scatter.me)
     greetings = greet_line(chips)
     greet(tensor=scatter.across)
     greet(tensor=scatter.along)
@@ -1206,36 +1206,36 @@
     for at in range(4):
         for load in rows_loads(at):
             load.start()
-        if at == 1:
+        if at == 0:
             for index in range(slabs):
                 slab_load(index).start()
     for load in late_loads:
         load.start()
 
-    def compute(blocks, first):
-        start = pl.multiple_of(scatter.start_of(jnp.minimum(order[blocks[0]], order[blocks[1]]), 0), rows)
-        here = pl.ds(start, 2 * rows)
-        for at in blocks:
-            for load in rows_loads(at):
-                load.wait()
+    def compute(at):
+        here = pl.ds(scatter.start_of(order[at], 0), rows)
+        for load in rows_loads(at):
+            load.wait()
 
         def column(index, carry):
             lanes = pl.ds(pl.multiple_of(index * slab, slab), slab)
-            if first:
+            if at == 0:
                 slab_load(index).wait()
             part[here, lanes] = mm_nt(grad_both[here, :], weight[lanes, :]).astype(bf16)
             return carry
 
         lax.fori_loop(0, slabs, column, 0)
 
-    compute((0, 1), True)
+    compute(0)
     wait_greetings(2 + greetings)
     scatter.start_far()
+    line.start()
+    compute(1)
+    scatter.start_near(0)
+    compute(2)
     scatter.start_near(1)
-    line.start()
-    compute((2, 3), False)
-    scatter.start_near(0)
     line.step(0, True)
+    compute(3)
     dgain[...] = jnp.zeros_like(dgain)
     scatter.relay(0)
     scatter.relay(1)

time: 580 us -> 576 us (level)
    pallas_call x1, Pallas kernels: 103 us -> 96 us  [resid_backward(): pl.pallas_call(functools.partial(resid_kernel, chips, 256), in_specs=anyw...]
where the time goes in v5:
time: 576 us; the launch traced here: 571 us
  Pallas kernels  468 us (81%)
  matrix products  62.1 us (11%)
  waiting for transfers between devices  20.4 us (4%)
  between operations  14.7 us (3%)
    pallas_call x1, Pallas kernels, last_scatter(): pl.pallas_call(functools.partial(last_kernel, chips), in_specs=anywhere(9...  109 us
    pallas_call x1, Pallas kernels, first_gather(): pl.pallas_call(functools.partial(first_gather_kernel, shards // 2), in_sp...  96.9 us
    pallas_call x1, Pallas kernels, resid_backward(): pl.pallas_call(functools.partial(resid_kernel, chips, 256), in_specs=anyw...  96 us
    pallas_call x1, Pallas kernels, branch_and_norm(): pl.pallas_call(branch_kernel, in_specs=in_vmem(4), out_specs=in_vmem(1) +...  80.7 us
    dot_general x4, matrix products, mm_tn(): lax.dot_general(a, b, (((0,), (0,)), ((), ())), preferred_element_type=f32)  44.3 us
    pallas_call x1, Pallas kernels, mixer_backward(): pl.pallas_call(functools.partial(backward_kernel, heads), grid=(steps,),...  28.6 us
    all_gather x2, waiting for transfers between devices, gather(): return lax.all_gather(values, axis, axis=0, tiled=True)  19.6 us
    pallas_call x1, Pallas kernels, ffn(): pl.pallas_call(ffn_kernel, grid=(hidden // LANES,), in_specs=[pl.BlockSpe...  19.4 us
  transfers between devices with their start and end apart: 4, of which 1 were waited for; matrix products, arithmetic and copies ran while one was open for 11% of the time, Pallas kernels for 64%

profile of v5, /device:TPU:0, one launch (start us, length us, event | category | flops | bytes accessed | tf_op | source)
XLA Modules:
  0.0 570.9 jit_solution(11259305408596176163)
XLA Ops:
  7.2 0.0 all-gather.5.cloned.1.call-start
  7.9 0.7 convert_bitcast_fusion
  8.6 0.6 pad.5.refs_4_
  9.2 0.7 fusion.refs_8_.refs_9_
  9.8 0.0 copy-start.3
  9.8 96.9 %shard_map.271 = (bf16[8,256,2048]{2,1,0:T(8,128)(2,1)}, bf16[8,256,512]{2,1,0:T(8,128)(2,1)}, bf16[8,16,256]{2,1,0:T(8,128)(2,1)}, bf16[1024,2048]{1,0:T(8,128)...) custom-call(f32[256,512]{1,0:T(8,128)} %refs_0_.1, ...), custom_call_target="tpu_custom_call" | custom-call | flops 80000000000 | bytes 20000000 | tf_op jit(solution)/shard_map/pallas_call | solution.py:911
  106.8 0.0 all-gather.5.cloned.1.call-update
  106.8 0.0 all-gather.3.cloned.1.call-start
  106.9 0.7 all-gather.3.cloned.1.call-update
  107.6 0.0 reduce-scatter.5.cloned.1.call-start
  107.6 0.0 copy-done.3
  107.6 0.6 reshape.79.taps_ref
  108.3 0.0 copy-start
  108.3 1.0 copy.37
  109.3 4.5 fusion.1.beta_ref
  113.7 0.0 copy-done
  113.7 13.3 %convolution_convert_fusion.3.pre_ref = bf16[1024,2048]{1,0:T(8,128)(2,1)} fusion(bf16[1024,2048]{1,0:T(8,128)(2,1)S(1)} %copy-done, bf16[2048,2048]{1,0:T(8,128)(2,1)} %bitcast.32), kind=kOutput, calls=%fused_computation.3 | convolution fusion | flops 8592031744 | bytes 16777216 | tf_op jit(solution)/shard_map/dot_general | solution.py:1707
  127.0 18.4 %shard_map.272 = (bf16[1024,512]{1,0:T(8,128)(2,1)}, f32[1024,1536]{1,0:T(8,128)}, f32[1024,512]{1,0:T(8,128)}, bf16[4,8,128,128]{3,2,1,0:T(8,128)(2,1)}, bf16[4,8,128,128]{3,2,1,0:T(8,128)(2,1)}) custom-call(bf16[1024,2048]{1,0:T(8,128)(2,1)} %convolution_convert_fusion.3.pre_ref, f32[1024,16]{1,0:T(8,128)} %fusion.1.beta_ref, f32[12,512]{1,0:T(8,128)} %reshape.79.taps_ref, ...), custom_call_target="tpu_custom_call" | custom-call | flops 8053063680 | bytes 20971520 | tf_op jit(solution)/shard_map/pallas_call | solution.py:136
  145.4 80.7 %shard_map.273 = (f32[256,2048]{1,0:T(8,128)}, bf16[1024,2048]{1,0:T(8,128)(2,1)}) custom-call(bf16[1024,512]{1,0:T(8,128)(2,1)} %get-tuple-element.81.z.z_far, bf16[8,256,512]{2,1,0:T(8,128)(2,1)} %get-tuple-element.82.weight, bf16[256,2048]{1,0:T(8,128)(2,1)} %refs_6_.3, f32[1,2048]{1,0:T(1,128)} %bitcast.40), custom_call_target="tpu_custom_call" | custom-call | flops 49999998976 | bytes 20000000 | tf_op jit(solution)/shard_map/pallas_call | solution.py:995
  226.1 0.0 all-gather.5.cloned.1.call-done.weight.weight_far
  226.1 0.0 copy-start.4
  226.1 19.4 %shard_map.274 = (bf16[1024,1408]{1,0:T(8,128)(2,1)}, bf16[1024,2816]{1,0:T(8,128)(2,1)}) custom-call(bf16[1024,2048]{1,0:T(8,128)(2,1)} %get-tuple-element.83.normed, bf16[2048,2816]{1,0:T(8,128)(2,1)} %all-gather.5.cloned.1.call-done.weight.weight_far), custom_call_target="tpu_custom_call" | custom-call | flops 11811160064 | bytes 15728640 | tf_op jit(solution)/shard_map/pallas_call | solution.py:760
  245.5 0.0 copy-done.4
  245.5 10.5 %convolution_convert_fusion.2 = bf16[2048,1408]{1,0:T(8,128)(2,1)} fusion(bf16[1024,2048]{1,0:T(8,128)(2,1)S(1)} %copy-done.4, bf16[1024,1408]{1,0:T(8,128)(2,1)} %get-tuple-element.85.refs_5_), kind=kOutput, calls=%fused_computation.2 | convolution fusion | flops 5908463616 | bytes 12845056 | tf_op jit(solution)/shard_map/dot_general | solution.py:30
  256.0 19.6 %all-gather.3.cloned.1.call-done.weight = bf16[2048,1408]{1,0:T(8,128)(2,1)} async-done(((bf16[256,1408]{1,0:T(8,128)(2,1)}), bf16[2048,1408]{1,0:T(8,128)(2,1)}) %all-gather.3.cloned.1.call-update) | async-done | bytes 5767184 | tf_op jit(solution)/shard_map/all_gather | solution.py:1597
  275.6 0.0 reduce-scatter.5.cloned.1.call-update
  275.6 0.3 reduce-scatter.3.cloned.1.call-start
  275.9 0.0 copy-start.5
  275.9 12.9 %shard_map.275 = (bf16[1024,2304]{1,0:T(8,128)(2,1)}, bf16[1024,512]{1,0:T(8,128)(2,1)}) custom-call(bf16[1024,2048]{1,0:T(8,128)(2,1)} %get-tuple-element.76.grad, bf16[2048,1408]{1,0:T(8,128)(2,1)} %all-gather.3.cloned.1.call-done.weight, bf16[1024,2816]{1,0:T(8,128)(2,1)} %get-tuple-element.87.slopes), custom_call_target="tpu_custom_call" | custom-call | flops 5905580032 | bytes 21495808 | tf_op jit(solution)/shard_map/pallas_call | solution.py:801
  288.8 0.0 copy-done.5
  288.8 14.6 %convolution_convert_fusion = bf16[2048,2304]{1,0:T(8,128)(2,1)} fusion(bf16[1024,2048]{1,0:T(8,128)(2,1)S(1)} %copy-done.5, bf16[1024,2304]{1,0:T(8,128)(2,1)} %get-tuple-element.91.low_far), kind=kOutput, calls=%fused_computation | convolution fusion | flops 9668395008 | bytes 18350080 | tf_op jit(solution)/shard_map/dot_general | solution.py:30
  303.4 0.0 copy-start.2
  303.4 0.0 reduce-scatter.3.cloned.1.call-update
  303.4 1.2 copy-done.2
  304.6 5.9 %convolution_convert_fusion.4 = bf16[2048,512]{1,0:T(8,128)(2,1)} fusion(bf16[1024,2048]{1,0:T(8,128)(2,1)} %get-tuple-element.83.normed, bf16[1024,512]{1,0:T(8,128)(2,1)S(1)} %copy-done.2), kind=kOutput, calls=%fused_computation.4 | convolution fusion | flops 2148532224 | bytes 7340032 | tf_op jit(solution)/shard_map/dot_general | solution.py:30
  310.5 96.0 %shard_map.276 = (f32[256,2048]{1,0:T(8,128)}, f32[1,2048]{1,0:T(1,128)}, bf16[1024,512]{1,0:T(8,128)(2,1)}, bf16[2048,512]{1,0:T(8,128)(2,1)}, f32[256,512]{1,0:T(8,128)}) custom-call(bf16[1024,2304]{1,0:T(8,128)(2,1)} %get-tuple-element.91.low_far, bf16[1024,512]{1,0:T(8,128)(2,1)} %get-tuple-element.92.high_far, ...), custom_call_target="tpu_custom_call" | custom-call | flops 1000000 | bytes 1000000 | tf_op jit(solution)/shard_map/pallas_call | solution.py:1307
  406.5 0.0 copy-start.1
  406.5 28.6 %shard_map.277 = (bf16[1024,2048]{1,0:T(8,128)(2,1)}, bf16[1024,16]{1,0:T(8,128)(2,1)}, f32[16,2048]{1,0:T(8,128)}, f32[12,512]{1,0:T(8,128)}, f32[1,128]{1,0:T(1,128)}) custom-call(bf16[1024,2048]{1,0:T(8,128)(2,1)} %convolution_convert_fusion.3.pre_ref, f32[1024,16]{1,0:T(8,128)} %fusion.1.beta_ref, bf16[1024,2048]{1,0:T(8,128)(2,1)} %get-tuple-element.78.source_ref, ...), custom_call_target="tpu_custom_call" | custom-call | flops 1000000 | bytes 1000000 | tf_op jit(solution)/shard_map/pallas_call | solution.py:323
  435.1 0.0 copy-done.1
  435.2 13.4 %convolution_convert_fusion.1 = bf16[2048,2048]{1,0:T(8,128)(2,1)} fusion(bf16[1024,2048]{1,0:T(8,128)(2,1)S(1)} %copy-done.1, bf16[1024,2048]{1,0:T(8,128)(2,1)} %get-tuple-element.102.refs_4_), kind=kOutput, calls=%fused_computation.1 | convolution fusion | flops 8594128896 | bytes 16777216 | tf_op jit(solution)/shard_map/dot_general | solution.py:30
  448.5 108.8 %shard_map.278 = (f32[256,512]{1,0:T(8,128)}, f32[256,512]{1,0:T(8,128)}, f32[256,512]{1,0:T(8,128)}, f32[256,512]{1,0:T(8,128)}, f32[4,256]{1,0:T(4,128)}, /*in...) custom-call(bf16[8,256,2048]{2,1,0:T(8,128)(2,1)} %bitcast.33, ...), custom_call_target="tpu_custom_call" | custom-call | flops 1000000 | bytes 1000000 | tf_op jit(solution)/shard_map/pallas_call | solution.py:1545
  557.3 0.0 reduce-scatter.5.cloned.1.call-done.refs_2_
  557.3 0.0 reduce-scatter.3.cloned.1.call-done.refs_0_
  557.4 6.8 %shard_map.279 = (f32[256,1408]{1,0:T(8,128)}, f32[256,1408]{1,0:T(8,128)}, f32[1408,256]{1,0:T(8,128)}, f32[256,512]{1,0:T(8,128)}, f32[256,512]{1,0:T(8,128)},...) custom-call(bf16[256,2304]{1,0:T(8,128)(2,1)} %reduce-scatter.3.clon, ...), custom_call_target="tpu_custom_call" | custom-call | bytes 14417920 | tf_op jit(solution)/shard_map/pallas_call | solution.py:864
Async XLA Ops:
  7.2 218.9 %all-gather.5.cloned.1.call-start = ((), (), s32[]{:S(2)}) async-start(), calls=%async_computation.3 | async-start | bytes 12976128 | tf_op jit(solution)/shard_map/all_gather | solution.py:1597
  9.8 97.8 %copy-start.3 = (f32[3,4,512]{2,1,0:T(4,128)S(1)}, f32[3,4,512]{2,1,0:T(4,128)}, u32[]{:S(2)}) copy-start(f32[3,4,512]{2,1,0:T(4,128)} %param.25) | copy-start | bytes 73732
  106.8 168.8 %all-gather.3.cloned.1.call-start = ((), (), s32[]{:S(2)}) async-start(), calls=%async_computation.2 | async-start | bytes 6488064 | tf_op jit(solution)/shard_map/all_gather | solution.py:1597
  107.6 449.8 %reduce-scatter.5.cloned.1.call-start = ((), (), s32[]{:S(2)}) async-start(), calls=%async_computation.5 | async-start | bytes 6488064 | tf_op jit(solution)/shard_map/reduce_scatter | solution.py:1601
  108.3 5.5 copy-start
  226.1 19.4 %copy-start.4 = (bf16[1024,2048]{1,0:T(8,128)(2,1)S(1)}, bf16[1024,2048]{1,0:T(8,128)(2,1)}, u32[]{:S(2)}) copy-start(bf16[1024,2048]{1,0:T(8,128)(2,1)} %get-tuple-element.76.grad) | copy-start | bytes 12582916
  275.6 281.7 %reduce-scatter.3.cloned.1.call-start = ((), (), s32[]{:S(2)}) async-start(), calls=%async_computation.4 | async-start | bytes 10616832 | tf_op jit(solution)/shard_map/reduce_scatter | solution.py:1601
  275.9 12.9 %copy-start.5 = (bf16[1024,2048]{1,0:T(8,128)(2,1)S(1)}, bf16[1024,2048]{1,0:T(8,128)(2,1)}, u32[]{:S(2)}) copy-start(bf16[1024,2048]{1,0:T(8,128)(2,1)} %get-tuple-element.83.normed) | copy-start | bytes 12582916
  303.4 1.2 copy-start.2
  406.5 28.7 %copy-start.1 = (bf16[1024,2048]{1,0:T(8,128)(2,1)S(1)}, bf16[1024,2048]{1,0:T(8,128)(2,1)}, u32[]{:S(2)}) copy-start(bf16[1024,2048]{1,0:T(8,128)(2,1)} %get-tuple-element.78.source_ref) | copy-start | bytes 12582916
Sparse Core Ops, SparseCore 0:
  106.9 108.2 all-gather.4
  216.9 58.7 all-gather.2
  277.9 73.4 reduce-scatter.4
  353.6 96.9 reduce-scatter.2
